TPU v7x, 256 devices: a whole 4x4x8 slice. The times are simulated.
256 devices in a mesh: tgt: 64 (over x, z, core), rep: 4 (over y).
Axes of the slice: x: 4, y: 4, z: 8, core: 2. Of those that a mesh axis runs over, the one named last changes fastest.
Arguments:
- flux: bfloat16 [16384, 7808], P(('tgt', 'rep')), may hold values from 0.19921875 to 4
- ivar: bfloat16 [16384, 7808], P(('tgt', 'rep')), may hold values from 0.099609375 to 10
- row_target: int32 [16384], P(('tgt', 'rep')), may hold values from 0 to 8191, as said below
- start_w: float32 [8192, 64], P(('tgt', 'rep')), may hold values from 0.02 to 0.25
- start_h: float32 [64, 7808], P(None, 'tgt'), may hold values from 0.02 to 0.25
Outputs:
- activations: float32 [8192, 64], P(('tgt', 'rep'))
- templates: float32 [64, 7808], P(None, 'tgt')
Inputs may be any that keep to these rules, and one draw needn't show every extreme that they name: `row_target`: row i lies on device d = i // 64; its target t is owned by device t // 32, which has the same index along rep as d, i.e. (t // 32) % 4 == d % 4. The rows of one device name targets of one owning device at most 2 times, and every device reaches 2 for some owner. A target may have several rows or none.
All inputs are finite; a program needn't handle non-finite values.
Results may differ from a plain program's by a relative error of at most 0.035.
Values may be sent and summed in bfloat16 or wider, within the bound.
No kernel may reach another device: no remote copies, remote signals or barrier semaphores. Data moves between devices by JAX's collectives and lax.ppermute only.
A program may use at most 64 MiB of HBM per device.

v0:
```python
import jax
import jax.numpy as jnp
from jax import lax
from jax.sharding import PartitionSpec as P

SWEEPS = 2


PRIOR_IVAR = 0.5
EPSILON = 1e-06


def update_columns(activation, cross, gram):

    def column_step(index, current):
        gram_col = lax.dynamic_index_in_dim(gram, index, 1, keepdims=False)
        pivot = lax.dynamic_index_in_dim(gram_col, index, 0, keepdims=False)
        column = lax.dynamic_index_in_dim(current, index, 1, keepdims=False)
        wanted = lax.dynamic_index_in_dim(cross, index, 1, keepdims=False)
        fitted = jnp.dot(current, gram_col, precision=lax.Precision.HIGHEST)
        updated = jnp.maximum(column + (wanted - fitted) / (pivot + EPSILON), 0.0)
        return lax.dynamic_update_index_in_dim(current, updated, index, 1)

    return lax.fori_loop(0, activation.shape[1], column_step, activation)


def update_rows(templates, proj, gram):

    def row_step(index, current):
        gram_row = lax.dynamic_index_in_dim(gram, index, 0, keepdims=False)
        pivot = lax.dynamic_index_in_dim(gram_row, index, 0, keepdims=False)
        row_now = lax.dynamic_index_in_dim(current, index, 0, keepdims=False)
        wanted = lax.dynamic_index_in_dim(proj, index, 0, keepdims=False)
        fitted = jnp.dot(gram_row, current, precision=lax.Precision.HIGHEST)
        updated = jnp.maximum(row_now + (wanted - fitted) / (pivot + EPSILON), 0.0)
        return lax.dynamic_update_index_in_dim(current, updated, index, 0)

    return lax.fori_loop(0, templates.shape[0], row_step, templates)


def shards(flux, ivar, row_target, start_w, start_h):
    tgt_count = lax.axis_size("tgt")
    rep_count = lax.axis_size("rep")
    rows_dev = flux.shape[0]
    tgt_dev = start_w.shape[0]
    weighted = (ivar.astype(jnp.float32) * flux.astype(jnp.float32)).astype(jnp.bfloat16)
    owner_dev = row_target // tgt_dev
    peer_dev = owner_dev // rep_count
    capacity = 2 * rows_dev // tgt_count
    peer_onehot = (peer_dev[:, None] == jnp.arange(tgt_count, dtype=jnp.int32)[None, :]).astype(
        jnp.int32
    )
    running = jnp.cumsum(peer_onehot, axis=0)
    slot_index = jnp.sum(running * peer_onehot, axis=1) - 1
    place = peer_dev * capacity + slot_index
    source_row = (
        jnp.zeros((tgt_count * capacity,), jnp.int32)
        .at[place]
        .set(jnp.arange(rows_dev, dtype=jnp.int32))
    )
    filled = jnp.zeros((tgt_count * capacity,), jnp.int32).at[place].set(1)
    keep_rows = filled[:, None].astype(jnp.bfloat16)
    send_weighted = jnp.take(weighted, source_row, axis=0) * keep_rows
    send_ivar = jnp.take(ivar, source_row, axis=0) * keep_rows
    send_target = jnp.where(filled == 1, jnp.take(row_target, source_row, axis=0), -1)
    got_weighted, got_ivar, got_target = (
        lax.all_to_all(send_weighted, "tgt", split_axis=0, concat_axis=0, tiled=True),
        lax.all_to_all(send_ivar, "tgt", split_axis=0, concat_axis=0, tiled=True),
        lax.all_to_all(send_target, "tgt", split_axis=0, concat_axis=0, tiled=True),
    )
    first_target = (lax.axis_index("tgt") * rep_count + lax.axis_index("rep")) * tgt_dev
    selector = (
        got_target[None, :] - first_target == jnp.arange(tgt_dev, dtype=jnp.int32)[:, None]
    ).astype(jnp.bfloat16)
    numerator = jnp.dot(selector, got_weighted, preferred_element_type=jnp.float32)
    denominator = jnp.dot(selector, got_ivar, preferred_element_type=jnp.float32)
    coadd = (numerator / (denominator + PRIOR_IVAR)).astype(jnp.bfloat16)
    spectra = lax.all_to_all(coadd, "tgt", split_axis=1, concat_axis=0, tiled=True)
    activation = lax.all_gather(start_w, "tgt", axis=0, tiled=True)
    templates = start_h
    for sweep in range(SWEEPS):
        templ_bf = templates.astype(jnp.bfloat16)
        hgram_part = jnp.dot(templates, templates.T, precision=lax.Precision.HIGHEST)
        cross_part = jnp.dot(spectra, templ_bf.T, preferred_element_type=jnp.float32)
        cross, hgram = lax.psum((cross_part, hgram_part), "tgt")
        activation = update_columns(activation, cross, hgram)
        proj_part = lax.dot_general(
            activation.astype(jnp.bfloat16),
            spectra,
            (((0,), (0,)), ((), ())),
            preferred_element_type=jnp.float32,
        )
        wgram_part = jnp.dot(activation.T, activation, precision=lax.Precision.HIGHEST)
        proj, wgram = lax.psum((proj_part, wgram_part), "rep")
        templates = update_rows(templates, proj, wgram)
    own_w = lax.dynamic_slice_in_dim(activation, lax.axis_index("tgt") * tgt_dev, tgt_dev, 0)
    return (own_w, templates)


def solution(mesh):
    placed = (
        P(("tgt", "rep"), None),
        P(("tgt", "rep"), None),
        P(("tgt", "rep")),
        P(("tgt", "rep"), None),
        P(None, "tgt"),
    )
    return jax.shard_map(
        shards,
        mesh=mesh,
        in_specs=placed,
        out_specs=(P(("tgt", "rep"), None), P(None, "tgt")),
        check_vma=False,
    )
```

profile of v0, /device:TPU:1, one launch (start us, length us, event | category | flops | bytes accessed | tf_op | source)
XLA Modules:
  0.0 1312.0 jit_solution(9789575537605206230)
XLA Ops:
  13.6 13.0 all-to-all-start
  26.6 6.4 gather_fusion.2
  33.2 3.1 gather_fusion.1
  36.4 4.0 select_multiply_fusion.1
  40.4 1.7 all_to_all.41
  42.1 10.3 all-to-all-start.2
  52.5 5.0 all_to_all.38
  57.5 44.1 %all-to-all-done.2 = bf16[64,2,7808]{2,1,0:T(2,128)(2,1)S(1)} async-done(((bf16[64,2,7808]{2,1,0:T(2,128)(2,1)}), bf16[64,2,7808]{2,1,0:T(2,128)(2,1)S(1)}, u32[]{:S(2)}, u32[]{:S(2)}) %all-to-all-start.2) | async-done | bytes 1998880 | tf_op jit(solution)/shard_map/all_to_all | solution.py:68
  101.6 6.0 all-to-all-start.1
  107.9 4.3 all_to_all.43
  112.6 44.1 %all-to-all-done.1 = bf16[64,2,7808]{2,1,0:T(2,128)(2,1)} async-done(((bf16[64,2,7808]{2,1,0:T(2,128)(2,1)}), bf16[64,2,7808]{2,1,0:T(2,128)(2,1)}, u32[]{:S(2)}, u32[]{:S(2)}) %all-to-all-start.1) | async-done | bytes 1998880 | tf_op jit(solution)/shard_map/all_to_all | solution.py:67
  156.7 4.3 all_to_all.40
  161.4 2.1 all_to_all.44
  164.7 5.8 all-to-all-start.3
  170.6 17.3 %all-to-all-done.3 = bf16[32,64,122]{2,0,1:T(8,128)(2,1)S(1)} async-done(((bf16[32,64,122]{2,0,1:T(8,128)(2,1)}), bf16[32,64,122]{2,0,1:T(8,128)(2,1)S(1)}, u32[]{:S(2)}, u32[]{:S(2)}) %all-to-all-start.3) | async-done | bytes 499744 | tf_op jit(solution)/shard_map/all_to_all | solution.py:78
  189.2 242.6 %psum.57 = f32[64,64]{1,0:T(8,128)S(1)} all-reduce(f32[64,64]{1,0:T(8,128)S(1)} %fusion.36), channel_id=1, replica_groups=mesh['tgt'=64,'rep'=4] {'tgt'}, use_global_device_ids=true, to_apply=%region_0.1 | all-reduce | flops 4096 | bytes 32768 | tf_op jit(solution)/shard_map/psum | solution.py:85
  431.9 52.6 %all_gather.3 = f32[2048,64]{1,0:T(8,128)S(1)} all-gather(f32[32,64]{1,0:T(8,128)S(1)} %copy-done.4), channel_id=1, replica_groups=mesh['tgt'=64,'rep'=4] {'tgt'}, dimensions={0}, use_global_device_ids=true | all-gather | bytes 532480 | tf_op jit(solution)/shard_map/all_gather | solution.py:79
  484.9 181.6 %while.64 = (s32[]{:T(128)}, f32[2048,64]{0,1:T(8,128)S(1)}, f32[2048,64]{0,1:T(8,128)}, f32[64,64]{0,1:T(8,128)S(1)}, s32[]{:T(128)}, /*index=5*/s32[]{:T(128)}, s32[]{:T(128)}, f32[1,1]{0,1:T(1,128)}) while((s32[]{:T(128)}, f32[2048,64]{0,1:T(8,128)S(1)}, f32[2048,64]{0,1:T(8,128)}, f32[64,64]{0,1:T(8,128)S(1)}, s32[]{:T(128)}, ...), condition=%wide.region_7.9_spmd, body=%wide.region_6.8_spmd.sunk | while | flops 1581060 | bytes 615053 | solution.py:24
  667.2 14.1 %all-reduce.1 = (f32[64,122]{1,0:T(8,128)S(1)}, f32[64,64]{1,0:T(8,128)S(1)}) all-reduce(f32[64,122]{1,0:T(8,128)S(1)} %fusion.23, f32[64,64]{1,0:T(8,128)S(1)} %fusion.37), channel_id=1, replica_groups=mesh['tgt'=64,'rep'=4] {'rep'}, use_global_device_ids=true, to_apply=%region_9.11 | all-reduce | flops 11904 | bytes 95232 | tf_op jit(solution)/shard_map/psum | solution.py:94
  681.3 91.4 %while.65 = (s32[]{:T(128)}, f32[64,122]{1,0:T(8,128)S(1)}, f32[64,122]{1,0:T(8,128)S(1)}, f32[64,64]{1,0:T(8,128)S(1)}, s32[]{:T(128)}, /*index=5*/s32[]{:T(128)}, s32[]{:T(128)}, f32[1,1]{1,0:T(1,128)}) while((s32[]{:T(128)}, f32[64,122]{1,0:T(8,128)S(1)}, f32[64,122]{1,0:T(8,128)S(1)}, f32[64,64]{1,0:T(8,128)S(1)}, s32[]{:T(128)}, ...), condition=%wide.region_11.13_spmd, body=%wide.region_10.12_spmd.sunk | while | flops 94188 | bytes 37433 | solution.py:38
  774.1 244.4 %psum.61 = f32[64,64]{1,0:T(8,128)S(1)} all-reduce(f32[64,64]{1,0:T(8,128)S(1)} %fusion.38), channel_id=1, replica_groups=mesh['tgt'=64,'rep'=4] {'tgt'}, use_global_device_ids=true, to_apply=%region_12.14 | all-reduce | flops 4096 | bytes 32768 | tf_op jit(solution)/shard_map/psum | solution.py:85
  1018.6 181.6 %while.66 = (s32[]{:T(128)}, f32[2048,64]{0,1:T(8,128)S(1)}, f32[2048,64]{0,1:T(8,128)}, f32[64,64]{0,1:T(8,128)S(1)}, s32[]{:T(128)}, /*index=5*/s32[]{:T(128)}, s32[]{:T(128)}, f32[1,1]{0,1:T(1,128)}) while((s32[]{:T(128)}, f32[2048,64]{0,1:T(8,128)S(1)}, f32[2048,64]{0,1:T(8,128)}, f32[64,64]{0,1:T(8,128)S(1)}, s32[]{:T(128)}, ...), condition=%wide.region_15.17_spmd, body=%wide.region_14.16_spmd.sunk | while | flops 1581060 | bytes 615053 | solution.py:24
  1201.3 11.8 all-reduce
  1213.1 91.4 %while.67 = (s32[]{:T(128)}, f32[64,122]{1,0:T(8,128)S(1)}, f32[64,122]{1,0:T(8,128)S(1)}, f32[64,64]{1,0:T(8,128)S(1)}, s32[]{:T(128)}, /*index=5*/s32[]{:T(128)}, s32[]{:T(128)}, f32[1,1]{1,0:T(1,128)}) while((s32[]{:T(128)}, f32[64,122]{1,0:T(8,128)S(1)}, f32[64,122]{1,0:T(8,128)S(1)}, f32[64,64]{1,0:T(8,128)S(1)}, s32[]{:T(128)}, ...), condition=%wide.region_19.21_spmd, body=%wide.region_18.20_spmd.sunk | while | flops 94188 | bytes 37433 | solution.py:38
  (1075 shorter events, 381.3 us)
Async XLA Ops:
  13.6 28.6 %all-to-all-start = ((s32[64,2,1]{1,2,0:T(1,128)}), s32[64,2,1]{1,2,0:T(1,128)S(1)}, u32[]{:S(2)}, u32[]{:S(2)}) async-start(s32[64,2,1]{1,2,0:T(1,128)} %bitcast.26), calls=%async_computation | async-start | bytes 65536 | tf_op jit(solution)/shard_map/all_to_all | solution.py:69
  26.6 6.4 copy-start
  26.6 6.4 copy-start.3
  42.1 59.5 %all-to-all-start.2 = ((bf16[64,2,7808]{2,1,0:T(2,128)(2,1)}), bf16[64,2,7808]{2,1,0:T(2,128)(2,1)S(1)}, u32[]{:S(2)}, u32[]{:S(2)}) async-start(bf16[64,2,7808]{2,1,0:T(2,128)(2,1)} %all_to_all.41), calls=%async_computation.2 | async-start | bytes 3997696 | tf_op jit(solution)/shard_map/all_to_all | solution.py:68
  101.6 6.0 copy-start.2
  101.6 55.1 %all-to-all-start.1 = ((bf16[64,2,7808]{2,1,0:T(2,128)(2,1)}), bf16[64,2,7808]{2,1,0:T(2,128)(2,1)}, u32[]{:S(2)}, u32[]{:S(2)}) async-start(bf16[64,2,7808]{2,1,0:T(2,128)(2,1)} %all_to_all.38), calls=%async_computation.1 | async-start | bytes 3997696 | tf_op jit(solution)/shard_map/all_to_all | solution.py:67
  163.5 268.3 %copy-start.4 = (f32[32,64]{1,0:T(8,128)S(1)}, f32[32,64]{1,0:T(8,128)}, u32[]{:S(2)}) copy-start(f32[32,64]{1,0:T(8,128)} %param.18) | copy-start | bytes 24580
  164.7 23.2 %all-to-all-start.3 = ((bf16[32,64,122]{2,0,1:T(8,128)(2,1)}), bf16[32,64,122]{2,0,1:T(8,128)(2,1)S(1)}, u32[]{:S(2)}, u32[]{:S(2)}) async-start(bf16[32,64,122]{2,0,1:T(8,128)(2,1)} %copy.17), calls=%async_computation.3 | async-start | bytes 1048576 | tf_op jit(solution)/shard_map/all_to_all | solution.py:78
  170.5 314.3 %all-reduce.5.cloned.1.call-start = ((), (), s32[]{:S(2)}) async-start(), calls=%async_computation.4 | async-start | bytes 1048576 | tf_op jit(solution)/shard_map/psum | solution.py:85
  189.0 829.7 %all-reduce.7.cloned.1.call-start = ((), (), s32[]{:S(2)}) async-start(), calls=%async_computation.5 | async-start | bytes 1048576 | tf_op jit(solution)/shard_map/psum | solution.py:85
  1304.5 0.6 copy-start.1
Sparse Core Ops, SparseCore 0:
  189.1 176.5 all-reduce.4
  774.0 178.4 all-reduce.6
where the time goes:
time: 1330 us; the launch traced here: 1310 us
  blocking collectives  566 us (43%)
  local copies, waits for them, and re-layouts  335 us (25%)
  loops' own time  179 us (13%)
  waiting for transfers between devices  106 us (8%)
  matrix products  70.2 us (5%)
  starting transfers between devices  35.2 us (3%)
  between operations  14.4 us (1%)
    psum x2, blocking collectives, shards(): cross, hgram = lax.psum((cross_part, hgram_part), 'tgt')  487 us
    dynamic_slice x128, local copies, waits for them, and re-layouts, column_step(): wanted = lax.dynamic_index_in_dim(cross, index, 1, keepdims=False)  110 us
    another operation x2, loops' own time, update_columns(): return lax.fori_loop(0, activation.shape[1], column_step, activation)  93.4 us
    dynamic_slice x128, local copies, waits for them, and re-layouts, column_step(): pivot = lax.dynamic_index_in_dim(gram_col, index, 0, keepdims=False)  85.8 us
    another operation x2, loops' own time, update_rows(): return lax.fori_loop(0, templates.shape[0], row_step, templates)  85.8 us
    dynamic_slice x128, local copies, waits for them, and re-layouts, row_step(): pivot = lax.dynamic_index_in_dim(gram_row, index, 0, keepdims=False)  75.3 us
    all_gather x1, blocking collectives, shards(): activation = lax.all_gather(start_w, 'tgt', axis=0, tiled=True)  52.6 us
    dot_general x128, matrix products, column_step(): fitted = jnp.dot(current, gram_col, precision=lax.Precision.HIGHEST)  46.8 us
  transfers between devices with their start and end apart: 6, of which 3 were waited for; matrix products, arithmetic and copies ran while one was open for 1% of the time, Pallas kernels for 0%

commit v1 on v0

v1 whole, which is shorter than its diff:
```python
import jax
import jax.numpy as jnp
from jax import lax
from jax.experimental import pallas as pl
from jax.experimental.pallas import tpu as pltpu
from jax.sharding import Mesh, PartitionSpec as P

SWEEPS = 2
PRIOR_IVAR = 0.5
EPSILON = 1e-06

NX, NZ, NC, NY = 4, 8, 2, 4
N_TGT = NX * NZ * NC
ROWS = 64
RANK = 64
PIX = 122
LANES = 128
TGT = ("x", "z", "c")
BF = jnp.bfloat16
F32 = jnp.float32
VMEM = pl.BlockSpec(memory_space=pltpu.VMEM)
SMEM = pl.BlockSpec(memory_space=pltpu.SMEM)
NT = (((1,), (1,)), ((), ()))
TN = (((0,), (0,)), ((), ()))


def call(body, outs, args, scratch=(), scalars=0):
    return pl.pallas_call(
        body,
        out_shape=outs,
        in_specs=[SMEM] * scalars + [VMEM] * (len(args) - scalars),
        out_specs=jax.tree.map(lambda _: VMEM, outs),
        scratch_shapes=list(scratch),
        compiler_params=pltpu.CompilerParams(vmem_limit_bytes=40 * 2**20),
    )(*args)


def pack_body(flux_ref, ivar_ref, extra_ref, send_ref, weighted_ref):
    weighted_ref[...] = (
        ivar_ref[...].astype(F32) * flux_ref[...].astype(F32)
    ).astype(BF)
    extra = extra_ref[...]
    for dev in range(N_TGT):
        span = slice(dev * PIX, dev * PIX + PIX)
        send_ref[dev, :, 0:PIX] = weighted_ref[:, span]
        send_ref[dev, :, PIX:LANES] = extra[:, 0:LANES - PIX]
        send_ref[dev, :, LANES:LANES + PIX] = ivar_ref[:, span]
        send_ref[dev, :, LANES + PIX:2 * LANES] = jnp.zeros((ROWS, LANES - PIX), BF)


def template_pair(templ_bf):
    none = jnp.zeros_like(templ_bf)
    return jnp.concatenate(
        [
            jnp.concatenate([templ_bf, none], axis=1),
            jnp.concatenate([none, templ_bf], axis=1),
        ],
        axis=0,
    )


def cross_block(core, block, spectra, pair, keep_ref, send_ref):
    part = lax.dot_general(spectra, pair, NT, preferred_element_type=F32)
    place = pl.ds(pl.multiple_of((block % 2) * 256, 256), 256)

    @pl.when(block // 2 == core)
    def _():
        keep_ref[place, :] = part

    @pl.when(block // 2 != core)
    def _():
        send_ref[place, :] = part


def coadd_body(core_ref, got_ref, templ_ref, spectra_ref, keep_ref, send_ref, low_ref, high_ref):
    lane = lax.broadcasted_iota(jnp.int32, (16, 2 * LANES), 1)
    row = lax.broadcasted_iota(jnp.int32, (16, 2 * LANES), 0)
    pick = jnp.where(lane == PIX + row, 1.0, 0.0)
    pick = jnp.where(row < 2, pick, 0.0).astype(BF)
    ids = lax.dot_general(pick, got_ref[...], NT, preferred_element_type=F32)
    high_ref[...] = jnp.broadcast_to(ids[0:1, :], high_ref.shape)
    low = ids[1:2, :].astype(jnp.int32)
    low_ref[...] = jnp.where(
        low == lax.broadcasted_iota(jnp.int32, low_ref.shape, 0), 1.0, 0.0
    ).astype(BF)
    inside = lax.broadcasted_iota(jnp.int32, (256, LANES), 1) < PIX
    pair = template_pair(templ_ref[...].astype(BF))

    def block_step(block, carry):
        for half in range(2):
            first = ((half * 4 + block) * 4).astype(F32)
            selector = jnp.concatenate(
                [
                    low_ref[...]
                    * jnp.where(high_ref[0:1, :] == first + float(i), 1.0, 0.0).astype(BF)
                    for i in range(4)
                ],
                axis=0,
            )
            sums = jnp.dot(selector, got_ref[...], preferred_element_type=F32)
            coadd = sums[:, 0:LANES] / (sums[:, LANES:] + PRIOR_IVAR)
            spectra_ref[
                pl.ds(pl.multiple_of(block * 256, 256), 256),
                half * LANES:(half + 1) * LANES,
            ] = jnp.where(inside, coadd, 0.0).astype(BF)
        spectra = spectra_ref[pl.ds(pl.multiple_of(block * 256, 256), 256), :]
        cross_block(core_ref[0], block, spectra, pair, keep_ref, send_ref)
        return carry

    lax.fori_loop(0, 4, block_step, 0)


def pack_gram(gram):
    turned = pltpu.roll(
        jnp.concatenate([gram[32:64, :], jnp.zeros((32, 64), F32)], axis=1), 64, 1
    )
    return jnp.concatenate([gram[0:32, :], jnp.zeros((32, 64), F32)], axis=1) + turned


def unpack_gram(packed):
    return jnp.concatenate([packed[:, 0:64], pltpu.roll(packed, 64, 1)[:, 0:64]], axis=0)


def descend(state, wanted, gram):
    eye = lax.broadcasted_iota(jnp.int32, (RANK, RANK), 0) == lax.broadcasted_iota(
        jnp.int32, (RANK, RANK), 1
    )
    pivot = jnp.sum(jnp.where(eye, gram, 0.0), axis=1, keepdims=True) + EPSILON
    inverse = 1.0 / pivot
    fitted = jnp.dot(
        gram, state, precision=lax.Precision.HIGHEST, preferred_element_type=F32
    )
    goal = state + (wanted - fitted) * inverse
    scaled = gram * inverse
    goals = [goal[8 * i:8 * i + 8, :] for i in range(8)]
    done = []
    for k in range(RANK):
        old = state[k:k + 1, :]
        new = jnp.maximum(goals[k // 8][k % 8:k % 8 + 1, :], 0.0)
        done.append(new)
        change = new - old
        for i in range(k // 8, 8):
            goals[i] = goals[i] - scaled[8 * i:8 * i + 8, k:k + 1] * change
    return jnp.concatenate(done, axis=0)


def pad_to(value, rows, lanes):
    if value.shape[1] < lanes:
        value = jnp.concatenate(
            [value, jnp.zeros((value.shape[0], lanes - value.shape[1]), F32)], axis=1
        )
    if value.shape[0] < rows:
        value = jnp.concatenate(
            [value, jnp.zeros((rows - value.shape[0], value.shape[1]), F32)], axis=0
        )
    return value


def activation_body(first, cross_ref, gram_ref, state_ref, new_ref, out_ref):
    cross = pad_to(jnp.sum(cross_ref[...], axis=0), LANES, LANES).T
    wanted = cross[0:64, :] + pltpu.roll(cross[64:128, :], 16, 1)
    gram = unpack_gram(jnp.sum(gram_ref[...], axis=0))
    if first:
        state = pad_to(state_ref[...], LANES, LANES).T[0:RANK, :]
    else:
        state = state_ref[...]
    updated = descend(state, wanted, gram)
    if first:
        new_ref[...] = updated
    else:
        new_ref[...] = pad_to(updated, LANES, LANES).T[0:32, 0:RANK]
    both = jnp.concatenate([updated, pltpu.roll(updated, LANES - 16, 1)], axis=0).T
    out_ref[...] = jnp.broadcast_to(both[0:16, :].astype(BF)[None], out_ref.shape)


def project_body(core_ref, own_ref, other_ref, spectra_ref, out_ref):
    core = core_ref[0]
    proj, gram = 0.0, 0.0
    for ref, at in ((own_ref, core), (other_ref, 1 - core)):
        rows = spectra_ref[pl.ds(pl.multiple_of(at * 512, 512), 512), :]
        proj += lax.dot_general(ref[...], rows, TN, preferred_element_type=F32)
        gram += lax.dot_general(ref[...], ref[...], TN, preferred_element_type=F32)
    out_ref[0:64, :] = proj[0:64, 0:LANES] + proj[64:128, LANES:]
    gram = gram[0:64, 0:64] + pltpu.roll(gram[64:128, :], 64, 1)[:, 0:64]
    out_ref[64:96, :] = pack_gram(gram)


def new_templates(part_refs, templ_ref):
    one, two, three, four = (ref[...] for ref in part_refs)
    total = (one + three) + (two + four)
    return descend(templ_ref[...], total[0:64, :], unpack_gram(total[64:96, :]))


def template_body(core_ref, a_ref, b_ref, c_ref, d_ref, templ_ref, spectra_ref, new_ref, keep_ref, send_ref, gram_ref):
    updated = new_templates((a_ref, b_ref, c_ref, d_ref), templ_ref)
    new_ref[...] = updated
    templ_bf = updated.astype(BF)
    gram_ref[...] = pack_gram(
        lax.dot_general(templ_bf, templ_bf, NT, preferred_element_type=F32)
    )
    pair = template_pair(templ_bf)
    for block in range(4):
        spectra = spectra_ref[block * 256:(block + 1) * 256, :]
        cross_block(core_ref[0], block, spectra, pair, keep_ref, send_ref)


def last_template_body(a_ref, b_ref, c_ref, d_ref, templ_ref, new_ref):
    updated = new_templates((a_ref, b_ref, c_ref, d_ref), templ_ref)
    new_ref[...] = updated[:, 0:PIX]


def first_gram_body(templ_ref, gram_ref):
    templ_bf = templ_ref[...].astype(BF)
    gram_ref[...] = pack_gram(
        lax.dot_general(templ_bf, templ_bf, NT, preferred_element_type=F32)
    )


def shift(value, axis, size, by):
    return lax.ppermute(value, axis, [(i, (i + by) % size) for i in range(size)])


def everywhere(part):
    part = part + shift(part, "c", NC, 1)
    part = (part + shift(part, "x", NX, 2)) + (shift(part, "x", NX, 1) + shift(part, "x", NX, 3))
    return lax.all_to_all(
        jnp.broadcast_to(part[None], (NZ, *part.shape)), "z", split_axis=0, concat_axis=0, tiled=True
    )


def sds(*shape, dtype=F32):
    return jax.ShapeDtypeStruct(shape, dtype)


def shards(flux, ivar, row_target, start_w, start_h):
    core = lax.axis_index("c").astype(jnp.int32).reshape(1)
    peer, local = row_target // 128, row_target % 32
    index = (local // 16) * 1024 + (peer % 2) * 512 + (peer // 2) * 16 + local % 16
    extra = jnp.pad(
        jnp.stack([index // 64, index % 64], axis=1).astype(BF), ((0, 0), (0, LANES - 2))
    )
    send = call(
        pack_body,
        sds(N_TGT, ROWS, 2 * LANES, dtype=BF),
        (flux, ivar, extra),
        scratch=[pltpu.VMEM(flux.shape, BF)],
    )
    got = lax.all_to_all(send, TGT, split_axis=0, concat_axis=0, tiled=True)
    templates = jnp.pad(start_h, ((0, 0), (0, LANES - PIX)))
    gram = everywhere(call(first_gram_body, sds(32, LANES), (templates,)))
    spectra, keep, away = call(
        coadd_body,
        (sds(1024, 2 * LANES, dtype=BF), sds(512, LANES), sds(512, LANES)),
        (core, got.reshape(N_TGT * ROWS, 2 * LANES), templates),
        scratch=[pltpu.VMEM((64, N_TGT * ROWS), BF), pltpu.VMEM((8, N_TGT * ROWS), F32)],
        scalars=1,
    )
    state = start_w
    for sweep in range(SWEEPS):
        cross = (keep + shift(away, "c", NC, 1)).reshape(32, 16, LANES)
        cross = lax.all_to_all(cross, ("x", "z"), split_axis=0, concat_axis=0, tiled=True)
        first = sweep == 0
        state, message = call(
            lambda *refs, first=first: activation_body(first, *refs),
            (sds(RANK, LANES) if first else sds(32, RANK), sds(32, 16, LANES, dtype=BF)),
            (cross, gram, state),
        )
        own = lax.all_to_all(message, ("x", "z"), split_axis=0, concat_axis=0, tiled=True)
        own = own.reshape(512, LANES)
        other = shift(own, "c", NC, 1)
        part = call(
            project_body, sds(96, LANES), (core, own, other, spectra), scalars=1
        )
        parts = (part, *(shift(part, "y", NY, by) for by in (1, 2, 3)))
        if first:
            templates, keep, away, gram = call(
                template_body,
                (sds(RANK, LANES), sds(512, LANES), sds(512, LANES), sds(32, LANES)),
                (core, *parts, templates, spectra),
                scalars=1,
            )
            gram = everywhere(gram)
        else:
            templates = call(last_template_body, sds(RANK, PIX), (*parts, templates))
    return state, templates


def solution(mesh):
    grid = Mesh(mesh.devices.reshape(NX, NZ, NC, NY), ("x", "z", "c", "y"))
    every = ("x", "z", "c", "y")
    return jax.shard_map(
        shards,
        mesh=grid,
        in_specs=(P(every, None), P(every, None), P(every), P(every, None), P(None, TGT)),
        out_specs=(P(every, None), P(None, TGT)),
        check_vma=False,
    )
```

time: 1330 us -> 198 us (0.15); the launches traced: 1310 us -> 197 us
  blocking collectives: 566 us -> 54.6 us
  local copies, waits for them, and re-layouts: 335 us -> 5.22 us
  loops' own time: 179 us -> 0 us
  matrix products: 70.2 us -> 0 us
  waiting for transfers between devices: 106 us -> 73.7 us
  Pallas kernels: 0 us -> 13.7 us
  between operations: 14.4 us -> 0.8 us
    psum x4 -> x0, blocking collectives: 513 us -> none  [the longest x2 487 us: shards(): cross, hgram = lax.psum((cross_part, hgram_part), 'tgt')]
    dynamic_slice x385 -> x0, local copies, waits for them, and re-layouts: 272 us -> none  [the longest x128 110 us: column_step(): wanted = lax.dynamic_index_in_dim(cross, index, 1, keepdims=False)]
    another operation x4 -> x0, loops' own time: 179 us -> none  [the longest x2 93.4 us: update_columns(): return lax.fori_loop(0, activation.shape[1], column_step, activation)]
    dot_general x266 -> x0, matrix products: 70.2 us -> none  [the longest x128 46.8 us: column_step(): fitted = jnp.dot(current, gram_col, precision=lax.Precision.HIGHEST)]
    all_to_all x0 -> x4, blocking collectives: none -> 54.6 us  [the longest x2 28.5 us: shards(): lax.all_to_all(message, ('x', 'z'), split_axis=0, concat_axis=0, tiled=True)]
    all_gather x1 -> x0, blocking collectives: 52.6 us -> none  [shards(): activation = lax.all_gather(start_w, 'tgt', axis=0, tiled=True)]
    all_to_all x4 -> x3, waiting for transfers between devices: 106 us -> 61.7 us  [the longest x1 45.3 us: shards(): got = lax.all_to_all(send, TGT, split_axis=0, concat_axis=0, tiled=True)]
    dynamic_update_slice x256 -> x0, local copies, waits for them, and re-layouts: 29.5 us -> none  [the longest x128 26.2 us: column_step(): return lax.dynamic_update_index_in_dim(current, updated, index, 1)]
  transfers between devices with their start and end apart: 6 -> 21, of which waited for: 3 -> 13; matrix products, arithmetic and copies ran while one was open for 1% -> 1% of each run, Pallas kernels for 0% -> 3%
where the time goes in v1:
time: 198 us; the launch traced here: 197 us
  waiting for transfers between devices  73.7 us (37%)
  blocking collectives  54.6 us (28%)
  starting transfers between devices  48.4 us (24%)
  Pallas kernels  13.7 us (7%)
  local copies, waits for them, and re-layouts  5.22 us (3%)
    all_to_all x1, waiting for transfers between devices, shards(): got = lax.all_to_all(send, TGT, split_axis=0, concat_axis=0, tiled=True)  45.3 us
    all_to_all x2, blocking collectives, shards(): lax.all_to_all(message, ('x', 'z'), split_axis=0, concat_axis=0, tiled=True)  28.5 us
    ppermute x18, starting transfers between devices, shift(): lax.ppermute(value, axis, [(i, (i + by) % size) for i in range(size)])  28.2 us
    all_to_all x2, blocking collectives, shards(): lax.all_to_all(cross, ('x', 'z'), split_axis=0, concat_axis=0, tiled=True)  26.1 us
    all_to_all x2, waiting for transfers between devices, everywhere(): lax.all_to_all(jnp.broadcast_to(part[None], (NZ, *part.shape)), 'z', spli...  16.3 us
    pallas_call x9, Pallas kernels, call(): pl.pallas_call(body, out_shape=outs, in_specs=[SMEM] * scalars + [VMEM] *...  13.7 us
    all_to_all x1, starting transfers between devices, shards(): got = lax.all_to_all(send, TGT, split_axis=0, concat_axis=0, tiled=True)  13.1 us
    ppermute x18, waiting for transfers between devices, shift(): lax.ppermute(value, axis, [(i, (i + by) % size) for i in range(size)])  12.1 us
  transfers between devices with their start and end apart: 21, of which 13 were waited for; matrix products, arithmetic and copies ran while one was open for 1% of the time, Pallas kernels for 3%

profile of v1, /device:TPU:1, one launch (start us, length us, event | category | flops | bytes accessed | tf_op | source)
XLA Modules:
  0.0 197.3 jit_solution(5814347857215428846)
XLA Ops:
  5.0 1.3 copy-done
  6.4 13.1 %all-to-all-start = ((bf16[64,64,256]{2,1,0:T(8,128)(2,1)}), bf16[64,64,256]{2,1,0:T(8,128)(2,1)S(1)}, u32[]{:S(2)}, u32[]{:S(2)}) async-start(bf16[64,64,256]{2,1,0:T(8,128)(2,1)} %copy-done), calls=%async_computation | async-start | bytes 4194304 | tf_op jit(solution)/shard_map/all_to_all | solution.py:248
  22.4 1.5 collective-permute-start.4
  23.8 1.6 collective-permute-start.2
  25.4 45.3 %all-to-all-done = bf16[64,64,256]{2,1,0:T(8,128)(2,1)S(1)} async-done(((bf16[64,64,256]{2,1,0:T(8,128)(2,1)}), bf16[64,64,256]{2,1,0:T(8,128)(2,1)S(1)}, u32[]{:S(2)}, u32[]{:S(2)}) %all-to-all-start) | async-done | bytes 2097184 | tf_op jit(solution)/shard_map/all_to_all | solution.py:248
  70.8 6.4 %shard_map.69 = (bf16[1024,256]{1,0:T(8,128)(2,1)S(1)}, f32[512,128]{1,0:T(8,128)S(1)}, f32[512,128]{1,0:T(8,128)S(1)}) custom-call(s32[1]{0:T(128)} %bitcast.core_ref, bf16[4096,256]{1,0:T(8,128)(2,1)S(1)} %bitcast.10, f32[64,128]{1,0:T(8,128)S(1)} %pad.9.templ_ref), custom_call_target="tpu_custom_call" | custom-call | tf_op jit(solution)/shard_map/pallas_call | solution.py:28
  78.4 3.8 %all-to-all-start.2 = ((f32[8,32,128]{2,1,0:T(8,128)}), f32[8,32,128]{2,1,0:T(8,128)S(1)}, u32[]{:S(2)}, u32[]{:S(2)}) async-start(f32[8,32,128]{2,1,0:T(8,128)} %broadcast_in_dim.4), calls=%async_computation.2 | async-start | bytes 262144 | tf_op jit(solution)/shard_map/all_to_all | solution.py:226
  82.2 8.4 %all-to-all-done.2.refs_1_ = f32[8,32,128]{2,1,0:T(8,128)S(1)} async-done(((f32[8,32,128]{2,1,0:T(8,128)}), f32[8,32,128]{2,1,0:T(8,128)S(1)}, u32[]{:S(2)}, u32[]{:S(2)}) %all-to-all-start.2) | async-done | bytes 131104 | tf_op jit(solution)/shard_map/all_to_all | solution.py:226
  90.7 13.4 %all_to_all.35.refs_0_ = f32[32,16,128]{2,1,0:T(8,128)S(1)} all-to-all(f32[32,16,128]{2,1,0:T(8,128)S(1)} %bitcast.15), channel_id=1, replica_groups=mesh['x'=4,'z'=8,'c'=2,'y'=4] {'x','z'}, dimensions={0} | all-to-all | bytes 524288 | tf_op jit(solution)/shard_map/all_to_all | solution.py:261
  104.9 15.0 %all_to_all.36 = bf16[32,16,128]{2,1,0:T(8,128)(2,1)S(1)} all-to-all(bf16[32,16,128]{2,1,0:T(8,128)(2,1)S(1)} %get-tuple-element.15), channel_id=1, replica_groups=mesh['x'=4,'z'=8,'c'=2,'y'=4] {'x','z'}, dimensions={0} | all-to-all | bytes 262144 | tf_op jit(solution)/shard_map/all_to_all | solution.py:268
  119.9 3.3 %collective-permute-start.5 = (bf16[512,128]{1,0:T(8,128)(2,1)S(1)}, bf16[512,128]{1,0:T(8,128)(2,1)S(1)}, u32[]{:S(2)}, u32[]{:S(2)}) collective-permute-start(bf16[512,128]{1,0:T(8,128)(2,1)S(1)} %bitcast.13), channel_id=1, source_target_pairs={{0,4},{4,0},{1,5},{5,1},{2,6},{6,2},{3,7},{7,3},{8,12},{12,8},{9,1... | collective-permute-start | bytes 393224 | tf_op jit(solution)/shard_map/ppermute | solution.py:220
  126.0 2.6 %collective-permute-start.7 = (f32[96,128]{1,0:T(8,128)S(1)}, f32[96,128]{1,0:T(8,128)S(1)}, u32[]{:S(2)}, u32[]{:S(2)}) collective-permute-start(f32[96,128]{1,0:T(8,128)S(1)} %shard_map.72.a_ref), channel_id=1, source_target_pairs={{0,2},{1,3},{2,0},{3,1},{4,6},{5,7},{6,4},{7,5},{8,10},{9,11},{10,... | collective-permute-start | bytes 147464 | tf_op jit(solution)/shard_map/ppermute | solution.py:220
  131.9 1.6 shard_map.73
  133.4 1.9 collective-permute-start.10
  136.5 2.3 %collective-permute-start.13 = (f32[32,128]{1,0:T(8,128)S(1)}, f32[32,128]{1,0:T(8,128)S(1)}, u32[]{:S(2)}, u32[]{:S(2)}) collective-permute-start(f32[32,128]{1,0:T(8,128)S(1)} %add.78), channel_id=1, source_target_pairs={{0,192},{64,0},{128,64},{192,128},{1,193},{65,1},{129,65},{193,129... | collective-permute-start | bytes 49160 | tf_op jit(solution)/shard_map/ppermute | solution.py:220
  139.9 3.0 %collective-permute-done.11 = f32[32,128]{1,0:T(8,128)S(1)} collective-permute-done((f32[32,128]{1,0:T(8,128)S(1)}, f32[32,128]{1,0:T(8,128)S(1)}, u32[]{:S(2)}, u32[]{:S(2)}) %collective-permute-start.11) | collective-permute-done | bytes 16416 | tf_op jit(solution)/shard_map/ppermute | solution.py:220
  143.6 3.4 %all-to-all-start.5 = ((f32[8,32,128]{2,1,0:T(8,128)}), f32[8,32,128]{2,1,0:T(8,128)S(1)}, u32[]{:S(2)}, u32[]{:S(2)}) async-start(f32[8,32,128]{2,1,0:T(8,128)} %broadcast_in_dim.5), calls=%async_computation.5 | async-start | bytes 262144 | tf_op jit(solution)/shard_map/all_to_all | solution.py:226
  147.0 7.9 %all-to-all-done.5.refs_1_ = f32[8,32,128]{2,1,0:T(8,128)S(1)} async-done(((f32[8,32,128]{2,1,0:T(8,128)}), f32[8,32,128]{2,1,0:T(8,128)S(1)}, u32[]{:S(2)}, u32[]{:S(2)}) %all-to-all-start.5) | async-done | bytes 131104 | tf_op jit(solution)/shard_map/all_to_all | solution.py:226
  154.9 12.7 %all_to_all.37.refs_0_ = f32[32,16,128]{2,1,0:T(8,128)S(1)} all-to-all(f32[32,16,128]{2,1,0:T(8,128)S(1)} %bitcast.16), channel_id=1, replica_groups=mesh['x'=4,'z'=8,'c'=2,'y'=4] {'x','z'}, dimensions={0} | all-to-all | bytes 524288 | tf_op jit(solution)/shard_map/all_to_all | solution.py:261
  167.6 1.4 shard_map.74
  169.0 13.5 %all_to_all.38 = bf16[32,16,128]{2,1,0:T(8,128)(2,1)S(1)} all-to-all(bf16[32,16,128]{2,1,0:T(8,128)(2,1)S(1)} %get-tuple-element.22), channel_id=1, replica_groups=mesh['x'=4,'z'=8,'c'=2,'y'=4] {'x','z'}, dimensions={0} | all-to-all | bytes 262144 | tf_op jit(solution)/shard_map/all_to_all | solution.py:268
  182.5 5.4 %collective-permute-start.14 = (bf16[512,128]{1,0:T(8,128)(2,1)S(1)}, bf16[512,128]{1,0:T(8,128)(2,1)S(1)}, u32[]{:S(2)}, u32[]{:S(2)}) collective-permute-start(bf16[512,128]{1,0:T(8,128)(2,1)S(1)} %bitcast.11), channel_id=1, source_target_pairs={{0,4},{4,0},{1,5},{5,1},{2,6},{6,2},{3,7},{7,3},{8,12},{12,8},{9,1... | collective-permute-start | bytes 393224 | tf_op jit(solution)/shard_map/ppermute | solution.py:220
  189.4 3.5 %collective-permute-start.16 = (f32[96,128]{1,0:T(8,128)S(1)}, f32[96,128]{1,0:T(8,128)S(1)}, u32[]{:S(2)}, u32[]{:S(2)}) collective-permute-start(f32[96,128]{1,0:T(8,128)S(1)} %shard_map.75.a_ref), channel_id=1, source_target_pairs={{0,2},{1,3},{2,0},{3,1},{4,6},{5,7},{6,4},{7,5},{8,10},{9,11},{10,... | collective-permute-start | bytes 147464 | tf_op jit(solution)/shard_map/ppermute | solution.py:220
  193.5 1.6 collective-permute-done.16.c_ref
  (55 shorter events, 22.6 us)
Async XLA Ops:
  5.0 1.4 copy-start
  6.4 13.1 %copy-start.4 = (f32[64,122]{1,0:T(8,128)S(1)}, f32[64,122]{1,0:T(8,128)}, u32[]{:S(2)}) copy-start(f32[64,122]{1,0:T(8,128)} %param.9) | copy-start | bytes 93700
  6.4 64.4 %all-to-all-start = ((bf16[64,64,256]{2,1,0:T(8,128)(2,1)}), bf16[64,64,256]{2,1,0:T(8,128)(2,1)S(1)}, u32[]{:S(2)}, u32[]{:S(2)}) async-start(bf16[64,64,256]{2,1,0:T(8,128)(2,1)} %copy-done), calls=%async_computation | async-start | bytes 4194304 | tf_op jit(solution)/shard_map/all_to_all | solution.py:248
  19.5 84.6 %copy-start.3 = (f32[32,64]{1,0:T(8,128)S(1)}, f32[32,64]{1,0:T(8,128)}, u32[]{:S(2)}) copy-start(f32[32,64]{1,0:T(8,128)} %refs_2_.1) | copy-start | bytes 24580
  19.7 1.3 collective-permute-start.1
  21.1 56.7 %collective-permute-start.3 = (f32[32,128]{1,0:T(8,128)S(1)}, f32[32,128]{1,0:T(8,128)S(1)}, u32[]{:S(2)}, u32[]{:S(2)}) collective-permute-start(f32[32,128]{1,0:T(8,128)S(1)} %add.73), channel_id=1, source_target_pairs={{0,64},{64,128},{128,192},{192,0},{1,65},{65,129},{129,193},{193,1... | collective-permute-start | bytes 49160 | tf_op jit(solution)/shard_map/ppermute | solution.py:220
  22.4 55.4 %collective-permute-start.4 = (f32[32,128]{1,0:T(8,128)S(1)}, f32[32,128]{1,0:T(8,128)S(1)}, u32[]{:S(2)}, u32[]{:S(2)}) collective-permute-start(f32[32,128]{1,0:T(8,128)S(1)} %add.73), channel_id=1, source_target_pairs={{0,192},{64,0},{128,64},{192,128},{1,193},{65,1},{129,65},{193,129... | collective-permute-start | bytes 49160 | tf_op jit(solution)/shard_map/ppermute | solution.py:220
  23.8 53.9 %collective-permute-start.2 = (f32[32,128]{1,0:T(8,128)S(1)}, f32[32,128]{1,0:T(8,128)S(1)}, u32[]{:S(2)}, u32[]{:S(2)}) collective-permute-start(f32[32,128]{1,0:T(8,128)S(1)} %add.73), channel_id=1, source_target_pairs={{0,128},{64,192},{128,0},{192,64},{1,129},{65,193},{129,1},{193,65... | collective-permute-start | bytes 49160 | tf_op jit(solution)/shard_map/ppermute | solution.py:220
  77.2 5.0 %collective-permute-start = (f32[512,128]{1,0:T(8,128)S(1)}, f32[512,128]{1,0:T(8,128)S(1)}, u32[]{:S(2)}, u32[]{:S(2)}) collective-permute-start(f32[512,128]{1,0:T(8,128)S(1)} %get-tuple-element.14), channel_id=1, source_target_pairs={{0,4},{4,0},{1,5},{5,1},{2,6},{6,2},{3,7},{7,3},{8,12},{12,8},{9,1... | collective-permute-start | bytes 786440 | tf_op jit(solution)/shard_map/ppermute | solution.py:220
  78.4 12.3 %all-to-all-start.2 = ((f32[8,32,128]{2,1,0:T(8,128)}), f32[8,32,128]{2,1,0:T(8,128)S(1)}, u32[]{:S(2)}, u32[]{:S(2)}) async-start(f32[8,32,128]{2,1,0:T(8,128)} %broadcast_in_dim.4), calls=%async_computation.2 | async-start | bytes 262144 | tf_op jit(solution)/shard_map/all_to_all | solution.py:226
  119.9 4.3 %collective-permute-start.5 = (bf16[512,128]{1,0:T(8,128)(2,1)S(1)}, bf16[512,128]{1,0:T(8,128)(2,1)S(1)}, u32[]{:S(2)}, u32[]{:S(2)}) collective-permute-start(bf16[512,128]{1,0:T(8,128)(2,1)S(1)} %bitcast.13), channel_id=1, source_target_pairs={{0,4},{4,0},{1,5},{5,1},{2,6},{6,2},{3,7},{7,3},{8,12},{12,8},{9,1... | collective-permute-start | bytes 393224 | tf_op jit(solution)/shard_map/ppermute | solution.py:220
  124.7 5.0 %collective-permute-start.6 = (f32[96,128]{1,0:T(8,128)S(1)}, f32[96,128]{1,0:T(8,128)S(1)}, u32[]{:S(2)}, u32[]{:S(2)}) collective-permute-start(f32[96,128]{1,0:T(8,128)S(1)} %shard_map.72.a_ref), channel_id=1, source_target_pairs={{0,1},{1,2},{2,3},{3,0},{4,5},{5,6},{6,7},{7,4},{8,9},{9,10},{10,1... | collective-permute-start | bytes 147464 | tf_op jit(solution)/shard_map/ppermute | solution.py:220
  126.0 4.9 %collective-permute-start.7 = (f32[96,128]{1,0:T(8,128)S(1)}, f32[96,128]{1,0:T(8,128)S(1)}, u32[]{:S(2)}, u32[]{:S(2)}) collective-permute-start(f32[96,128]{1,0:T(8,128)S(1)} %shard_map.72.a_ref), channel_id=1, source_target_pairs={{0,2},{1,3},{2,0},{3,1},{4,6},{5,7},{6,4},{7,5},{8,10},{9,11},{10,... | collective-permute-start | bytes 147464 | tf_op jit(solution)/shard_map/ppermute | solution.py:220
  128.6 3.2 %collective-permute-start.8 = (f32[96,128]{1,0:T(8,128)S(1)}, f32[96,128]{1,0:T(8,128)S(1)}, u32[]{:S(2)}, u32[]{:S(2)}) collective-permute-start(f32[96,128]{1,0:T(8,128)S(1)} %shard_map.72.a_ref), channel_id=1, source_target_pairs={{0,3},{1,0},{2,1},{3,2},{4,7},{5,4},{6,5},{7,6},{8,11},{9,8},{10,9... | collective-permute-start | bytes 147464 | tf_op jit(solution)/shard_map/ppermute | solution.py:220
  133.4 2.7 %collective-permute-start.10 = (f32[32,128]{1,0:T(8,128)S(1)}, f32[32,128]{1,0:T(8,128)S(1)}, u32[]{:S(2)}, u32[]{:S(2)}) collective-permute-start(f32[32,128]{1,0:T(8,128)S(1)} %get-tuple-element.19), channel_id=1, source_target_pairs={{0,4},{4,0},{1,5},{5,1},{2,6},{6,2},{3,7},{7,3},{8,12},{12,8},{9,1... | collective-permute-start | bytes 49160 | tf_op jit(solution)/shard_map/ppermute | solution.py:220
  136.1 3.8 %collective-permute-start.12 = (f32[32,128]{1,0:T(8,128)S(1)}, f32[32,128]{1,0:T(8,128)S(1)}, u32[]{:S(2)}, u32[]{:S(2)}) collective-permute-start(f32[32,128]{1,0:T(8,128)S(1)} %add.78), channel_id=1, source_target_pairs={{0,64},{64,128},{128,192},{192,0},{1,65},{65,129},{129,193},{193,1... | collective-permute-start | bytes 49160 | tf_op jit(solution)/shard_map/ppermute | solution.py:220
  136.5 3.5 %collective-permute-start.13 = (f32[32,128]{1,0:T(8,128)S(1)}, f32[32,128]{1,0:T(8,128)S(1)}, u32[]{:S(2)}, u32[]{:S(2)}) collective-permute-start(f32[32,128]{1,0:T(8,128)S(1)} %add.78), channel_id=1, source_target_pairs={{0,192},{64,0},{128,64},{192,128},{1,193},{65,1},{129,65},{193,129... | collective-permute-start | bytes 49160 | tf_op jit(solution)/shard_map/ppermute | solution.py:220
  138.8 4.1 %collective-permute-start.11 = (f32[32,128]{1,0:T(8,128)S(1)}, f32[32,128]{1,0:T(8,128)S(1)}, u32[]{:S(2)}, u32[]{:S(2)}) collective-permute-start(f32[32,128]{1,0:T(8,128)S(1)} %add.78), channel_id=1, source_target_pairs={{0,128},{64,192},{128,0},{192,64},{1,129},{65,193},{129,1},{193,65... | collective-permute-start | bytes 49160 | tf_op jit(solution)/shard_map/ppermute | solution.py:220
  138.8 8.1 %collective-permute-start.9 = (f32[512,128]{1,0:T(8,128)S(1)}, f32[512,128]{1,0:T(8,128)S(1)}, u32[]{:S(2)}, u32[]{:S(2)}) collective-permute-start(f32[512,128]{1,0:T(8,128)S(1)} %get-tuple-element.18), channel_id=1, source_target_pairs={{0,4},{4,0},{1,5},{5,1},{2,6},{6,2},{3,7},{7,3},{8,12},{12,8},{9,1... | collective-permute-start | bytes 786440 | tf_op jit(solution)/shard_map/ppermute | solution.py:220
  143.6 11.3 %all-to-all-start.5 = ((f32[8,32,128]{2,1,0:T(8,128)}), f32[8,32,128]{2,1,0:T(8,128)S(1)}, u32[]{:S(2)}, u32[]{:S(2)}) async-start(f32[8,32,128]{2,1,0:T(8,128)} %broadcast_in_dim.5), calls=%async_computation.5 | async-start | bytes 262144 | tf_op jit(solution)/shard_map/all_to_all | solution.py:226
  182.5 6.4 %collective-permute-start.14 = (bf16[512,128]{1,0:T(8,128)(2,1)S(1)}, bf16[512,128]{1,0:T(8,128)(2,1)S(1)}, u32[]{:S(2)}, u32[]{:S(2)}) collective-permute-start(bf16[512,128]{1,0:T(8,128)(2,1)S(1)} %bitcast.11), channel_id=1, source_target_pairs={{0,4},{4,0},{1,5},{5,1},{2,6},{6,2},{3,7},{7,3},{8,12},{12,8},{9,1... | collective-permute-start | bytes 393224 | tf_op jit(solution)/shard_map/ppermute | solution.py:220
  189.3 4.2 %collective-permute-start.15 = (f32[96,128]{1,0:T(8,128)S(1)}, f32[96,128]{1,0:T(8,128)S(1)}, u32[]{:S(2)}, u32[]{:S(2)}) collective-permute-start(f32[96,128]{1,0:T(8,128)S(1)} %shard_map.75.a_ref), channel_id=1, source_target_pairs={{0,1},{1,2},{2,3},{3,0},{4,5},{5,6},{6,7},{7,4},{8,9},{9,10},{10,1... | collective-permute-start | bytes 147464 | tf_op jit(solution)/shard_map/ppermute | solution.py:220
  189.4 5.7 %collective-permute-start.16 = (f32[96,128]{1,0:T(8,128)S(1)}, f32[96,128]{1,0:T(8,128)S(1)}, u32[]{:S(2)}, u32[]{:S(2)}) collective-permute-start(f32[96,128]{1,0:T(8,128)S(1)} %shard_map.75.a_ref), channel_id=1, source_target_pairs={{0,2},{1,3},{2,0},{3,1},{4,6},{5,7},{6,4},{7,5},{8,10},{9,11},{10,... | collective-permute-start | bytes 147464 | tf_op jit(solution)/shard_map/ppermute | solution.py:220
  192.8 3.2 %collective-permute-start.17 = (f32[96,128]{1,0:T(8,128)S(1)}, f32[96,128]{1,0:T(8,128)S(1)}, u32[]{:S(2)}, u32[]{:S(2)}) collective-permute-start(f32[96,128]{1,0:T(8,128)S(1)} %shard_map.75.a_ref), channel_id=1, source_target_pairs={{0,3},{1,0},{2,1},{3,2},{4,7},{5,4},{6,5},{7,6},{8,11},{9,8},{10,9... | collective-permute-start | bytes 147464 | tf_op jit(solution)/shard_map/ppermute | solution.py:220
  (2 other events, 2.4 us)

commit v2 on v1

v2 whole, which is shorter than its diff:
```python
import jax
import jax.numpy as jnp
from jax import lax
from jax.experimental import pallas as pl
from jax.experimental.pallas import tpu as pltpu
from jax.sharding import Mesh, PartitionSpec as P

SWEEPS = 2
PRIOR_IVAR = 0.5
EPSILON = 1e-06

NX, NZ, NC, NY = 4, 8, 2, 4
N_TGT = NX * NZ * NC
ROWS = 64
RANK = 64
PIX = 122
LANES = 128
TGT = ("x", "z", "c")
BF = jnp.bfloat16
F32 = jnp.float32
VMEM = pl.BlockSpec(memory_space=pltpu.VMEM)
SMEM = pl.BlockSpec(memory_space=pltpu.SMEM)
NT = (((1,), (1,)), ((), ()))
TN = (((0,), (0,)), ((), ()))


def call(body, outs, args, scratch=(), scalars=0, flops=0):
    return pl.pallas_call(
        body,
        out_shape=outs,
        in_specs=[SMEM] * scalars + [VMEM] * (len(args) - scalars),
        out_specs=jax.tree.map(lambda _: VMEM, outs),
        scratch_shapes=list(scratch),
        compiler_params=pltpu.CompilerParams(vmem_limit_bytes=40 * 2**20),
        cost_estimate=pl.CostEstimate(flops=flops, bytes_accessed=0, transcendentals=0)
        if flops
        else None,
    )(*args)


def pack_body(flux_ref, ivar_ref, target_ref, send_ref, weighted_ref):
    weighted_ref[...] = (
        ivar_ref[...].astype(F32) * flux_ref[...].astype(F32)
    ).astype(BF)
    rows = flux_ref.shape[0]
    at = lax.broadcasted_iota(jnp.int32, (rows, ROWS), 0) + pl.program_id(0) * rows
    here = at == lax.broadcasted_iota(jnp.int32, (rows, ROWS), 1)
    target = jnp.where(here, jnp.broadcast_to(target_ref[...], (rows, ROWS)), 0)
    target = jnp.broadcast_to(jnp.sum(target, axis=1, keepdims=True), (rows, LANES))
    peer, local = target // 128, target % 32
    index = (local // 16) * 1024 + (peer % 2) * 512 + (peer // 2) * 16 + local % 16
    lane = lax.broadcasted_iota(jnp.int32, (rows, LANES), 1)
    extra = jnp.where(lane == 0, index // 64, jnp.where(lane == 1, index % 64, 0))
    extra = extra.astype(F32).astype(BF)
    for dev in range(N_TGT):
        span = slice(dev * PIX, dev * PIX + PIX)
        send_ref[dev, :, 0:PIX] = weighted_ref[:, span]
        send_ref[dev, :, PIX:LANES] = extra[:, 0:LANES - PIX]
        send_ref[dev, :, LANES:LANES + PIX] = ivar_ref[:, span]
        send_ref[dev, :, LANES + PIX:2 * LANES] = jnp.zeros((rows, LANES - PIX), BF)


def pack(flux, ivar, target):
    rows, wide = 32, flux.shape[1]
    return pl.pallas_call(
        pack_body,
        grid=(ROWS // rows,),
        out_shape=sds(N_TGT, ROWS, 2 * LANES, dtype=BF),
        in_specs=[
            pl.BlockSpec((rows, wide), lambda i: (i, 0)),
            pl.BlockSpec((rows, wide), lambda i: (i, 0)),
            pl.BlockSpec((1, ROWS), lambda i: (0, 0)),
        ],
        out_specs=pl.BlockSpec((N_TGT, rows, 2 * LANES), lambda i: (0, i, 0)),
        scratch_shapes=[pltpu.VMEM((rows, wide), BF)],
        compiler_params=pltpu.CompilerParams(vmem_limit_bytes=60 * 2**20),
        cost_estimate=pl.CostEstimate(
            flops=2 * ROWS * wide, bytes_accessed=8 * ROWS * wide, transcendentals=0
        ),
    )(flux, ivar, target)


def template_pair(templ_bf):
    none = jnp.zeros_like(templ_bf)
    return jnp.concatenate(
        [
            jnp.concatenate([templ_bf, none], axis=1),
            jnp.concatenate([none, templ_bf], axis=1),
        ],
        axis=0,
    )


def cross_block(core, block, spectra, pair, keep_ref, send_ref, less=None):
    part = lax.dot_general(spectra, pair, NT, preferred_element_type=F32)
    start = block % 2 * 256
    place = pl.ds(start if isinstance(start, int) else pl.multiple_of(start, 256), 256)

    @pl.when(block // 2 == core)
    def _():
        keep_ref[place, :] = part if less is None else part - less(0, place)

    @pl.when(block // 2 != core)
    def _():
        send_ref[place, :] = part if less is None else part - less(1, place)


def coadd_body(core_ref, got_ref, templ_ref, spectra_ref, keep_ref, send_ref, low_ref, high_ref):
    lane = lax.broadcasted_iota(jnp.int32, (16, 2 * LANES), 1)
    row = lax.broadcasted_iota(jnp.int32, (16, 2 * LANES), 0)
    pick = jnp.where(lane == PIX + row, 1.0, 0.0)
    pick = jnp.where(row < 2, pick, 0.0).astype(BF)
    ids = lax.dot_general(pick, got_ref[...], NT, preferred_element_type=F32)
    high_ref[...] = jnp.broadcast_to(ids[0:1, :], high_ref.shape)
    low = ids[1:2, :].astype(jnp.int32)
    low_ref[...] = jnp.where(
        low == lax.broadcasted_iota(jnp.int32, low_ref.shape, 0), 1.0, 0.0
    ).astype(BF)
    inside = lax.broadcasted_iota(jnp.int32, (256, LANES), 1) < PIX
    pair = template_pair(templ_ref[...].astype(BF))

    def block_step(block, carry):
        first = (block * 4).astype(F32)
        selector = jnp.concatenate(
            [
                low_ref[...]
                * jnp.where(high_ref[0:1, :] == first + float(half * 16 + i), 1.0, 0.0).astype(BF)
                for half in range(2)
                for i in range(4)
            ],
            axis=0,
        )
        sums = jnp.dot(selector, got_ref[...], preferred_element_type=F32)
        coadd = sums[:, 0:LANES] / (sums[:, LANES:] + PRIOR_IVAR)
        for half in range(2):
            spectra_ref[
                pl.ds(pl.multiple_of(block * 256, 256), 256),
                half * LANES:(half + 1) * LANES,
            ] = jnp.where(inside, coadd[half * 256:(half + 1) * 256, :], 0.0).astype(BF)
        spectra = spectra_ref[pl.ds(pl.multiple_of(block * 256, 256), 256), :]
        cross_block(core_ref[0], block, spectra, pair, keep_ref, send_ref)
        return carry

    lax.fori_loop(0, 4, block_step, 0)


def spread(value, lane):
    width = value.shape[1]
    wide = jnp.concatenate(
        [value, jnp.zeros((value.shape[0], LANES - width), F32)], axis=1
    )
    return wide if lane == 0 else pltpu.roll(wide, lane, 1)


def pack_gram(gram):
    top = spread(gram[0:16, :], 0) + spread(gram[16:32, :], 64)
    corner = gram[32:64, 32:64]
    low = sum(spread(corner[8 * i:8 * i + 8, :], 32 * i) for i in range(4))
    return jnp.concatenate([top, low], axis=0)


def unpack_gram(packed):
    top = jnp.concatenate(
        [packed[0:16, :], pltpu.roll(packed[0:16, :], 64, 1)], axis=0
    )[:, 0:RANK]
    low = packed[16:24, :]
    corner = jnp.concatenate(
        [low] + [pltpu.roll(low, LANES - 32 * i, 1) for i in range(1, 4)], axis=0
    )
    side = pad_to(top, LANES, LANES).T[32:64, :]
    lane = lax.broadcasted_iota(jnp.int32, (32, LANES), 1)
    bottom = jnp.where(lane < 32, side, pltpu.roll(corner, 32, 1))
    return jnp.concatenate([top, bottom[:, 0:RANK]], axis=0)


def exact(left, right):
    return jnp.dot(left, right, precision=lax.Precision.HIGHEST, preferred_element_type=F32)


def descend(state, residual, gram):
    eye = lax.broadcasted_iota(jnp.int32, (RANK, RANK), 0) == lax.broadcasted_iota(
        jnp.int32, (RANK, RANK), 1
    )
    pivot = jnp.sum(jnp.where(eye, gram, 0.0), axis=1, keepdims=True) + EPSILON
    inverse = 1.0 / pivot
    goal = state + residual * inverse
    scaled = gram * inverse
    goals = [goal[8 * i:8 * i + 8, :] for i in range(8)]
    done = []
    for k in range(RANK):
        old = state[k:k + 1, :]
        new = jnp.maximum(goals[k // 8][k % 8:k % 8 + 1, :], 0.0)
        done.append(new)
        change = new - old
        for i in range(k // 8, 8):
            goals[i] = goals[i] - scaled[8 * i:8 * i + 8, k:k + 1] * change
    return jnp.concatenate(done, axis=0)


def pad_to(value, rows, lanes):
    if value.shape[1] < lanes:
        value = jnp.concatenate(
            [value, jnp.zeros((value.shape[0], lanes - value.shape[1]), F32)], axis=1
        )
    if value.shape[0] < rows:
        value = jnp.concatenate(
            [value, jnp.zeros((rows - value.shape[0], value.shape[1]), F32)], axis=0
        )
    return value


def activation_body(first, *refs):
    if first:
        cross_ref, gram_ref, state_ref, new_ref, out_ref = refs
    else:
        cross_ref, state_ref, new_ref, out_ref = refs
    total = jnp.sum(cross_ref[...].astype(F32), axis=0)
    cross = pad_to(total[0:16, :], LANES, LANES).T
    wanted = cross[0:64, :] + pltpu.roll(cross[64:128, :], 16, 1)
    gram = unpack_gram(gram_ref[...] if first else total[16:40, :])
    if first:
        state = pad_to(state_ref[...], LANES, LANES).T[0:RANK, :]
    else:
        state = state_ref[...]
    rest = state if first else state - state.astype(BF).astype(F32)
    updated = descend(state, wanted - exact(gram, rest), gram)
    if first:
        new_ref[...] = updated
    else:
        new_ref[...] = pad_to(updated, LANES, LANES).T[0:32, 0:RANK]
    both = jnp.concatenate([updated, pltpu.roll(updated, LANES - 16, 1)], axis=0).T
    out_ref[...] = jnp.broadcast_to(both[0:16, :].astype(BF)[None], out_ref.shape)


def project_body(core_ref, own_ref, other_ref, spectra_ref, out_ref):
    core = core_ref[0]
    proj, gram = 0.0, 0.0
    for ref, at in ((own_ref, core), (other_ref, 1 - core)):
        rows = spectra_ref[pl.ds(pl.multiple_of(at * 512, 512), 512), :]
        proj += lax.dot_general(ref[...], rows, TN, preferred_element_type=F32)
        gram += lax.dot_general(ref[...], ref[...], TN, preferred_element_type=F32)
    out_ref[0:64, :] = proj[0:64, 0:LANES] + proj[64:128, LANES:]
    gram = gram[0:64, 0:64] + pltpu.roll(gram[64:128, :], 64, 1)[:, 0:64]
    out_ref[64:88, :] = pack_gram(gram)


def new_templates(part_refs, templ_ref):
    one, two, three, four = (ref[...] for ref in part_refs)
    total = (one + three) + (two + four)
    templ, gram = templ_ref[...], unpack_gram(total[64:88, :])
    return descend(templ, total[0:64, :] - exact(gram, templ), gram)


def template_body(core_ref, a_ref, b_ref, c_ref, d_ref, templ_ref, own_ref, other_ref, spectra_ref, new_ref, keep_ref, send_ref):
    updated = new_templates((a_ref, b_ref, c_ref, d_ref), templ_ref)
    new_ref[...] = updated
    templ_bf = updated.astype(BF)
    full = lax.dot_general(templ_bf, templ_bf, NT, preferred_element_type=F32)
    square = template_pair(full)
    high = square.astype(BF)
    low = (square - high.astype(F32)).astype(BF)

    def fitted(which, place):
        rows = (own_ref, other_ref)[which][place, :]
        return jnp.dot(rows, high, preferred_element_type=F32) + jnp.dot(
            rows, low, preferred_element_type=F32
        )

    gram = pack_gram(full)
    keep_ref[512:536, :] = gram
    send_ref[512:536, :] = gram
    pair = template_pair(templ_bf)
    for block in range(4):
        spectra = spectra_ref[block * 256:(block + 1) * 256, :]
        cross_block(core_ref[0], block, spectra, pair, keep_ref, send_ref, fitted)


def last_template_body(a_ref, b_ref, c_ref, d_ref, templ_ref, new_ref):
    updated = new_templates((a_ref, b_ref, c_ref, d_ref), templ_ref)
    new_ref[...] = updated[:, 0:PIX]


def first_gram_body(templ_ref, gram_ref):
    templ_bf = templ_ref[...].astype(BF)
    gram_ref[...] = pack_gram(
        lax.dot_general(templ_bf, templ_bf, NT, preferred_element_type=F32)
    )


def shift(value, axis, size, by):
    return lax.ppermute(value, axis, [(i, (i + by) % size) for i in range(size)])


def ring_sum(value, axis, size, step):
    return (value + shift(value, axis, size, 2 * step)) + (
        shift(value, axis, size, step) + shift(value, axis, size, 3 * step)
    )


def from_ahead(value, by):
    pairs = [
        ((z + 2 * y + by) % NZ * NY + y, z * NY + y) for z in range(NZ) for y in range(NY)
    ]
    return lax.ppermute(value, ("z", "y"), pairs)


def two_along_z(part):
    return from_ahead(part, 0) + from_ahead(part, 1)


def near(part):
    return ring_sum(part + shift(part, "c", NC, 1), "x", NX, 1)


def message_body(keep_ref, came_ref, out_ref):
    cross = (keep_ref[0:512, :] + came_ref[0:512, :]).reshape(32, 16, LANES)
    if out_ref.shape[1] > 16:
        gram = keep_ref[512:536, :] + came_ref[512:536, :]
        gram = jnp.broadcast_to(gram[None], (32, 24, LANES))
        cross = jnp.concatenate([cross, gram], axis=1)
    out_ref[...] = cross.astype(out_ref.dtype)


def sds(*shape, dtype=F32):
    return jax.ShapeDtypeStruct(shape, dtype)


def shards(flux, ivar, row_target, start_w, start_h):
    core = lax.axis_index("c").astype(jnp.int32).reshape(1)
    send = pack(flux, ivar, row_target.reshape(1, ROWS))
    templates = jnp.pad(start_h, ((0, 0), (0, LANES - PIX)))
    got = lax.all_to_all(send, TGT, split_axis=0, concat_axis=0, tiled=True)
    gram = near(call(first_gram_body, sds(24, LANES), (templates,)))
    got, gram = lax.optimization_barrier((got, gram))
    gram = two_along_z(gram)
    spectra, keep, away = call(
        coadd_body,
        (sds(1024, 2 * LANES, dtype=BF), sds(512, LANES), sds(512, LANES)),
        (core, got.reshape(N_TGT * ROWS, 2 * LANES), templates),
        scratch=[pltpu.VMEM((64, N_TGT * ROWS), BF), pltpu.VMEM((8, N_TGT * ROWS), F32)],
        scalars=1,
        flops=2 * 2048 * N_TGT * ROWS * 2 * LANES,
    )
    keep, away, gram = lax.optimization_barrier((keep, away, gram))
    gram = ring_sum(gram, "y", NY, 1)
    state = start_w
    for sweep in range(SWEEPS):
        first = sweep == 0
        cross = call(
            message_body,
            sds(32, 16, LANES) if first else sds(32, 40, LANES, dtype=BF),
            (keep, shift(away, "c", NC, 1)),
        )
        cross = lax.all_to_all(cross, ("x", "z"), split_axis=0, concat_axis=0, tiled=True)
        state, message = call(
            lambda *refs, first=first: activation_body(first, *refs),
            (sds(RANK, LANES) if first else sds(32, RANK), sds(32, 16, LANES, dtype=BF)),
            (cross, gram, state) if first else (cross, state),
        )
        own = lax.all_to_all(message, ("x", "z"), split_axis=0, concat_axis=0, tiled=True)
        own = own.reshape(512, LANES)
        other = shift(own, "c", NC, 1)
        part = call(
            project_body, sds(88, LANES), (core, own, other, spectra), scalars=1
        )
        parts = (part, *(shift(part, "y", NY, by) for by in (1, 2, 3)))
        if first:
            templates, keep, away = call(
                template_body,
                (sds(RANK, LANES), sds(536, LANES), sds(536, LANES)),
                (core, *parts, templates, own, other, spectra),
                scalars=1,
            )
        else:
            templates = call(last_template_body, sds(RANK, PIX), (*parts, templates))
    return state, templates


def solution(mesh):
    grid = Mesh(mesh.devices.reshape(NX, NZ, NC, NY), ("x", "z", "c", "y"))
    every = ("x", "z", "c", "y")
    return jax.shard_map(
        shards,
        mesh=grid,
        in_specs=(P(every, None), P(every, None), P(every), P(every, None), P(None, TGT)),
        out_specs=(P(every, None), P(None, TGT)),
        check_vma=False,
    )
```

time: 198 us -> 178 us (0.90)
  waiting for transfers between devices: 73.7 us -> 56.2 us
  blocking collectives: 54.6 us -> 48.1 us
  starting transfers between devices: 48.4 us -> 53.7 us
  local copies, waits for them, and re-layouts: 5.22 us -> 0.02 us
  Pallas kernels: 13.7 us -> 18.2 us
    all_to_all x2 -> x1, waiting for transfers between devices: 16.3 us -> 0.01 us  [shards(): lax.all_to_all(cross, ('x', 'z'), split_axis=0, concat_axis=0, tiled=True)]
    all_to_all x2 -> x1, blocking collectives: 26.1 us -> 13.7 us  [shards(): lax.all_to_all(cross, ('x', 'z'), split_axis=0, concat_axis=0, tiled=True)]
    all_to_all x2, blocking collectives: 28.5 us -> 34.4 us  [shards(): lax.all_to_all(message, ('x', 'z'), split_axis=0, concat_axis=0, tiled=True)]
    ppermute x18 -> x17, starting transfers between devices: 28.2 us -> 33.6 us  [shift(): lax.ppermute(value, axis, [(i, (i + by) % size) for i in range(size)])]
    unnamed x10 -> x4, local copies, waits for them, and re-layouts: 3.77 us -> 0.01 us
    pallas_call x0 -> x1, Pallas kernels: none -> 3.57 us  [pack(): pl.pallas_call(pack_body, grid=(ROWS // rows,), out_shape=sds(N_TGT, ROWS...]
    all_to_all x1, waiting for transfers between devices: 45.3 us -> 42.4 us  [shards(): got = lax.all_to_all(send, TGT, split_axis=0, concat_axis=0, tiled=True)]
    ppermute x18 -> x17, waiting for transfers between devices: 12.1 us -> 13.8 us  [shift(): lax.ppermute(value, axis, [(i, (i + by) % size) for i in range(size)])]
  transfers between devices with their start and end apart: 21 -> 21, of which waited for: 13 -> 15; matrix products, arithmetic and copies ran while one was open for 1% -> 0% of each run, Pallas kernels for 3% -> 4%
where the time goes in v2:
time: 178 us; the launch traced here: 177 us
  waiting for transfers between devices  56.2 us (32%)
  starting transfers between devices  53.7 us (30%)
  blocking collectives  48.1 us (27%)
  Pallas kernels  18.2 us (10%)
    all_to_all x1, waiting for transfers between devices, shards(): got = lax.all_to_all(send, TGT, split_axis=0, concat_axis=0, tiled=True)  42.4 us
    all_to_all x2, blocking collectives, shards(): lax.all_to_all(message, ('x', 'z'), split_axis=0, concat_axis=0, tiled=True)  34.4 us
    ppermute x17, starting transfers between devices, shift(): lax.ppermute(value, axis, [(i, (i + by) % size) for i in range(size)])  33.6 us
    pallas_call x10, Pallas kernels, call(): pl.pallas_call(body, out_shape=outs, in_specs=[SMEM] * scalars + [VMEM] *...  14.7 us
    ppermute x17, waiting for transfers between devices, shift(): lax.ppermute(value, axis, [(i, (i + by) % size) for i in range(size)])  13.8 us
    all_to_all x1, blocking collectives, shards(): lax.all_to_all(cross, ('x', 'z'), split_axis=0, concat_axis=0, tiled=True)  13.7 us
    all_to_all x1, starting transfers between devices, shards(): got = lax.all_to_all(send, TGT, split_axis=0, concat_axis=0, tiled=True)  13.1 us
    all_to_all x1, starting transfers between devices, shards(): lax.all_to_all(cross, ('x', 'z'), split_axis=0, concat_axis=0, tiled=True)  6.23 us
  transfers between devices with their start and end apart: 21, of which 15 were waited for; matrix products, arithmetic and copies ran while one was open for 0% of the time, Pallas kernels for 4%

profile of v2, /device:TPU:1, one launch (start us, length us, event | category | flops | bytes accessed | tf_op | source)
XLA Modules:
  0.0 177.0 jit_solution(16399659013733575074)
XLA Ops:
  0.6 3.6 %shard_map.68 = bf16[64,64,256]{2,1,0:T(8,128)(2,1)} custom-call(bf16[64,7808]{1,0:T(8,128)(2,1)} %flux_ref.1, bf16[64,7808]{1,0:T(8,128)(2,1)} %ivar_ref.1, s32[1,64]{1,0:T(1,128)} %bitcast.11), custom_call_target="tpu_custom_call" | custom-call | flops 999424 | bytes 3997696 | tf_op jit(solution)/shard_map/pallas_call | solution.py:65
  4.2 13.1 %all-to-all-start = ((bf16[64,64,256]{2,1,0:T(8,128)(2,1)}), bf16[64,64,256]{2,1,0:T(8,128)(2,1)S(1)}, u32[]{:S(2)}, u32[]{:S(2)}) async-start(bf16[64,64,256]{2,1,0:T(8,128)(2,1)} %shard_map.68), calls=%async_computation | async-start | bytes 4194304 | tf_op jit(solution)/shard_map/all_to_all | solution.py:332
  20.2 1.4 collective-permute-start.3
  21.7 1.6 collective-permute-start.1
  23.7 2.4 %collective-permute-done.1 = f32[24,128]{1,0:T(8,128)S(1)} collective-permute-done((f32[24,128]{1,0:T(8,128)S(1)}, f32[24,128]{1,0:T(8,128)S(1)}, u32[]{:S(2)}, u32[]{:S(2)}) %collective-permute-start.1) | collective-permute-done | bytes 12320 | tf_op jit(solution)/shard_map/ppermute | solution.py:291
  26.2 42.4 %all-to-all-done = bf16[64,64,256]{2,1,0:T(8,128)(2,1)S(1)} async-done(((bf16[64,64,256]{2,1,0:T(8,128)(2,1)}), bf16[64,64,256]{2,1,0:T(8,128)(2,1)S(1)}, u32[]{:S(2)}, u32[]{:S(2)}) %all-to-all-start) | async-done | bytes 2097184 | tf_op jit(solution)/shard_map/all_to_all | solution.py:332
  69.3 6.5 %shard_map.70 = (bf16[1024,256]{1,0:T(8,128)(2,1)S(1)}, f32[512,128]{1,0:T(8,128)S(1)}, f32[512,128]{1,0:T(8,128)S(1)}) custom-call(s32[1]{0:T(128)} %bitcast.core_ref, bf16[4096,256]{1,0:T(8,128)(2,1)S(1)} %bitcast.5, f32[64,128]{1,0:T(8,128)S(1)} %pad.4.templ_ref), custom_call_target="tpu_custom_call" | custom-call | flops 4294967296 | tf_op jit(solution)/shard_map/pallas_call | solution.py:28
  78.8 6.2 %all-to-all-start.1 = ((f32[32,16,128]{2,1,0:T(8,128)}), f32[32,16,128]{2,1,0:T(8,128)S(1)}, u32[]{:S(2)}, u32[]{:S(2)}) async-start(f32[32,16,128]{2,1,0:T(8,128)} %shard_map.71), calls=%async_computation.1 | async-start | bytes 524288 | tf_op jit(solution)/shard_map/all_to_all | solution.py:354
  85.0 5.4 %collective-permute-start.8 = (f32[24,128]{1,0:T(8,128)S(1)}, f32[24,128]{1,0:T(8,128)S(1)}, u32[]{:S(2)}, u32[]{:S(2)}) collective-permute-start(f32[24,128]{1,0:T(8,128)S(1)} %add.30), channel_id=1, source_target_pairs={{0,1},{1,2},{2,3},{3,0},{4,5},{5,6},{6,7},{7,4},{8,9},{9,10},{10,1... | collective-permute-start | bytes 36872 | tf_op jit(solution)/shard_map/ppermute | solution.py:291
  91.1 3.7 %collective-permute-start.7 = (f32[24,128]{1,0:T(8,128)S(1)}, f32[24,128]{1,0:T(8,128)S(1)}, u32[]{:S(2)}, u32[]{:S(2)}) collective-permute-start(f32[24,128]{1,0:T(8,128)S(1)} %add.30), channel_id=1, source_target_pairs={{0,2},{1,3},{2,0},{3,1},{4,6},{5,7},{6,4},{7,5},{8,10},{9,11},{10,... | collective-permute-start | bytes 36872 | tf_op jit(solution)/shard_map/ppermute | solution.py:291
  94.8 1.4 collective-permute-done.7
  97.2 18.0 %all_to_all.25 = bf16[32,16,128]{2,1,0:T(8,128)(2,1)S(1)} all-to-all(bf16[32,16,128]{2,1,0:T(8,128)(2,1)S(1)} %get-tuple-element.24), channel_id=1, replica_groups=mesh['x'=4,'z'=8,'c'=2,'y'=4] {'x','z'}, dimensions={0} | all-to-all | bytes 262144 | tf_op jit(solution)/shard_map/all_to_all | solution.py:360
  115.2 3.8 %collective-permute-start.10 = (bf16[512,128]{1,0:T(8,128)(2,1)S(1)}, bf16[512,128]{1,0:T(8,128)(2,1)S(1)}, u32[]{:S(2)}, u32[]{:S(2)}) collective-permute-start(bf16[512,128]{1,0:T(8,128)(2,1)S(1)} %bitcast.6), channel_id=1, source_target_pairs={{0,4},{4,0},{1,5},{5,1},{2,6},{6,2},{3,7},{7,3},{8,12},{12,8},{9,1... | collective-permute-start | bytes 393224 | tf_op jit(solution)/shard_map/ppermute | solution.py:291
  121.8 2.2 %collective-permute-start.12 = (f32[88,128]{1,0:T(8,128)S(1)}, f32[88,128]{1,0:T(8,128)S(1)}, u32[]{:S(2)}, u32[]{:S(2)}) collective-permute-start(f32[88,128]{1,0:T(8,128)S(1)} %shard_map.73.a_ref), channel_id=1, source_target_pairs={{0,2},{1,3},{2,0},{3,1},{4,6},{5,7},{6,4},{7,5},{8,10},{9,11},{10,... | collective-permute-start | bytes 135176 | tf_op jit(solution)/shard_map/ppermute | solution.py:291
  124.0 2.0 %collective-permute-start.13 = (f32[88,128]{1,0:T(8,128)S(1)}, f32[88,128]{1,0:T(8,128)S(1)}, u32[]{:S(2)}, u32[]{:S(2)}) collective-permute-start(f32[88,128]{1,0:T(8,128)S(1)} %shard_map.73.a_ref), channel_id=1, source_target_pairs={{0,3},{1,0},{2,1},{3,2},{4,7},{5,4},{6,5},{7,6},{8,11},{9,8},{10,9... | collective-permute-start | bytes 135176 | tf_op jit(solution)/shard_map/ppermute | solution.py:291
  127.3 2.3 %shard_map.74 = (f32[64,128]{1,0:T(8,128)S(1)}, f32[536,128]{1,0:T(8,128)S(1)}, f32[536,128]{1,0:T(8,128)S(1)}) custom-call(s32[1]{0:T(128)} %bitcast.core_ref, f32[88,128]{1,0:T(8,128)S(1)} %shard_map.73.a_ref, f32[88,128]{1,0:T(8,128)S(1)} %collective-permute-done.11.b_ref, f32[88,128]{1,0:T(8,128)S(1)} %collective-permute-done.12.c_ref, ...), custom_call_target="tpu_custom_call" | custom-call | tf_op jit(solution)/shard_map/pallas_call | solution.py:28
  129.6 1.7 collective-permute-start.14
  132.6 13.7 %all_to_all.26.refs_0_ = bf16[32,40,128]{2,1,0:T(8,128)(2,1)S(1)} all-to-all(bf16[32,40,128]{2,1,0:T(8,128)(2,1)S(1)} %shard_map.75), channel_id=1, replica_groups=mesh['x'=4,'z'=8,'c'=2,'y'=4] {'x','z'}, dimensions={0} | all-to-all | bytes 655360 | tf_op jit(solution)/shard_map/all_to_all | solution.py:354
  146.2 1.5 shard_map.76
  147.7 16.5 %all_to_all.27 = bf16[32,16,128]{2,1,0:T(8,128)(2,1)S(1)} all-to-all(bf16[32,16,128]{2,1,0:T(8,128)(2,1)S(1)} %get-tuple-element.30), channel_id=1, replica_groups=mesh['x'=4,'z'=8,'c'=2,'y'=4] {'x','z'}, dimensions={0} | all-to-all | bytes 262144 | tf_op jit(solution)/shard_map/all_to_all | solution.py:360
  164.1 2.4 %collective-permute-start.15 = (bf16[512,128]{1,0:T(8,128)(2,1)S(1)}, bf16[512,128]{1,0:T(8,128)(2,1)S(1)}, u32[]{:S(2)}, u32[]{:S(2)}) collective-permute-start(bf16[512,128]{1,0:T(8,128)(2,1)S(1)} %bitcast.9), channel_id=1, source_target_pairs={{0,4},{4,0},{1,5},{5,1},{2,6},{6,2},{3,7},{7,3},{8,12},{12,8},{9,1... | collective-permute-start | bytes 393224 | tf_op jit(solution)/shard_map/ppermute | solution.py:291
  168.9 3.6 %collective-permute-start.17 = (f32[88,128]{1,0:T(8,128)S(1)}, f32[88,128]{1,0:T(8,128)S(1)}, u32[]{:S(2)}, u32[]{:S(2)}) collective-permute-start(f32[88,128]{1,0:T(8,128)S(1)} %shard_map.77.a_ref), channel_id=1, source_target_pairs={{0,2},{1,3},{2,0},{3,1},{4,6},{5,7},{6,4},{7,5},{8,10},{9,11},{10,... | collective-permute-start | bytes 135176 | tf_op jit(solution)/shard_map/ppermute | solution.py:291
  172.8 1.8 %collective-permute-done.17.c_ref = f32[88,128]{1,0:T(8,128)S(1)} collective-permute-done((f32[88,128]{1,0:T(8,128)S(1)}, f32[88,128]{1,0:T(8,128)S(1)}, u32[]{:S(2)}, u32[]{:S(2)}) %collective-permute-start.17) | collective-permute-done | bytes 45088 | tf_op jit(solution)/shard_map/ppermute | solution.py:291
  175.7 1.4 shard_map.78
  (41 shorter events, 17.7 us)
Async XLA Ops:
  4.2 13.1 %copy-start.1 = (f32[64,122]{1,0:T(8,128)S(1)}, f32[64,122]{1,0:T(8,128)}, u32[]{:S(2)}) copy-start(f32[64,122]{1,0:T(8,128)} %param.9) | copy-start | bytes 93700
  4.2 64.4 %all-to-all-start = ((bf16[64,64,256]{2,1,0:T(8,128)(2,1)}), bf16[64,64,256]{2,1,0:T(8,128)(2,1)S(1)}, u32[]{:S(2)}, u32[]{:S(2)}) async-start(bf16[64,64,256]{2,1,0:T(8,128)(2,1)} %shard_map.68), calls=%async_computation | async-start | bytes 4194304 | tf_op jit(solution)/shard_map/all_to_all | solution.py:332
  17.6 1.3 collective-permute-start
  18.9 4.5 %collective-permute-start.2 = (f32[24,128]{1,0:T(8,128)S(1)}, f32[24,128]{1,0:T(8,128)S(1)}, u32[]{:S(2)}, u32[]{:S(2)}) collective-permute-start(f32[24,128]{1,0:T(8,128)S(1)} %add.26), channel_id=1, source_target_pairs={{0,64},{64,128},{128,192},{192,0},{1,65},{65,129},{129,193},{193,1... | collective-permute-start | bytes 36872 | tf_op jit(solution)/shard_map/ppermute | solution.py:291
  20.2 3.5 %collective-permute-start.3 = (f32[24,128]{1,0:T(8,128)S(1)}, f32[24,128]{1,0:T(8,128)S(1)}, u32[]{:S(2)}, u32[]{:S(2)}) collective-permute-start(f32[24,128]{1,0:T(8,128)S(1)} %add.26), channel_id=1, source_target_pairs={{0,192},{64,0},{128,64},{192,128},{1,193},{65,1},{129,65},{193,129... | collective-permute-start | bytes 36872 | tf_op jit(solution)/shard_map/ppermute | solution.py:291
  21.7 4.5 %collective-permute-start.1 = (f32[24,128]{1,0:T(8,128)S(1)}, f32[24,128]{1,0:T(8,128)S(1)}, u32[]{:S(2)}, u32[]{:S(2)}) collective-permute-start(f32[24,128]{1,0:T(8,128)S(1)} %add.26), channel_id=1, source_target_pairs={{0,128},{64,192},{128,0},{192,64},{1,129},{65,193},{129,1},{193,65... | collective-permute-start | bytes 36872 | tf_op jit(solution)/shard_map/ppermute | solution.py:291
  68.6 7.2 %collective-permute-start.4 = (f32[24,128]{1,0:T(8,128)S(1)}, f32[24,128]{1,0:T(8,128)S(1)}, u32[]{:S(2)}, u32[]{:S(2)}) collective-permute-start(f32[24,128]{1,0:T(8,128)S(1)} %add_add_fusion.1), channel_id=1, source_target_pairs={{0,0},{17,1},{34,2},{51,3},{8,8},{25,9},{42,10},{59,11},{16,16},{3... | collective-permute-start | bytes 36872 | tf_op jit(solution)/shard_map/ppermute | solution.py:304
  69.2 6.6 %collective-permute-start.5 = (f32[24,128]{1,0:T(8,128)S(1)}, f32[24,128]{1,0:T(8,128)S(1)}, u32[]{:S(2)}, u32[]{:S(2)}) collective-permute-start(f32[24,128]{1,0:T(8,128)S(1)} %add_add_fusion.1), channel_id=1, source_target_pairs={{8,0},{25,1},{42,2},{59,3},{16,8},{33,9},{50,10},{3,11},{24,16},{4... | collective-permute-start | bytes 36872 | tf_op jit(solution)/shard_map/ppermute | solution.py:304
  69.3 26.9 %copy-start = (f32[32,64]{1,0:T(8,128)S(1)}, f32[32,64]{1,0:T(8,128)}, u32[]{:S(2)}) copy-start(f32[32,64]{1,0:T(8,128)} %refs_2_.1) | copy-start | bytes 24580
  75.8 2.2 %collective-permute-start.6 = (f32[512,128]{1,0:T(8,128)S(1)}, f32[512,128]{1,0:T(8,128)S(1)}, u32[]{:S(2)}, u32[]{:S(2)}) collective-permute-start(f32[512,128]{1,0:T(8,128)S(1)} %get-tuple-element.22), channel_id=1, source_target_pairs={{0,4},{4,0},{1,5},{5,1},{2,6},{6,2},{3,7},{7,3},{8,12},{12,8},{9,1... | collective-permute-start | bytes 786440 | tf_op jit(solution)/shard_map/ppermute | solution.py:291
  78.8 17.4 %all-to-all-start.1 = ((f32[32,16,128]{2,1,0:T(8,128)}), f32[32,16,128]{2,1,0:T(8,128)S(1)}, u32[]{:S(2)}, u32[]{:S(2)}) async-start(f32[32,16,128]{2,1,0:T(8,128)} %shard_map.71), calls=%async_computation.1 | async-start | bytes 524288 | tf_op jit(solution)/shard_map/all_to_all | solution.py:354
  85.0 9.8 %collective-permute-start.8 = (f32[24,128]{1,0:T(8,128)S(1)}, f32[24,128]{1,0:T(8,128)S(1)}, u32[]{:S(2)}, u32[]{:S(2)}) collective-permute-start(f32[24,128]{1,0:T(8,128)S(1)} %add.30), channel_id=1, source_target_pairs={{0,1},{1,2},{2,3},{3,0},{4,5},{5,6},{6,7},{7,4},{8,9},{9,10},{10,1... | collective-permute-start | bytes 36872 | tf_op jit(solution)/shard_map/ppermute | solution.py:291
  90.5 4.4 %collective-permute-start.9 = (f32[24,128]{1,0:T(8,128)S(1)}, f32[24,128]{1,0:T(8,128)S(1)}, u32[]{:S(2)}, u32[]{:S(2)}) collective-permute-start(f32[24,128]{1,0:T(8,128)S(1)} %add.30), channel_id=1, source_target_pairs={{0,3},{1,0},{2,1},{3,2},{4,7},{5,4},{6,5},{7,6},{8,11},{9,8},{10,9... | collective-permute-start | bytes 36872 | tf_op jit(solution)/shard_map/ppermute | solution.py:291
  91.1 5.1 %collective-permute-start.7 = (f32[24,128]{1,0:T(8,128)S(1)}, f32[24,128]{1,0:T(8,128)S(1)}, u32[]{:S(2)}, u32[]{:S(2)}) collective-permute-start(f32[24,128]{1,0:T(8,128)S(1)} %add.30), channel_id=1, source_target_pairs={{0,2},{1,3},{2,0},{3,1},{4,6},{5,7},{6,4},{7,5},{8,10},{9,11},{10,... | collective-permute-start | bytes 36872 | tf_op jit(solution)/shard_map/ppermute | solution.py:291
  115.2 4.8 %collective-permute-start.10 = (bf16[512,128]{1,0:T(8,128)(2,1)S(1)}, bf16[512,128]{1,0:T(8,128)(2,1)S(1)}, u32[]{:S(2)}, u32[]{:S(2)}) collective-permute-start(bf16[512,128]{1,0:T(8,128)(2,1)S(1)} %bitcast.6), channel_id=1, source_target_pairs={{0,4},{4,0},{1,5},{5,1},{2,6},{6,2},{3,7},{7,3},{8,12},{12,8},{9,1... | collective-permute-start | bytes 393224 | tf_op jit(solution)/shard_map/ppermute | solution.py:291
  120.5 5.5 %collective-permute-start.11 = (f32[88,128]{1,0:T(8,128)S(1)}, f32[88,128]{1,0:T(8,128)S(1)}, u32[]{:S(2)}, u32[]{:S(2)}) collective-permute-start(f32[88,128]{1,0:T(8,128)S(1)} %shard_map.73.a_ref), channel_id=1, source_target_pairs={{0,1},{1,2},{2,3},{3,0},{4,5},{5,6},{6,7},{7,4},{8,9},{9,10},{10,1... | collective-permute-start | bytes 135176 | tf_op jit(solution)/shard_map/ppermute | solution.py:291
  121.8 4.6 %collective-permute-start.12 = (f32[88,128]{1,0:T(8,128)S(1)}, f32[88,128]{1,0:T(8,128)S(1)}, u32[]{:S(2)}, u32[]{:S(2)}) collective-permute-start(f32[88,128]{1,0:T(8,128)S(1)} %shard_map.73.a_ref), channel_id=1, source_target_pairs={{0,2},{1,3},{2,0},{3,1},{4,6},{5,7},{6,4},{7,5},{8,10},{9,11},{10,... | collective-permute-start | bytes 135176 | tf_op jit(solution)/shard_map/ppermute | solution.py:291
  124.0 3.2 %collective-permute-start.13 = (f32[88,128]{1,0:T(8,128)S(1)}, f32[88,128]{1,0:T(8,128)S(1)}, u32[]{:S(2)}, u32[]{:S(2)}) collective-permute-start(f32[88,128]{1,0:T(8,128)S(1)} %shard_map.73.a_ref), channel_id=1, source_target_pairs={{0,3},{1,0},{2,1},{3,2},{4,7},{5,4},{6,5},{7,6},{8,11},{9,8},{10,9... | collective-permute-start | bytes 135176 | tf_op jit(solution)/shard_map/ppermute | solution.py:291
  129.6 2.9 %collective-permute-start.14 = (f32[536,128]{1,0:T(8,128)S(1)}, f32[536,128]{1,0:T(8,128)S(1)}, u32[]{:S(2)}, u32[]{:S(2)}) collective-permute-start(f32[536,128]{1,0:T(8,128)S(1)} %get-tuple-element.27), channel_id=1, source_target_pairs={{0,4},{4,0},{1,5},{5,1},{2,6},{6,2},{3,7},{7,3},{8,12},{12,8},{9,1... | collective-permute-start | bytes 823304 | tf_op jit(solution)/shard_map/ppermute | solution.py:291
  164.1 3.3 %collective-permute-start.15 = (bf16[512,128]{1,0:T(8,128)(2,1)S(1)}, bf16[512,128]{1,0:T(8,128)(2,1)S(1)}, u32[]{:S(2)}, u32[]{:S(2)}) collective-permute-start(bf16[512,128]{1,0:T(8,128)(2,1)S(1)} %bitcast.9), channel_id=1, source_target_pairs={{0,4},{4,0},{1,5},{5,1},{2,6},{6,2},{3,7},{7,3},{8,12},{12,8},{9,1... | collective-permute-start | bytes 393224 | tf_op jit(solution)/shard_map/ppermute | solution.py:291
  168.0 4.7 %collective-permute-start.16 = (f32[88,128]{1,0:T(8,128)S(1)}, f32[88,128]{1,0:T(8,128)S(1)}, u32[]{:S(2)}, u32[]{:S(2)}) collective-permute-start(f32[88,128]{1,0:T(8,128)S(1)} %shard_map.77.a_ref), channel_id=1, source_target_pairs={{0,1},{1,2},{2,3},{3,0},{4,5},{5,6},{6,7},{7,4},{8,9},{9,10},{10,1... | collective-permute-start | bytes 135176 | tf_op jit(solution)/shard_map/ppermute | solution.py:291
  168.9 5.6 %collective-permute-start.17 = (f32[88,128]{1,0:T(8,128)S(1)}, f32[88,128]{1,0:T(8,128)S(1)}, u32[]{:S(2)}, u32[]{:S(2)}) collective-permute-start(f32[88,128]{1,0:T(8,128)S(1)} %shard_map.77.a_ref), channel_id=1, source_target_pairs={{0,2},{1,3},{2,0},{3,1},{4,6},{5,7},{6,4},{7,5},{8,10},{9,11},{10,... | collective-permute-start | bytes 135176 | tf_op jit(solution)/shard_map/ppermute | solution.py:291
  172.5 3.2 %collective-permute-start.18 = (f32[88,128]{1,0:T(8,128)S(1)}, f32[88,128]{1,0:T(8,128)S(1)}, u32[]{:S(2)}, u32[]{:S(2)}) collective-permute-start(f32[88,128]{1,0:T(8,128)S(1)} %shard_map.77.a_ref), channel_id=1, source_target_pairs={{0,3},{1,0},{2,1},{3,2},{4,7},{5,4},{6,5},{7,6},{8,11},{9,8},{10,9... | collective-permute-start | bytes 135176 | tf_op jit(solution)/shard_map/ppermute | solution.py:291

commit v3 on v2

--- a/solution.py
+++ b/solution.py
@@ -210,14 +210,20 @@
 
 
 def activation_body(first, *refs):
-    if first:
-        cross_ref, gram_ref, state_ref, new_ref, out_ref = refs
-    else:
-        cross_ref, state_ref, new_ref, out_ref = refs
+    cross_ref, state_ref, new_ref, out_ref = refs
     total = jnp.sum(cross_ref[...].astype(F32), axis=0)
     cross = pad_to(total[0:16, :], LANES, LANES).T
     wanted = cross[0:64, :] + pltpu.roll(cross[64:128, :], 16, 1)
-    gram = unpack_gram(gram_ref[...] if first else total[16:40, :])
+    if first:
+        packed = jnp.concatenate(
+            [jnp.sum(cross_ref[NZ * i:NZ * i + NZ, 16:24, :], axis=0) for i in range(NX)],
+            axis=0,
+        )
+        gram = jnp.concatenate(
+            [packed[:, 0:RANK], pltpu.roll(packed, RANK, 1)[:, 0:RANK]], axis=0
+        )
+    else:
+        gram = unpack_gram(total[16:40, :])
     if first:
         state = pad_to(state_ref[...], LANES, LANES).T[0:RANK, :]
     else:
@@ -245,14 +251,13 @@
 
 
 def new_templates(part_refs, templ_ref):
-    one, two, three, four = (ref[...] for ref in part_refs)
-    total = (one + three) + (two + four)
+    total = part_refs[0][...] + part_refs[1][...]
     templ, gram = templ_ref[...], unpack_gram(total[64:88, :])
     return descend(templ, total[0:64, :] - exact(gram, templ), gram)
 
 
-def template_body(core_ref, a_ref, b_ref, c_ref, d_ref, templ_ref, own_ref, other_ref, spectra_ref, new_ref, keep_ref, send_ref):
-    updated = new_templates((a_ref, b_ref, c_ref, d_ref), templ_ref)
+def template_body(core_ref, a_ref, b_ref, templ_ref, own_ref, other_ref, spectra_ref, new_ref, keep_ref, send_ref):
+    updated = new_templates((a_ref, b_ref), templ_ref)
     new_ref[...] = updated
     templ_bf = updated.astype(BF)
     full = lax.dot_general(templ_bf, templ_bf, NT, preferred_element_type=F32)
@@ -275,16 +280,15 @@
         cross_block(core_ref[0], block, spectra, pair, keep_ref, send_ref, fitted)
 
 
-def last_template_body(a_ref, b_ref, c_ref, d_ref, templ_ref, new_ref):
-    updated = new_templates((a_ref, b_ref, c_ref, d_ref), templ_ref)
+def last_template_body(a_ref, b_ref, templ_ref, new_ref):
+    updated = new_templates((a_ref, b_ref), templ_ref)
     new_ref[...] = updated[:, 0:PIX]
 
 
 def first_gram_body(templ_ref, gram_ref):
     templ_bf = templ_ref[...].astype(BF)
-    gram_ref[...] = pack_gram(
-        lax.dot_general(templ_bf, templ_bf, NT, preferred_element_type=F32)
-    )
+    gram = lax.dot_general(templ_bf, templ_bf, NT, preferred_element_type=F32)
+    gram_ref[...] = spread(gram[0:32, :], 0) + spread(gram[32:64, :], 64)
 
 
 def shift(value, axis, size, by):
@@ -297,28 +301,21 @@
     )
 
 
-def from_ahead(value, by):
-    pairs = [
-        ((z + 2 * y + by) % NZ * NY + y, z * NY + y) for z in range(NZ) for y in range(NY)
-    ]
-    return lax.ppermute(value, ("z", "y"), pairs)
-
-
-def two_along_z(part):
-    return from_ahead(part, 0) + from_ahead(part, 1)
-
-
 def near(part):
     return ring_sum(part + shift(part, "c", NC, 1), "x", NX, 1)
 
 
+def first_message_body(quarter_ref, gram_ref, keep_ref, came_ref, out_ref):
+    rows = pl.ds(pl.multiple_of(quarter_ref[0] * 8, 8), 8)
+    out_ref[:, 0:16, :] = (keep_ref[...] + came_ref[...]).reshape(32, 16, LANES)
+    out_ref[:, 16:24, :] = jnp.broadcast_to(gram_ref[rows, :][None], (32, 8, LANES))
+
+
 def message_body(keep_ref, came_ref, out_ref):
     cross = (keep_ref[0:512, :] + came_ref[0:512, :]).reshape(32, 16, LANES)
-    if out_ref.shape[1] > 16:
-        gram = keep_ref[512:536, :] + came_ref[512:536, :]
-        gram = jnp.broadcast_to(gram[None], (32, 24, LANES))
-        cross = jnp.concatenate([cross, gram], axis=1)
-    out_ref[...] = cross.astype(out_ref.dtype)
+    gram = keep_ref[512:536, :] + came_ref[512:536, :]
+    gram = jnp.broadcast_to(gram[None], (32, 24, LANES))
+    out_ref[...] = jnp.concatenate([cross, gram], axis=1).astype(BF)
 
 
 def sds(*shape, dtype=F32):
@@ -330,9 +327,8 @@
     send = pack(flux, ivar, row_target.reshape(1, ROWS))
     templates = jnp.pad(start_h, ((0, 0), (0, LANES - PIX)))
     got = lax.all_to_all(send, TGT, split_axis=0, concat_axis=0, tiled=True)
-    gram = near(call(first_gram_body, sds(24, LANES), (templates,)))
+    gram = near(call(first_gram_body, sds(32, LANES), (templates,)))
     got, gram = lax.optimization_barrier((got, gram))
-    gram = two_along_z(gram)
     spectra, keep, away = call(
         coadd_body,
         (sds(1024, 2 * LANES, dtype=BF), sds(512, LANES), sds(512, LANES)),
@@ -341,21 +337,24 @@
         scalars=1,
         flops=2 * 2048 * N_TGT * ROWS * 2 * LANES,
     )
-    keep, away, gram = lax.optimization_barrier((keep, away, gram))
-    gram = ring_sum(gram, "y", NY, 1)
     state = start_w
     for sweep in range(SWEEPS):
         first = sweep == 0
-        cross = call(
-            message_body,
-            sds(32, 16, LANES) if first else sds(32, 40, LANES, dtype=BF),
-            (keep, shift(away, "c", NC, 1)),
-        )
+        came = shift(away, "c", NC, 1)
+        if first:
+            cross = call(
+                first_message_body,
+                sds(32, 24, LANES),
+                (lax.axis_index("x").astype(jnp.int32).reshape(1), gram, keep, came),
+                scalars=1,
+            )
+        else:
+            cross = call(message_body, sds(32, 40, LANES, dtype=BF), (keep, came))
         cross = lax.all_to_all(cross, ("x", "z"), split_axis=0, concat_axis=0, tiled=True)
         state, message = call(
             lambda *refs, first=first: activation_body(first, *refs),
             (sds(RANK, LANES) if first else sds(32, RANK), sds(32, 16, LANES, dtype=BF)),
-            (cross, gram, state) if first else (cross, state),
+            (cross, state),
         )
         own = lax.all_to_all(message, ("x", "z"), split_axis=0, concat_axis=0, tiled=True)
         own = own.reshape(512, LANES)
@@ -363,7 +362,8 @@
         part = call(
             project_body, sds(88, LANES), (core, own, other, spectra), scalars=1
         )
-        parts = (part, *(shift(part, "y", NY, by) for by in (1, 2, 3)))
+        part = part + lax.ppermute(part, "y", [(0, 1), (1, 0), (2, 3), (3, 2)])
+        parts = (part, lax.ppermute(part, "y", [(0, 3), (3, 0), (1, 2), (2, 1)]))
         if first:
             templates, keep, away = call(
                 template_body,

time: 178 us -> 174 us (0.978)
  starting transfers between devices: 53.7 us -> 33 us
  blocking collectives: 48.1 us -> 63.2 us
    ppermute x17 -> x8, starting transfers between devices: 33.6 us -> 12.8 us  [shift(): lax.ppermute(value, axis, [(i, (i + by) % size) for i in range(size)])]
    all_to_all x1 -> x2, blocking collectives: 13.7 us -> 30.2 us  [shards(): lax.all_to_all(cross, ('x', 'z'), split_axis=0, concat_axis=0, tiled=True)]
    ppermute x2 -> x4, waiting for transfers between devices: 0.01 us -> 7.28 us  [the longest x2 4.41 us: shards(): part = part + lax.ppermute(part, 'y', [(0, 1), (1, 0), (2, 3), (3, 2)])]
    ppermute x2 -> x4, starting transfers between devices: 0.73 us -> 7.11 us  [the longest x2 5.64 us: shards(): parts = (part, lax.ppermute(part, 'y', [(0, 3), (3, 0), (1, 2), (2, 1)]))]
    all_to_all x1 -> x0, starting transfers between devices: 6.23 us -> none  [shards(): lax.all_to_all(cross, ('x', 'z'), split_axis=0, concat_axis=0, tiled=True)]
    ppermute x17 -> x8, waiting for transfers between devices: 13.8 us -> 8.13 us  [shift(): lax.ppermute(value, axis, [(i, (i + by) % size) for i in range(size)])]
  transfers between devices with their start and end apart: 21 -> 13, of which waited for: 15 -> 13; matrix products, arithmetic and copies ran while one was open for 0% -> 0% of each run, Pallas kernels for 4% -> 0%
where the time goes in v3:
time: 174 us; the launch traced here: 172 us
  blocking collectives  63.2 us (36%)
  waiting for transfers between devices  57.8 us (33%)
  starting transfers between devices  33 us (19%)
  Pallas kernels  17.3 us (10%)
    all_to_all x1, waiting for transfers between devices, shards(): got = lax.all_to_all(send, TGT, split_axis=0, concat_axis=0, tiled=True)  42.4 us
    all_to_all x2, blocking collectives, shards(): lax.all_to_all(message, ('x', 'z'), split_axis=0, concat_axis=0, tiled=True)  33 us
    all_to_all x2, blocking collectives, shards(): lax.all_to_all(cross, ('x', 'z'), split_axis=0, concat_axis=0, tiled=True)  30.2 us
    pallas_call x10, Pallas kernels, call(): pl.pallas_call(body, out_shape=outs, in_specs=[SMEM] * scalars + [VMEM] *...  13.7 us
    all_to_all x1, starting transfers between devices, shards(): got = lax.all_to_all(send, TGT, split_axis=0, concat_axis=0, tiled=True)  13.1 us
    ppermute x8, starting transfers between devices, shift(): lax.ppermute(value, axis, [(i, (i + by) % size) for i in range(size)])  12.8 us
    ppermute x8, waiting for transfers between devices, shift(): lax.ppermute(value, axis, [(i, (i + by) % size) for i in range(size)])  8.13 us
    ppermute x2, starting transfers between devices, shards(): parts = (part, lax.ppermute(part, 'y', [(0, 3), (3, 0), (1, 2), (2, 1)]))  5.64 us
  transfers between devices with their start and end apart: 13, of which 13 were waited for; matrix products, arithmetic and copies ran while one was open for 0% of the time, Pallas kernels for 0%

profile of v3, /device:TPU:1, one launch (start us, length us, event | category | flops | bytes accessed | tf_op | source)
XLA Modules:
  0.0 172.1 jit_solution(16746934291021976321)
XLA Ops:
  0.6 3.6 %shard_map.68 = bf16[64,64,256]{2,1,0:T(8,128)(2,1)} custom-call(bf16[64,7808]{1,0:T(8,128)(2,1)} %flux_ref.1, bf16[64,7808]{1,0:T(8,128)(2,1)} %ivar_ref.1, s32[1,64]{1,0:T(1,128)} %bitcast.12), custom_call_target="tpu_custom_call" | custom-call | flops 999424 | bytes 3997696 | tf_op jit(solution)/shard_map/pallas_call | solution.py:65
  4.2 13.1 %all-to-all-start = ((bf16[64,64,256]{2,1,0:T(8,128)(2,1)}), bf16[64,64,256]{2,1,0:T(8,128)(2,1)S(1)}, u32[]{:S(2)}, u32[]{:S(2)}) async-start(bf16[64,64,256]{2,1,0:T(8,128)(2,1)} %shard_map.68), calls=%async_computation | async-start | bytes 4194304 | tf_op jit(solution)/shard_map/all_to_all | solution.py:329
  20.2 1.5 collective-permute-start.3
  21.6 1.6 collective-permute-start.1
  23.9 2.3 %collective-permute-done.1 = f32[32,128]{1,0:T(8,128)S(1)} collective-permute-done((f32[32,128]{1,0:T(8,128)S(1)}, f32[32,128]{1,0:T(8,128)S(1)}, u32[]{:S(2)}, u32[]{:S(2)}) %collective-permute-start.1) | collective-permute-done | bytes 16416 | tf_op jit(solution)/shard_map/ppermute | solution.py:295
  26.2 42.4 %all-to-all-done = bf16[64,64,256]{2,1,0:T(8,128)(2,1)S(1)} async-done(((bf16[64,64,256]{2,1,0:T(8,128)(2,1)}), bf16[64,64,256]{2,1,0:T(8,128)(2,1)S(1)}, u32[]{:S(2)}, u32[]{:S(2)}) %all-to-all-start) | async-done | bytes 2097184 | tf_op jit(solution)/shard_map/all_to_all | solution.py:329
  68.6 6.5 %shard_map.70 = (bf16[1024,256]{1,0:T(8,128)(2,1)S(1)}, f32[512,128]{1,0:T(8,128)S(1)}, f32[512,128]{1,0:T(8,128)S(1)}) custom-call(s32[1]{0:T(128)} %bitcast.core_ref, bf16[4096,256]{1,0:T(8,128)(2,1)S(1)} %bitcast.6, f32[64,128]{1,0:T(8,128)S(1)} %pad.4.templ_ref), custom_call_target="tpu_custom_call" | custom-call | flops 4294967296 | tf_op jit(solution)/shard_map/pallas_call | solution.py:28
  76.7 16.6 %all_to_all.25.refs_0_ = f32[32,24,128]{2,1,0:T(8,128)S(1)} all-to-all(f32[32,24,128]{2,1,0:T(8,128)S(1)} %shard_map.71), channel_id=1, replica_groups=mesh['x'=4,'z'=8,'c'=2,'y'=4] {'x','z'}, dimensions={0} | all-to-all | bytes 786432 | tf_op jit(solution)/shard_map/all_to_all | solution.py:353
  94.1 16.5 %all_to_all.26 = bf16[32,16,128]{2,1,0:T(8,128)(2,1)S(1)} all-to-all(bf16[32,16,128]{2,1,0:T(8,128)(2,1)S(1)} %get-tuple-element.18), channel_id=1, replica_groups=mesh['x'=4,'z'=8,'c'=2,'y'=4] {'x','z'}, dimensions={0} | all-to-all | bytes 262144 | tf_op jit(solution)/shard_map/all_to_all | solution.py:359
  110.6 2.5 %collective-permute-start.5 = (bf16[512,128]{1,0:T(8,128)(2,1)S(1)}, bf16[512,128]{1,0:T(8,128)(2,1)S(1)}, u32[]{:S(2)}, u32[]{:S(2)}) collective-permute-start(bf16[512,128]{1,0:T(8,128)(2,1)S(1)} %bitcast.7), channel_id=1, source_target_pairs={{0,4},{4,0},{1,5},{5,1},{2,6},{6,2},{3,7},{7,3},{8,12},{12,8},{9,1... | collective-permute-start | bytes 393224 | tf_op jit(solution)/shard_map/ppermute | solution.py:295
  114.6 1.3 collective-permute-start.6
  115.9 1.6 collective-permute-done.6
  117.6 2.8 %collective-permute-start.7 = (f32[88,128]{1,0:T(8,128)S(1)}, f32[88,128]{1,0:T(8,128)S(1)}, u32[]{:S(2)}, u32[]{:S(2)}) collective-permute-start(f32[88,128]{1,0:T(8,128)S(1)} %add.24.a_ref), channel_id=1, source_target_pairs={{0,3},{3,0},{1,2},{2,1},{4,7},{7,4},{5,6},{6,5},{8,11},{11,8},{9,1... | collective-permute-start | bytes 135176 | tf_op jit(solution)/shard_map/ppermute | solution.py:366
  120.4 1.4 collective-permute-done.7.b_ref
  121.8 2.3 %shard_map.74 = (f32[64,128]{1,0:T(8,128)S(1)}, f32[536,128]{1,0:T(8,128)S(1)}, f32[536,128]{1,0:T(8,128)S(1)}) custom-call(s32[1]{0:T(128)} %bitcast.core_ref, f32[88,128]{1,0:T(8,128)S(1)} %add.24.a_ref, f32[88,128]{1,0:T(8,128)S(1)} %collective-permute-done.7.b_ref, f32[64,128]{1,0:T(8,128)S(1)} %pad.4.templ_ref, bf16[512,128]{1,0:T(8,128)(2,1)S(1)} %bitcast.9, ...), custom_call_target="tpu_custom_call" | custom-call | tf_op jit(solution)/shard_map/pallas_call | solution.py:28
  124.1 2.7 %collective-permute-start.8 = (f32[536,128]{1,0:T(8,128)S(1)}, f32[536,128]{1,0:T(8,128)S(1)}, u32[]{:S(2)}, u32[]{:S(2)}) collective-permute-start(f32[536,128]{1,0:T(8,128)S(1)} %get-tuple-element.21), channel_id=1, source_target_pairs={{0,4},{4,0},{1,5},{5,1},{2,6},{6,2},{3,7},{7,3},{8,12},{12,8},{9,1... | collective-permute-start | bytes 823304 | tf_op jit(solution)/shard_map/ppermute | solution.py:295
  128.0 13.7 %all_to_all.27.refs_0_ = bf16[32,40,128]{2,1,0:T(8,128)(2,1)S(1)} all-to-all(bf16[32,40,128]{2,1,0:T(8,128)(2,1)S(1)} %shard_map.75), channel_id=1, replica_groups=mesh['x'=4,'z'=8,'c'=2,'y'=4] {'x','z'}, dimensions={0} | all-to-all | bytes 655360 | tf_op jit(solution)/shard_map/all_to_all | solution.py:353
  141.7 1.5 shard_map.76
  143.2 16.5 %all_to_all.28 = bf16[32,16,128]{2,1,0:T(8,128)(2,1)S(1)} all-to-all(bf16[32,16,128]{2,1,0:T(8,128)(2,1)S(1)} %get-tuple-element.24), channel_id=1, replica_groups=mesh['x'=4,'z'=8,'c'=2,'y'=4] {'x','z'}, dimensions={0} | all-to-all | bytes 262144 | tf_op jit(solution)/shard_map/all_to_all | solution.py:359
  159.6 2.4 %collective-permute-start.9 = (bf16[512,128]{1,0:T(8,128)(2,1)S(1)}, bf16[512,128]{1,0:T(8,128)(2,1)S(1)}, u32[]{:S(2)}, u32[]{:S(2)}) collective-permute-start(bf16[512,128]{1,0:T(8,128)(2,1)S(1)} %bitcast.10), channel_id=1, source_target_pairs={{0,4},{4,0},{1,5},{5,1},{2,6},{6,2},{3,7},{7,3},{8,12},{12,8},{9,1... | collective-permute-start | bytes 393224 | tf_op jit(solution)/shard_map/ppermute | solution.py:295
  163.6 2.8 %collective-permute-done.10 = f32[88,128]{1,0:T(8,128)S(1)} collective-permute-done((f32[88,128]{1,0:T(8,128)S(1)}, f32[88,128]{1,0:T(8,128)S(1)}, u32[]{:S(2)}, u32[]{:S(2)}) %collective-permute-start.10) | collective-permute-done | bytes 45088 | tf_op jit(solution)/shard_map/ppermute | solution.py:365
  166.4 2.8 %collective-permute-start.11 = (f32[88,128]{1,0:T(8,128)S(1)}, f32[88,128]{1,0:T(8,128)S(1)}, u32[]{:S(2)}, u32[]{:S(2)}) collective-permute-start(f32[88,128]{1,0:T(8,128)S(1)} %add.25.a_ref), channel_id=1, source_target_pairs={{0,3},{3,0},{1,2},{2,1},{4,7},{7,4},{5,6},{6,5},{8,11},{11,8},{9,1... | collective-permute-start | bytes 135176 | tf_op jit(solution)/shard_map/ppermute | solution.py:366
  169.3 1.4 collective-permute-done.11.b_ref
  170.7 1.4 shard_map.78
  (26 shorter events, 10.4 us)
Async XLA Ops:
  4.2 13.1 %copy-start.1 = (f32[64,122]{1,0:T(8,128)S(1)}, f32[64,122]{1,0:T(8,128)}, u32[]{:S(2)}) copy-start(f32[64,122]{1,0:T(8,128)} %param.9) | copy-start | bytes 93700
  4.2 64.4 %all-to-all-start = ((bf16[64,64,256]{2,1,0:T(8,128)(2,1)}), bf16[64,64,256]{2,1,0:T(8,128)(2,1)S(1)}, u32[]{:S(2)}, u32[]{:S(2)}) async-start(bf16[64,64,256]{2,1,0:T(8,128)(2,1)} %shard_map.68), calls=%async_computation | async-start | bytes 4194304 | tf_op jit(solution)/shard_map/all_to_all | solution.py:329
  17.5 1.3 collective-permute-start
  18.9 4.6 %collective-permute-start.2 = (f32[32,128]{1,0:T(8,128)S(1)}, f32[32,128]{1,0:T(8,128)S(1)}, u32[]{:S(2)}, u32[]{:S(2)}) collective-permute-start(f32[32,128]{1,0:T(8,128)S(1)} %add.20), channel_id=1, source_target_pairs={{0,64},{64,128},{128,192},{192,0},{1,65},{65,129},{129,193},{193,1... | collective-permute-start | bytes 49160 | tf_op jit(solution)/shard_map/ppermute | solution.py:295
  20.2 3.7 %collective-permute-start.3 = (f32[32,128]{1,0:T(8,128)S(1)}, f32[32,128]{1,0:T(8,128)S(1)}, u32[]{:S(2)}, u32[]{:S(2)}) collective-permute-start(f32[32,128]{1,0:T(8,128)S(1)} %add.20), channel_id=1, source_target_pairs={{0,192},{64,0},{128,64},{192,128},{1,193},{65,1},{129,65},{193,129... | collective-permute-start | bytes 49160 | tf_op jit(solution)/shard_map/ppermute | solution.py:295
  21.6 4.6 %collective-permute-start.1 = (f32[32,128]{1,0:T(8,128)S(1)}, f32[32,128]{1,0:T(8,128)S(1)}, u32[]{:S(2)}, u32[]{:S(2)}) collective-permute-start(f32[32,128]{1,0:T(8,128)S(1)} %add.20), channel_id=1, source_target_pairs={{0,128},{64,192},{128,0},{192,64},{1,129},{65,193},{129,1},{193,65... | collective-permute-start | bytes 49160 | tf_op jit(solution)/shard_map/ppermute | solution.py:295
  68.6 24.7 %copy-start = (f32[32,64]{1,0:T(8,128)S(1)}, f32[32,64]{1,0:T(8,128)}, u32[]{:S(2)}) copy-start(f32[32,64]{1,0:T(8,128)} %refs_1_.1) | copy-start | bytes 24580
  75.0 1.7 collective-permute-start.4
  110.6 3.4 %collective-permute-start.5 = (bf16[512,128]{1,0:T(8,128)(2,1)S(1)}, bf16[512,128]{1,0:T(8,128)(2,1)S(1)}, u32[]{:S(2)}, u32[]{:S(2)}) collective-permute-start(bf16[512,128]{1,0:T(8,128)(2,1)S(1)} %bitcast.7), channel_id=1, source_target_pairs={{0,4},{4,0},{1,5},{5,1},{2,6},{6,2},{3,7},{7,3},{8,12},{12,8},{9,1... | collective-permute-start | bytes 393224 | tf_op jit(solution)/shard_map/ppermute | solution.py:295
  114.6 2.9 %collective-permute-start.6 = (f32[88,128]{1,0:T(8,128)S(1)}, f32[88,128]{1,0:T(8,128)S(1)}, u32[]{:S(2)}, u32[]{:S(2)}) collective-permute-start(f32[88,128]{1,0:T(8,128)S(1)} %shard_map.73), channel_id=1, source_target_pairs={{0,1},{1,0},{2,3},{3,2},{4,5},{5,4},{6,7},{7,6},{8,9},{9,8},{10,11... | collective-permute-start | bytes 135176 | tf_op jit(solution)/shard_map/ppermute | solution.py:365
  117.6 4.3 %collective-permute-start.7 = (f32[88,128]{1,0:T(8,128)S(1)}, f32[88,128]{1,0:T(8,128)S(1)}, u32[]{:S(2)}, u32[]{:S(2)}) collective-permute-start(f32[88,128]{1,0:T(8,128)S(1)} %add.24.a_ref), channel_id=1, source_target_pairs={{0,3},{3,0},{1,2},{2,1},{4,7},{7,4},{5,6},{6,5},{8,11},{11,8},{9,1... | collective-permute-start | bytes 135176 | tf_op jit(solution)/shard_map/ppermute | solution.py:366
  124.1 3.9 %collective-permute-start.8 = (f32[536,128]{1,0:T(8,128)S(1)}, f32[536,128]{1,0:T(8,128)S(1)}, u32[]{:S(2)}, u32[]{:S(2)}) collective-permute-start(f32[536,128]{1,0:T(8,128)S(1)} %get-tuple-element.21), channel_id=1, source_target_pairs={{0,4},{4,0},{1,5},{5,1},{2,6},{6,2},{3,7},{7,3},{8,12},{12,8},{9,1... | collective-permute-start | bytes 823304 | tf_op jit(solution)/shard_map/ppermute | solution.py:295
  159.6 3.3 %collective-permute-start.9 = (bf16[512,128]{1,0:T(8,128)(2,1)S(1)}, bf16[512,128]{1,0:T(8,128)(2,1)S(1)}, u32[]{:S(2)}, u32[]{:S(2)}) collective-permute-start(bf16[512,128]{1,0:T(8,128)(2,1)S(1)} %bitcast.10), channel_id=1, source_target_pairs={{0,4},{4,0},{1,5},{5,1},{2,6},{6,2},{3,7},{7,3},{8,12},{12,8},{9,1... | collective-permute-start | bytes 393224 | tf_op jit(solution)/shard_map/ppermute | solution.py:295
  163.5 2.9 %collective-permute-start.10 = (f32[88,128]{1,0:T(8,128)S(1)}, f32[88,128]{1,0:T(8,128)S(1)}, u32[]{:S(2)}, u32[]{:S(2)}) collective-permute-start(f32[88,128]{1,0:T(8,128)S(1)} %shard_map.77), channel_id=1, source_target_pairs={{0,1},{1,0},{2,3},{3,2},{4,5},{5,4},{6,7},{7,6},{8,9},{9,8},{10,11... | collective-permute-start | bytes 135176 | tf_op jit(solution)/shard_map/ppermute | solution.py:365
  166.4 4.3 %collective-permute-start.11 = (f32[88,128]{1,0:T(8,128)S(1)}, f32[88,128]{1,0:T(8,128)S(1)}, u32[]{:S(2)}, u32[]{:S(2)}) collective-permute-start(f32[88,128]{1,0:T(8,128)S(1)} %add.25.a_ref), channel_id=1, source_target_pairs={{0,3},{3,0},{1,2},{2,1},{4,7},{7,4},{5,6},{6,5},{8,11},{11,8},{9,1... | collective-permute-start | bytes 135176 | tf_op jit(solution)/shard_map/ppermute | solution.py:366

commit v4 on v3

--- a/solution.py
+++ b/solution.py
@@ -91,21 +91,33 @@
     )
 
 
-def cross_block(core, block, spectra, pair, keep_ref, send_ref, less=None):
-    part = lax.dot_general(spectra, pair, NT, preferred_element_type=F32)
-    start = block % 2 * 256
-    place = pl.ds(start if isinstance(start, int) else pl.multiple_of(start, 256), 256)
-
-    @pl.when(block // 2 == core)
-    def _():
-        keep_ref[place, :] = part if less is None else part - less(0, place)
-
-    @pl.when(block // 2 != core)
-    def _():
-        send_ref[place, :] = part if less is None else part - less(1, place)
-
-
-def coadd_body(core_ref, got_ref, templ_ref, spectra_ref, keep_ref, send_ref, low_ref, high_ref):
+def coadd_rows(core, got_ref, low_ref, high_ref, spectra_ref):
+    inside = lax.broadcasted_iota(jnp.int32, (256, LANES), 1) < PIX
+
+    def block_step(block, carry):
+        first = (core * 8 + block * 4).astype(F32)
+        selector = jnp.concatenate(
+            [
+                low_ref[...]
+                * jnp.where(high_ref[0:1, :] == first + float(half * 16 + i), 1.0, 0.0).astype(BF)
+                for half in range(2)
+                for i in range(4)
+            ],
+            axis=0,
+        )
+        sums = jnp.dot(selector, got_ref[...], preferred_element_type=F32)
+        coadd = sums[:, 0:LANES] / (sums[:, LANES:] + PRIOR_IVAR)
+        for half in range(2):
+            spectra_ref[
+                pl.ds(pl.multiple_of(block * 256, 256), 256),
+                half * LANES:(half + 1) * LANES,
+            ] = jnp.where(inside, coadd[half * 256:(half + 1) * 256, :], 0.0).astype(BF)
+        return carry
+
+    lax.fori_loop(0, 2, block_step, 0)
+
+
+def away_body(core_ref, got_ref, away_ref, low_ref, high_ref):
     lane = lax.broadcasted_iota(jnp.int32, (16, 2 * LANES), 1)
     row = lax.broadcasted_iota(jnp.int32, (16, 2 * LANES), 0)
     pick = jnp.where(lane == PIX + row, 1.0, 0.0)
@@ -116,32 +128,19 @@
     low_ref[...] = jnp.where(
         low == lax.broadcasted_iota(jnp.int32, low_ref.shape, 0), 1.0, 0.0
     ).astype(BF)
-    inside = lax.broadcasted_iota(jnp.int32, (256, LANES), 1) < PIX
-    pair = template_pair(templ_ref[...].astype(BF))
-
-    def block_step(block, carry):
-        first = (block * 4).astype(F32)
-        selector = jnp.concatenate(
-            [
-                low_ref[...]
-                * jnp.where(high_ref[0:1, :] == first + float(half * 16 + i), 1.0, 0.0).astype(BF)
-                for half in range(2)
-                for i in range(4)
-            ],
-            axis=0,
-        )
-        sums = jnp.dot(selector, got_ref[...], preferred_element_type=F32)
-        coadd = sums[:, 0:LANES] / (sums[:, LANES:] + PRIOR_IVAR)
-        for half in range(2):
-            spectra_ref[
-                pl.ds(pl.multiple_of(block * 256, 256), 256),
-                half * LANES:(half + 1) * LANES,
-            ] = jnp.where(inside, coadd[half * 256:(half + 1) * 256, :], 0.0).astype(BF)
-        spectra = spectra_ref[pl.ds(pl.multiple_of(block * 256, 256), 256), :]
-        cross_block(core_ref[0], block, spectra, pair, keep_ref, send_ref)
-        return carry
-
-    lax.fori_loop(0, 4, block_step, 0)
+    coadd_rows(1 - core_ref[0], got_ref, low_ref, high_ref, away_ref)
+
+
+def keep_body(core_ref, got_ref, low_ref, high_ref, keep_ref):
+    coadd_rows(core_ref[0], got_ref, low_ref, high_ref, keep_ref)
+
+
+def cross_of(keep_ref, came_ref, own_bf, other_bf):
+    return lax.dot_general(
+        keep_ref[...], template_pair(own_bf), NT, preferred_element_type=F32
+    ) + lax.dot_general(
+        came_ref[...], template_pair(other_bf), NT, preferred_element_type=F32
+    )
 
 
 def spread(value, lane):
@@ -238,50 +237,53 @@
     out_ref[...] = jnp.broadcast_to(both[0:16, :].astype(BF)[None], out_ref.shape)
 
 
-def project_body(core_ref, own_ref, other_ref, spectra_ref, out_ref):
-    core = core_ref[0]
-    proj, gram = 0.0, 0.0
-    for ref, at in ((own_ref, core), (other_ref, 1 - core)):
-        rows = spectra_ref[pl.ds(pl.multiple_of(at * 512, 512), 512), :]
-        proj += lax.dot_general(ref[...], rows, TN, preferred_element_type=F32)
-        gram += lax.dot_general(ref[...], ref[...], TN, preferred_element_type=F32)
-    out_ref[0:64, :] = proj[0:64, 0:LANES] + proj[64:128, LANES:]
-    gram = gram[0:64, 0:64] + pltpu.roll(gram[64:128, :], 64, 1)[:, 0:64]
-    out_ref[64:88, :] = pack_gram(gram)
-
-
-def new_templates(part_refs, templ_ref):
-    total = part_refs[0][...] + part_refs[1][...]
-    templ, gram = templ_ref[...], unpack_gram(total[64:88, :])
-    return descend(templ, total[0:64, :] - exact(gram, templ), gram)
-
-
-def template_body(core_ref, a_ref, b_ref, templ_ref, own_ref, other_ref, spectra_ref, new_ref, keep_ref, send_ref):
-    updated = new_templates((a_ref, b_ref), templ_ref)
-    new_ref[...] = updated
+def project_body(activ_ref, keep_ref, came_ref, own_ref, send_ref):
+    activ = activ_ref[...]
+    gram = lax.dot_general(activ, activ, TN, preferred_element_type=F32)
+    gram = pack_gram(gram[0:64, 0:64] + pltpu.roll(gram[64:128, :], 64, 1)[:, 0:64])
+    blocks = []
+    for ref in (keep_ref, came_ref):
+        proj = lax.dot_general(activ, ref[...], TN, preferred_element_type=F32)
+        blocks.append(proj[0:64, 0:LANES] + proj[64:128, LANES:])
+    own_ref[0:24, :] = gram
+    own_ref[24:88, :] = blocks[0]
+    send_ref[0:24, :] = gram
+    send_ref[24:88, :] = blocks[1]
+    if own_ref.shape[0] > 88:
+        own_ref[88:152, :] = blocks[1]
+        send_ref[24:88, :] = blocks[1]
+        send_ref[88:152, :] = blocks[0]
+
+
+def new_templates(part_refs, templ):
+    one, two, three, four = (ref[...] for ref in part_refs)
+    total = (one + three) + (two + four)
+    gram, proj = unpack_gram(total[0:24, :]), total[24:88, :]
+    if total.shape[0] > 88:
+        proj = jnp.concatenate([proj, total[88:152, :]], axis=1)
+    return descend(templ, proj - exact(gram, templ), gram)
+
+
+def template_body(a_ref, b_ref, c_ref, d_ref, own_ref, other_ref, activ_ref, keep_ref, came_ref, new_ref, out_ref):
+    templ = jnp.concatenate([own_ref[...], other_ref[...]], axis=1)
+    updated = new_templates((a_ref, b_ref, c_ref, d_ref), templ)
+    new_ref[...] = updated[:, 0:LANES]
     templ_bf = updated.astype(BF)
     full = lax.dot_general(templ_bf, templ_bf, NT, preferred_element_type=F32)
     square = template_pair(full)
     high = square.astype(BF)
     low = (square - high.astype(F32)).astype(BF)
-
-    def fitted(which, place):
-        rows = (own_ref, other_ref)[which][place, :]
-        return jnp.dot(rows, high, preferred_element_type=F32) + jnp.dot(
-            rows, low, preferred_element_type=F32
-        )
-
-    gram = pack_gram(full)
-    keep_ref[512:536, :] = gram
-    send_ref[512:536, :] = gram
-    pair = template_pair(templ_bf)
-    for block in range(4):
-        spectra = spectra_ref[block * 256:(block + 1) * 256, :]
-        cross_block(core_ref[0], block, spectra, pair, keep_ref, send_ref, fitted)
-
-
-def last_template_body(a_ref, b_ref, templ_ref, new_ref):
-    updated = new_templates((a_ref, b_ref), templ_ref)
+    rows = activ_ref[...]
+    fitted = jnp.dot(rows, high, preferred_element_type=F32) + jnp.dot(
+        rows, low, preferred_element_type=F32
+    )
+    cross = cross_of(keep_ref, came_ref, templ_bf[:, 0:LANES], templ_bf[:, LANES:]) - fitted
+    gram = jnp.broadcast_to(pack_gram(full)[None], (32, 24, LANES))
+    out_ref[...] = jnp.concatenate([cross.reshape(32, 16, LANES), gram], axis=1).astype(BF)
+
+
+def last_template_body(a_ref, b_ref, c_ref, d_ref, templ_ref, new_ref):
+    updated = new_templates((a_ref, b_ref, c_ref, d_ref), templ_ref[...])
     new_ref[...] = updated[:, 0:PIX]
 
 
@@ -305,17 +307,11 @@
     return ring_sum(part + shift(part, "c", NC, 1), "x", NX, 1)
 
 
-def first_message_body(quarter_ref, gram_ref, keep_ref, came_ref, out_ref):
+def first_message_body(quarter_ref, gram_ref, own_ref, other_ref, keep_ref, came_ref, out_ref):
     rows = pl.ds(pl.multiple_of(quarter_ref[0] * 8, 8), 8)
-    out_ref[:, 0:16, :] = (keep_ref[...] + came_ref[...]).reshape(32, 16, LANES)
+    cross = cross_of(keep_ref, came_ref, own_ref[...].astype(BF), other_ref[...].astype(BF))
+    out_ref[:, 0:16, :] = cross.reshape(32, 16, LANES)
     out_ref[:, 16:24, :] = jnp.broadcast_to(gram_ref[rows, :][None], (32, 8, LANES))
-
-
-def message_body(keep_ref, came_ref, out_ref):
-    cross = (keep_ref[0:512, :] + came_ref[0:512, :]).reshape(32, 16, LANES)
-    gram = keep_ref[512:536, :] + came_ref[512:536, :]
-    gram = jnp.broadcast_to(gram[None], (32, 24, LANES))
-    out_ref[...] = jnp.concatenate([cross, gram], axis=1).astype(BF)
 
 
 def sds(*shape, dtype=F32):
@@ -328,48 +324,49 @@
     templates = jnp.pad(start_h, ((0, 0), (0, LANES - PIX)))
     got = lax.all_to_all(send, TGT, split_axis=0, concat_axis=0, tiled=True)
     gram = near(call(first_gram_body, sds(32, LANES), (templates,)))
-    got, gram = lax.optimization_barrier((got, gram))
-    spectra, keep, away = call(
-        coadd_body,
-        (sds(1024, 2 * LANES, dtype=BF), sds(512, LANES), sds(512, LANES)),
-        (core, got.reshape(N_TGT * ROWS, 2 * LANES), templates),
-        scratch=[pltpu.VMEM((64, N_TGT * ROWS), BF), pltpu.VMEM((8, N_TGT * ROWS), F32)],
+    other = shift(templates, "c", NC, 1)
+    got, gram, other = lax.optimization_barrier((got, gram, other))
+    rows = got.reshape(N_TGT * ROWS, 2 * LANES)
+    half = sds(512, 2 * LANES, dtype=BF)
+    cost = 2 * 1024 * N_TGT * ROWS * 2 * LANES
+    away, low, high = call(
+        away_body,
+        (half, sds(64, N_TGT * ROWS, dtype=BF), sds(8, N_TGT * ROWS)),
+        (core, rows),
         scalars=1,
-        flops=2 * 2048 * N_TGT * ROWS * 2 * LANES,
+        flops=cost,
+    )
+    came = shift(away, "c", NC, 1)
+    keep = call(keep_body, half, (core, rows, low, high), scalars=1, flops=cost)
+    quarter = lax.axis_index("x").astype(jnp.int32).reshape(1)
+    cross = call(
+        first_message_body,
+        sds(32, 24, LANES),
+        (quarter, gram, templates, other, keep, came),
+        scalars=1,
     )
     state = start_w
     for sweep in range(SWEEPS):
         first = sweep == 0
-        came = shift(away, "c", NC, 1)
-        if first:
-            cross = call(
-                first_message_body,
-                sds(32, 24, LANES),
-                (lax.axis_index("x").astype(jnp.int32).reshape(1), gram, keep, came),
-                scalars=1,
-            )
-        else:
-            cross = call(message_body, sds(32, 40, LANES, dtype=BF), (keep, came))
         cross = lax.all_to_all(cross, ("x", "z"), split_axis=0, concat_axis=0, tiled=True)
         state, message = call(
             lambda *refs, first=first: activation_body(first, *refs),
             (sds(RANK, LANES) if first else sds(32, RANK), sds(32, 16, LANES, dtype=BF)),
             (cross, state),
         )
-        own = lax.all_to_all(message, ("x", "z"), split_axis=0, concat_axis=0, tiled=True)
-        own = own.reshape(512, LANES)
-        other = shift(own, "c", NC, 1)
-        part = call(
-            project_body, sds(88, LANES), (core, own, other, spectra), scalars=1
-        )
-        part = part + lax.ppermute(part, "y", [(0, 1), (1, 0), (2, 3), (3, 2)])
-        parts = (part, lax.ppermute(part, "y", [(0, 3), (3, 0), (1, 2), (2, 1)]))
+        activ = lax.all_to_all(message, ("x", "z"), split_axis=0, concat_axis=0, tiled=True)
+        activ = activ.reshape(512, LANES)
+        size = 152 if first else 88
+        part, away = call(
+            project_body, (sds(size, LANES), sds(size, LANES)), (activ, keep, came)
+        )
+        part = part + shift(away, "c", NC, 1)
+        parts = (part, *(shift(part, "y", NY, by) for by in (1, 2, 3)))
         if first:
-            templates, keep, away = call(
+            templates, cross = call(
                 template_body,
-                (sds(RANK, LANES), sds(536, LANES), sds(536, LANES)),
-                (core, *parts, templates, own, other, spectra),
-                scalars=1,
+                (sds(RANK, LANES), sds(32, 40, LANES, dtype=BF)),
+                (*parts, templates, other, activ, keep, came),
             )
         else:
             templates = call(last_template_body, sds(RANK, PIX), (*parts, templates))

time: 174 us -> 165 us (0.948); the launches traced: 172 us -> 165 us
  waiting for transfers between devices: 57.8 us -> 51.6 us
    ppermute x8 -> x14, starting transfers between devices: 12.8 us -> 21.5 us  [shift(): lax.ppermute(value, axis, [(i, (i + by) % size) for i in range(size)])]
    ppermute x4 -> x0, waiting for transfers between devices: 7.28 us -> none  [the longest x2 4.41 us: shards(): part = part + lax.ppermute(part, 'y', [(0, 1), (1, 0), (2, 3), (3, 2)])]
    ppermute x4 -> x0, starting transfers between devices: 7.11 us -> none  [the longest x2 5.64 us: shards(): parts = (part, lax.ppermute(part, 'y', [(0, 3), (3, 0), (1, 2), (2, 1)]))]
    ppermute x8 -> x14, waiting for transfers between devices: 8.13 us -> 9.23 us  [shift(): lax.ppermute(value, axis, [(i, (i + by) % size) for i in range(size)])]
  transfers between devices with their start and end apart: 13 -> 15, of which waited for: 13 -> 9; matrix products, arithmetic and copies ran while one was open for 0% -> 0% of each run, Pallas kernels for 0% -> 2%
where the time goes in v4:
time: 165 us
  blocking collectives  62.3 us (38%)
  waiting for transfers between devices  51.6 us (31%)
  starting transfers between devices  34.6 us (21%)
  Pallas kernels  15.7 us (10%)
    all_to_all x1, waiting for transfers between devices, shards(): got = lax.all_to_all(send, TGT, split_axis=0, concat_axis=0, tiled=True)  42.4 us
    all_to_all x2, blocking collectives, shards(): lax.all_to_all(message, ('x', 'z'), split_axis=0, concat_axis=0, tiled=True)  32.1 us
    all_to_all x2, blocking collectives, shards(): lax.all_to_all(cross, ('x', 'z'), split_axis=0, concat_axis=0, tiled=True)  30.3 us
    ppermute x14, starting transfers between devices, shift(): lax.ppermute(value, axis, [(i, (i + by) % size) for i in range(size)])  21.5 us
    all_to_all x1, starting transfers between devices, shards(): got = lax.all_to_all(send, TGT, split_axis=0, concat_axis=0, tiled=True)  13.1 us
    pallas_call x10, Pallas kernels, call(): pl.pallas_call(body, out_shape=outs, in_specs=[SMEM] * scalars + [VMEM] *...  12.2 us
    ppermute x14, waiting for transfers between devices, shift(): lax.ppermute(value, axis, [(i, (i + by) % size) for i in range(size)])  9.23 us
    pallas_call x1, Pallas kernels, pack(): pl.pallas_call(pack_body, grid=(ROWS // rows,), out_shape=sds(N_TGT, ROWS...  3.56 us
  transfers between devices with their start and end apart: 15, of which 9 were waited for; matrix products, arithmetic and copies ran while one was open for 0% of the time, Pallas kernels for 2%

profile of v4, /device:TPU:1, one launch (start us, length us, event | category | flops | bytes accessed | tf_op | source)
XLA Modules:
  0.0 165.0 jit_solution(10142464631869124042)
XLA Ops:
  0.6 3.6 %shard_map.68 = bf16[64,64,256]{2,1,0:T(8,128)(2,1)} custom-call(bf16[64,7808]{1,0:T(8,128)(2,1)} %flux_ref.1, bf16[64,7808]{1,0:T(8,128)(2,1)} %ivar_ref.1, s32[1,64]{1,0:T(1,128)} %bitcast.11), custom_call_target="tpu_custom_call" | custom-call | flops 999424 | bytes 3997696 | tf_op jit(solution)/shard_map/pallas_call | solution.py:65
  4.2 13.1 %all-to-all-start = ((bf16[64,64,256]{2,1,0:T(8,128)(2,1)}), bf16[64,64,256]{2,1,0:T(8,128)(2,1)S(1)}, u32[]{:S(2)}, u32[]{:S(2)}) async-start(bf16[64,64,256]{2,1,0:T(8,128)(2,1)} %shard_map.68), calls=%async_computation | async-start | bytes 4194304 | tf_op jit(solution)/shard_map/all_to_all | solution.py:325
  18.8 1.3 collective-permute-start.2
  20.1 1.5 collective-permute-start.3
  21.6 1.6 collective-permute-start.1
  23.2 1.2 collective-permute-start.4
  24.4 1.8 %collective-permute-done.1 = f32[32,128]{1,0:T(8,128)S(1)} collective-permute-done((f32[32,128]{1,0:T(8,128)S(1)}, f32[32,128]{1,0:T(8,128)S(1)}, u32[]{:S(2)}, u32[]{:S(2)}) %collective-permute-start.1) | collective-permute-done | bytes 16416 | tf_op jit(solution)/shard_map/ppermute | solution.py:297
  26.2 42.4 %all-to-all-done = bf16[64,64,256]{2,1,0:T(8,128)(2,1)S(1)} async-done(((bf16[64,64,256]{2,1,0:T(8,128)(2,1)}), bf16[64,64,256]{2,1,0:T(8,128)(2,1)S(1)}, u32[]{:S(2)}, u32[]{:S(2)}) %all-to-all-start) | async-done | bytes 2097184 | tf_op jit(solution)/shard_map/all_to_all | solution.py:325
  68.6 3.2 %shard_map.70 = (bf16[512,256]{1,0:T(8,128)(2,1)S(1)}, bf16[64,4096]{1,0:T(8,128)(2,1)S(1)}, f32[8,4096]{1,0:T(8,128)S(1)}) custom-call(s32[1]{0:T(128)} %bitcast.2.core_ref, bf16[4096,256]{1,0:T(8,128)(2,1)S(1)} %bitcast.6), custom_call_target="tpu_custom_call" | custom-call | flops 2147483648 | tf_op jit(solution)/shard_map/pallas_call | solution.py:28
  72.3 2.5 %shard_map.71.keep_ref = bf16[512,256]{1,0:T(8,128)(2,1)S(1)} custom-call(s32[1]{0:T(128)} %bitcast.2.core_ref, bf16[4096,256]{1,0:T(8,128)(2,1)S(1)} %bitcast.7, bf16[64,4096]{1,0:T(8,128)(2,1)S(1)} %get-tuple-element.21.low_ref, f32[8,4096]{1,0:T(8,128)S(1)} %get-tuple-element.22.high_ref), custom_call_target="tpu_custom_call" | custom-call | flops 2147483648 | tf_op jit(solution)/shard_map/pallas_call | solution.py:28
  75.1 17.0 %all_to_all.25.refs_0_ = f32[32,24,128]{2,1,0:T(8,128)S(1)} all-to-all(f32[32,24,128]{2,1,0:T(8,128)S(1)} %shard_map.72), channel_id=1, replica_groups=mesh['x'=4,'z'=8,'c'=2,'y'=4] {'x','z'}, dimensions={0} | all-to-all | bytes 786432 | tf_op jit(solution)/shard_map/all_to_all | solution.py:351
  93.0 16.2 %all_to_all.26 = bf16[32,16,128]{2,1,0:T(8,128)(2,1)S(1)} all-to-all(bf16[32,16,128]{2,1,0:T(8,128)(2,1)S(1)} %get-tuple-element.24), channel_id=1, replica_groups=mesh['x'=4,'z'=8,'c'=2,'y'=4] {'x','z'}, dimensions={0} | all-to-all | bytes 262144 | tf_op jit(solution)/shard_map/all_to_all | solution.py:357
  109.6 2.2 %collective-permute-start.6 = (f32[152,128]{1,0:T(8,128)S(1)}, f32[152,128]{1,0:T(8,128)S(1)}, u32[]{:S(2)}, u32[]{:S(2)}) collective-permute-start(f32[152,128]{1,0:T(8,128)S(1)} %get-tuple-element.26), channel_id=1, source_target_pairs={{0,4},{4,0},{1,5},{5,1},{2,6},{6,2},{3,7},{7,3},{8,12},{12,8},{9,1... | collective-permute-start | bytes 233480 | tf_op jit(solution)/shard_map/ppermute | solution.py:297
  112.8 1.4 collective-permute-start.7
  114.2 2.6 %collective-permute-start.8 = (f32[152,128]{1,0:T(8,128)S(1)}, f32[152,128]{1,0:T(8,128)S(1)}, u32[]{:S(2)}, u32[]{:S(2)}) collective-permute-start(f32[152,128]{1,0:T(8,128)S(1)} %add.24.a_ref), channel_id=1, source_target_pairs={{0,2},{1,3},{2,0},{3,1},{4,6},{5,7},{6,4},{7,5},{8,10},{9,11},{10,... | collective-permute-start | bytes 233480 | tf_op jit(solution)/shard_map/ppermute | solution.py:297
  117.8 2.7 %collective-permute-done.8.c_ref = f32[152,128]{1,0:T(8,128)S(1)} collective-permute-done((f32[152,128]{1,0:T(8,128)S(1)}, f32[152,128]{1,0:T(8,128)S(1)}, u32[]{:S(2)}, u32[]{:S(2)}) %collective-permute-start.8) | collective-permute-done | bytes 77856 | tf_op jit(solution)/shard_map/ppermute | solution.py:297
  120.6 1.5 shard_map.75
  122.0 13.2 %all_to_all.27.refs_0_ = bf16[32,40,128]{2,1,0:T(8,128)(2,1)S(1)} all-to-all(bf16[32,40,128]{2,1,0:T(8,128)(2,1)S(1)} %get-tuple-element.27), channel_id=1, replica_groups=mesh['x'=4,'z'=8,'c'=2,'y'=4] {'x','z'}, dimensions={0} | all-to-all | bytes 655360 | tf_op jit(solution)/shard_map/all_to_all | solution.py:351
  135.3 1.5 shard_map.76
  136.7 15.8 %all_to_all.28 = bf16[32,16,128]{2,1,0:T(8,128)(2,1)S(1)} all-to-all(bf16[32,16,128]{2,1,0:T(8,128)(2,1)S(1)} %get-tuple-element.30), channel_id=1, replica_groups=mesh['x'=4,'z'=8,'c'=2,'y'=4] {'x','z'}, dimensions={0} | all-to-all | bytes 262144 | tf_op jit(solution)/shard_map/all_to_all | solution.py:357
  153.0 3.7 %collective-permute-start.10 = (f32[88,128]{1,0:T(8,128)S(1)}, f32[88,128]{1,0:T(8,128)S(1)}, u32[]{:S(2)}, u32[]{:S(2)}) collective-permute-start(f32[88,128]{1,0:T(8,128)S(1)} %get-tuple-element.32), channel_id=1, source_target_pairs={{0,4},{4,0},{1,5},{5,1},{2,6},{6,2},{3,7},{7,3},{8,12},{12,8},{9,1... | collective-permute-start | bytes 135176 | tf_op jit(solution)/shard_map/ppermute | solution.py:297
  157.6 2.8 %collective-permute-start.12 = (f32[88,128]{1,0:T(8,128)S(1)}, f32[88,128]{1,0:T(8,128)S(1)}, u32[]{:S(2)}, u32[]{:S(2)}) collective-permute-start(f32[88,128]{1,0:T(8,128)S(1)} %add.25.a_ref), channel_id=1, source_target_pairs={{0,2},{1,3},{2,0},{3,1},{4,6},{5,7},{6,4},{7,5},{8,10},{9,11},{10,... | collective-permute-start | bytes 135176 | tf_op jit(solution)/shard_map/ppermute | solution.py:297
  162.4 1.2 collective-permute-done.13.d_ref
  163.7 1.4 shard_map.78
  (30 shorter events, 8.9 us)
Async XLA Ops:
  4.2 13.1 %copy-start.1 = (f32[64,122]{1,0:T(8,128)S(1)}, f32[64,122]{1,0:T(8,128)}, u32[]{:S(2)}) copy-start(f32[64,122]{1,0:T(8,128)} %param.9) | copy-start | bytes 93700
  4.2 64.4 %all-to-all-start = ((bf16[64,64,256]{2,1,0:T(8,128)(2,1)}), bf16[64,64,256]{2,1,0:T(8,128)(2,1)S(1)}, u32[]{:S(2)}, u32[]{:S(2)}) async-start(bf16[64,64,256]{2,1,0:T(8,128)(2,1)} %shard_map.68), calls=%async_computation | async-start | bytes 4194304 | tf_op jit(solution)/shard_map/all_to_all | solution.py:325
  17.5 1.3 collective-permute-start
  18.8 5.5 %collective-permute-start.2 = (f32[32,128]{1,0:T(8,128)S(1)}, f32[32,128]{1,0:T(8,128)S(1)}, u32[]{:S(2)}, u32[]{:S(2)}) collective-permute-start(f32[32,128]{1,0:T(8,128)S(1)} %add.20), channel_id=1, source_target_pairs={{0,64},{64,128},{128,192},{192,0},{1,65},{65,129},{129,193},{193,1... | collective-permute-start | bytes 49160 | tf_op jit(solution)/shard_map/ppermute | solution.py:297
  20.1 4.3 %collective-permute-start.3 = (f32[32,128]{1,0:T(8,128)S(1)}, f32[32,128]{1,0:T(8,128)S(1)}, u32[]{:S(2)}, u32[]{:S(2)}) collective-permute-start(f32[32,128]{1,0:T(8,128)S(1)} %add.20), channel_id=1, source_target_pairs={{0,192},{64,0},{128,64},{192,128},{1,193},{65,1},{129,65},{193,129... | collective-permute-start | bytes 49160 | tf_op jit(solution)/shard_map/ppermute | solution.py:297
  21.6 4.6 %collective-permute-start.1 = (f32[32,128]{1,0:T(8,128)S(1)}, f32[32,128]{1,0:T(8,128)S(1)}, u32[]{:S(2)}, u32[]{:S(2)}) collective-permute-start(f32[32,128]{1,0:T(8,128)S(1)} %add.20), channel_id=1, source_target_pairs={{0,128},{64,192},{128,0},{192,64},{1,129},{65,193},{129,1},{193,65... | collective-permute-start | bytes 49160 | tf_op jit(solution)/shard_map/ppermute | solution.py:297
  23.2 3.0 %collective-permute-start.4 = (f32[64,128]{1,0:T(8,128)S(1)}, f32[64,128]{1,0:T(8,128)S(1)}, u32[]{:S(2)}, u32[]{:S(2)}) collective-permute-start(f32[64,128]{1,0:T(8,128)S(1)} %pad.4.templ_ref.own_ref), channel_id=1, source_target_pairs={{0,4},{4,0},{1,5},{5,1},{2,6},{6,2},{3,7},{7,3},{8,12},{12,8},{9,1... | collective-permute-start | bytes 98312 | tf_op jit(solution)/shard_map/ppermute | solution.py:297
  71.8 3.0 %collective-permute-start.5 = (bf16[512,256]{1,0:T(8,128)(2,1)S(1)}, bf16[512,256]{1,0:T(8,128)(2,1)S(1)}, u32[]{:S(2)}, u32[]{:S(2)}) collective-permute-start(bf16[512,256]{1,0:T(8,128)(2,1)S(1)} %get-tuple-element.23), channel_id=1, source_target_pairs={{0,4},{4,0},{1,5},{5,1},{2,6},{6,2},{3,7},{7,3},{8,12},{12,8},{9,1... | collective-permute-start | bytes 786440 | tf_op jit(solution)/shard_map/ppermute | solution.py:297
  72.3 19.9 %copy-start = (f32[32,64]{1,0:T(8,128)S(1)}, f32[32,64]{1,0:T(8,128)}, u32[]{:S(2)}) copy-start(f32[32,64]{1,0:T(8,128)} %refs_1_.1) | copy-start | bytes 24580
  109.6 3.1 %collective-permute-start.6 = (f32[152,128]{1,0:T(8,128)S(1)}, f32[152,128]{1,0:T(8,128)S(1)}, u32[]{:S(2)}, u32[]{:S(2)}) collective-permute-start(f32[152,128]{1,0:T(8,128)S(1)} %get-tuple-element.26), channel_id=1, source_target_pairs={{0,4},{4,0},{1,5},{5,1},{2,6},{6,2},{3,7},{7,3},{8,12},{12,8},{9,1... | collective-permute-start | bytes 233480 | tf_op jit(solution)/shard_map/ppermute | solution.py:297
  112.8 5.1 %collective-permute-start.7 = (f32[152,128]{1,0:T(8,128)S(1)}, f32[152,128]{1,0:T(8,128)S(1)}, u32[]{:S(2)}, u32[]{:S(2)}) collective-permute-start(f32[152,128]{1,0:T(8,128)S(1)} %add.24.a_ref), channel_id=1, source_target_pairs={{0,1},{1,2},{2,3},{3,0},{4,5},{5,6},{6,7},{7,4},{8,9},{9,10},{10,1... | collective-permute-start | bytes 233480 | tf_op jit(solution)/shard_map/ppermute | solution.py:297
  114.2 6.4 %collective-permute-start.8 = (f32[152,128]{1,0:T(8,128)S(1)}, f32[152,128]{1,0:T(8,128)S(1)}, u32[]{:S(2)}, u32[]{:S(2)}) collective-permute-start(f32[152,128]{1,0:T(8,128)S(1)} %add.24.a_ref), channel_id=1, source_target_pairs={{0,2},{1,3},{2,0},{3,1},{4,6},{5,7},{6,4},{7,5},{8,10},{9,11},{10,... | collective-permute-start | bytes 233480 | tf_op jit(solution)/shard_map/ppermute | solution.py:297
  116.8 3.8 %collective-permute-start.9 = (f32[152,128]{1,0:T(8,128)S(1)}, f32[152,128]{1,0:T(8,128)S(1)}, u32[]{:S(2)}, u32[]{:S(2)}) collective-permute-start(f32[152,128]{1,0:T(8,128)S(1)} %add.24.a_ref), channel_id=1, source_target_pairs={{0,3},{1,0},{2,1},{3,2},{4,7},{5,4},{6,5},{7,6},{8,11},{9,8},{10,9... | collective-permute-start | bytes 233480 | tf_op jit(solution)/shard_map/ppermute | solution.py:297
  153.0 4.6 %collective-permute-start.10 = (f32[88,128]{1,0:T(8,128)S(1)}, f32[88,128]{1,0:T(8,128)S(1)}, u32[]{:S(2)}, u32[]{:S(2)}) collective-permute-start(f32[88,128]{1,0:T(8,128)S(1)} %get-tuple-element.32), channel_id=1, source_target_pairs={{0,4},{4,0},{1,5},{5,1},{2,6},{6,2},{3,7},{7,3},{8,12},{12,8},{9,1... | collective-permute-start | bytes 135176 | tf_op jit(solution)/shard_map/ppermute | solution.py:297
  157.6 4.1 %collective-permute-start.11 = (f32[88,128]{1,0:T(8,128)S(1)}, f32[88,128]{1,0:T(8,128)S(1)}, u32[]{:S(2)}, u32[]{:S(2)}) collective-permute-start(f32[88,128]{1,0:T(8,128)S(1)} %add.25.a_ref), channel_id=1, source_target_pairs={{0,1},{1,2},{2,3},{3,0},{4,5},{5,6},{6,7},{7,4},{8,9},{9,10},{10,1... | collective-permute-start | bytes 135176 | tf_op jit(solution)/shard_map/ppermute | solution.py:297
  157.6 4.8 %collective-permute-start.12 = (f32[88,128]{1,0:T(8,128)S(1)}, f32[88,128]{1,0:T(8,128)S(1)}, u32[]{:S(2)}, u32[]{:S(2)}) collective-permute-start(f32[88,128]{1,0:T(8,128)S(1)} %add.25.a_ref), channel_id=1, source_target_pairs={{0,2},{1,3},{2,0},{3,1},{4,6},{5,7},{6,4},{7,5},{8,10},{9,11},{10,... | collective-permute-start | bytes 135176 | tf_op jit(solution)/shard_map/ppermute | solution.py:297
  160.4 3.3 %collective-permute-start.13 = (f32[88,128]{1,0:T(8,128)S(1)}, f32[88,128]{1,0:T(8,128)S(1)}, u32[]{:S(2)}, u32[]{:S(2)}) collective-permute-start(f32[88,128]{1,0:T(8,128)S(1)} %add.25.a_ref), channel_id=1, source_target_pairs={{0,3},{1,0},{2,1},{3,2},{4,7},{5,4},{6,5},{7,6},{8,11},{9,8},{10,9... | collective-permute-start | bytes 135176 | tf_op jit(solution)/shard_map/ppermute | solution.py:297

commit v5 on v4

--- a/solution.py
+++ b/solution.py
@@ -92,37 +92,31 @@
 
 
 def coadd_rows(core, got_ref, low_ref, high_ref, spectra_ref):
-    inside = lax.broadcasted_iota(jnp.int32, (256, LANES), 1) < PIX
-
-    def block_step(block, carry):
-        first = (core * 8 + block * 4).astype(F32)
-        selector = jnp.concatenate(
-            [
-                low_ref[...]
-                * jnp.where(high_ref[0:1, :] == first + float(half * 16 + i), 1.0, 0.0).astype(BF)
-                for half in range(2)
-                for i in range(4)
-            ],
-            axis=0,
-        )
-        sums = jnp.dot(selector, got_ref[...], preferred_element_type=F32)
-        coadd = sums[:, 0:LANES] / (sums[:, LANES:] + PRIOR_IVAR)
-        for half in range(2):
-            spectra_ref[
-                pl.ds(pl.multiple_of(block * 256, 256), 256),
-                half * LANES:(half + 1) * LANES,
-            ] = jnp.where(inside, coadd[half * 256:(half + 1) * 256, :], 0.0).astype(BF)
-        return carry
-
-    lax.fori_loop(0, 2, block_step, 0)
+    inside = lax.broadcasted_iota(jnp.int32, (512, LANES), 1) < PIX
+    first = (core * 8).astype(F32)
+    selector = jnp.concatenate(
+        [
+            low_ref[...]
+            * jnp.where(high_ref[0:1, :] == first + float(half * 16 + i), 1.0, 0.0).astype(BF)
+            for half in range(2)
+            for i in range(8)
+        ],
+        axis=0,
+    )
+    sums = jnp.dot(selector, got_ref[...], preferred_element_type=F32)
+    coadd = sums[:, 0:LANES] / (sums[:, LANES:] + PRIOR_IVAR)
+    for half in range(2):
+        spectra_ref[:, half * LANES:(half + 1) * LANES] = jnp.where(
+            inside, coadd[half * 512:(half + 1) * 512, :], 0.0
+        ).astype(BF)
 
 
 def away_body(core_ref, got_ref, away_ref, low_ref, high_ref):
-    lane = lax.broadcasted_iota(jnp.int32, (16, 2 * LANES), 1)
-    row = lax.broadcasted_iota(jnp.int32, (16, 2 * LANES), 0)
+    lane = lax.broadcasted_iota(jnp.int32, (16, LANES), 1)
+    row = lax.broadcasted_iota(jnp.int32, (16, LANES), 0)
     pick = jnp.where(lane == PIX + row, 1.0, 0.0)
     pick = jnp.where(row < 2, pick, 0.0).astype(BF)
-    ids = lax.dot_general(pick, got_ref[...], NT, preferred_element_type=F32)
+    ids = lax.dot_general(pick, got_ref[:, 0:LANES], NT, preferred_element_type=F32)
     high_ref[...] = jnp.broadcast_to(ids[0:1, :], high_ref.shape)
     low = ids[1:2, :].astype(jnp.int32)
     low_ref[...] = jnp.where(
@@ -209,30 +203,21 @@
 
 
 def activation_body(first, *refs):
-    cross_ref, state_ref, new_ref, out_ref = refs
+    if first:
+        cross_ref, gram_ref, state_ref, new_ref, out_ref = refs
+    else:
+        cross_ref, state_ref, new_ref, out_ref = refs
     total = jnp.sum(cross_ref[...].astype(F32), axis=0)
     cross = pad_to(total[0:16, :], LANES, LANES).T
     wanted = cross[0:64, :] + pltpu.roll(cross[64:128, :], 16, 1)
-    if first:
-        packed = jnp.concatenate(
-            [jnp.sum(cross_ref[NZ * i:NZ * i + NZ, 16:24, :], axis=0) for i in range(NX)],
-            axis=0,
-        )
-        gram = jnp.concatenate(
-            [packed[:, 0:RANK], pltpu.roll(packed, RANK, 1)[:, 0:RANK]], axis=0
-        )
-    else:
-        gram = unpack_gram(total[16:40, :])
+    gram = unpack_gram(gram_ref[...] if first else total[16:40, :])
     if first:
         state = pad_to(state_ref[...], LANES, LANES).T[0:RANK, :]
     else:
         state = state_ref[...]
     rest = state if first else state - state.astype(BF).astype(F32)
     updated = descend(state, wanted - exact(gram, rest), gram)
-    if first:
-        new_ref[...] = updated
-    else:
-        new_ref[...] = pad_to(updated, LANES, LANES).T[0:32, 0:RANK]
+    new_ref[...] = updated
     both = jnp.concatenate([updated, pltpu.roll(updated, LANES - 16, 1)], axis=0).T
     out_ref[...] = jnp.broadcast_to(both[0:16, :].astype(BF)[None], out_ref.shape)
 
@@ -282,15 +267,17 @@
     out_ref[...] = jnp.concatenate([cross.reshape(32, 16, LANES), gram], axis=1).astype(BF)
 
 
-def last_template_body(a_ref, b_ref, c_ref, d_ref, templ_ref, new_ref):
+def last_template_body(a_ref, b_ref, c_ref, d_ref, templ_ref, state_ref, new_ref, activ_ref):
+    activ_ref[...] = pad_to(state_ref[...], LANES, LANES).T[0:32, 0:RANK]
     updated = new_templates((a_ref, b_ref, c_ref, d_ref), templ_ref[...])
     new_ref[...] = updated[:, 0:PIX]
 
 
 def first_gram_body(templ_ref, gram_ref):
     templ_bf = templ_ref[...].astype(BF)
-    gram = lax.dot_general(templ_bf, templ_bf, NT, preferred_element_type=F32)
-    gram_ref[...] = spread(gram[0:32, :], 0) + spread(gram[32:64, :], 64)
+    gram_ref[...] = pack_gram(
+        lax.dot_general(templ_bf, templ_bf, NT, preferred_element_type=F32)
+    )
 
 
 def shift(value, axis, size, by):
@@ -303,15 +290,21 @@
     )
 
 
+def from_ahead(value, by):
+    pairs = [
+        ((z + 2 * y + by) % NZ * NY + y, z * NY + y) for z in range(NZ) for y in range(NY)
+    ]
+    return lax.ppermute(value, ("z", "y"), pairs)
+
+
 def near(part):
-    return ring_sum(part + shift(part, "c", NC, 1), "x", NX, 1)
-
-
-def first_message_body(quarter_ref, gram_ref, own_ref, other_ref, keep_ref, came_ref, out_ref):
-    rows = pl.ds(pl.multiple_of(quarter_ref[0] * 8, 8), 8)
+    part = ring_sum(part + shift(part, "c", NC, 1), "x", NX, 1)
+    return from_ahead(part, 0) + from_ahead(part, 1)
+
+
+def first_message_body(own_ref, other_ref, keep_ref, came_ref, out_ref):
     cross = cross_of(keep_ref, came_ref, own_ref[...].astype(BF), other_ref[...].astype(BF))
-    out_ref[:, 0:16, :] = cross.reshape(32, 16, LANES)
-    out_ref[:, 16:24, :] = jnp.broadcast_to(gram_ref[rows, :][None], (32, 8, LANES))
+    out_ref[...] = cross.reshape(32, 16, LANES)
 
 
 def sds(*shape, dtype=F32):
@@ -323,7 +316,7 @@
     send = pack(flux, ivar, row_target.reshape(1, ROWS))
     templates = jnp.pad(start_h, ((0, 0), (0, LANES - PIX)))
     got = lax.all_to_all(send, TGT, split_axis=0, concat_axis=0, tiled=True)
-    gram = near(call(first_gram_body, sds(32, LANES), (templates,)))
+    gram = near(call(first_gram_body, sds(24, LANES), (templates,)))
     other = shift(templates, "c", NC, 1)
     got, gram, other = lax.optimization_barrier((got, gram, other))
     rows = got.reshape(N_TGT * ROWS, 2 * LANES)
@@ -338,21 +331,19 @@
     )
     came = shift(away, "c", NC, 1)
     keep = call(keep_body, half, (core, rows, low, high), scalars=1, flops=cost)
-    quarter = lax.axis_index("x").astype(jnp.int32).reshape(1)
     cross = call(
-        first_message_body,
-        sds(32, 24, LANES),
-        (quarter, gram, templates, other, keep, came),
-        scalars=1,
-    )
+        first_message_body, sds(32, 16, LANES), (templates, other, keep, came)
+    )
+    cross, gram = lax.optimization_barrier((cross, gram))
+    gram = ring_sum(gram, "y", NY, 1)
     state = start_w
     for sweep in range(SWEEPS):
         first = sweep == 0
         cross = lax.all_to_all(cross, ("x", "z"), split_axis=0, concat_axis=0, tiled=True)
         state, message = call(
             lambda *refs, first=first: activation_body(first, *refs),
-            (sds(RANK, LANES) if first else sds(32, RANK), sds(32, 16, LANES, dtype=BF)),
-            (cross, state),
+            (sds(RANK, LANES), sds(32, 16, LANES, dtype=BF)),
+            (cross, gram, state) if first else (cross, state),
         )
         activ = lax.all_to_all(message, ("x", "z"), split_axis=0, concat_axis=0, tiled=True)
         activ = activ.reshape(512, LANES)
@@ -369,7 +360,11 @@
                 (*parts, templates, other, activ, keep, came),
             )
         else:
-            templates = call(last_template_body, sds(RANK, PIX), (*parts, templates))
+            templates, state = call(
+                last_template_body,
+                (sds(RANK, PIX), sds(32, RANK)),
+                (*parts, templates, state),
+            )
     return state, templates
 
 

time: 165 us -> 164 us (level)
  blocking collectives: 62.3 us -> 44.5 us
  starting transfers between devices: 34.6 us -> 49 us
  waiting for transfers between devices: 51.6 us -> 54.1 us
    all_to_all x1, waiting for transfers between devices: 42.4 us -> 4.53 us  [shards(): got = lax.all_to_all(send, TGT, split_axis=0, concat_axis=0, tiled=True)]
    ppermute x0 -> x2, waiting for transfers between devices: none -> 34.3 us  [from_ahead(): return lax.ppermute(value, ('z', 'y'), pairs)]
    all_to_all x2 -> x1, blocking collectives: 30.3 us -> 13.3 us  [shards(): lax.all_to_all(cross, ('x', 'z'), split_axis=0, concat_axis=0, tiled=True)]
    ppermute x14 -> x17, starting transfers between devices: 21.5 us -> 27 us  [shift(): lax.ppermute(value, axis, [(i, (i + by) % size) for i in range(size)])]
    all_to_all x0 -> x1, starting transfers between devices: none -> 5.31 us  [shards(): lax.all_to_all(cross, ('x', 'z'), split_axis=0, concat_axis=0, tiled=True)]
    ppermute x0 -> x2, starting transfers between devices: none -> 3.58 us  [from_ahead(): return lax.ppermute(value, ('z', 'y'), pairs)]
    ppermute x14 -> x17, waiting for transfers between devices: 9.23 us -> 12.5 us  [shift(): lax.ppermute(value, axis, [(i, (i + by) % size) for i in range(size)])]
    all_to_all x0 -> x1, waiting for transfers between devices: none -> 2.79 us  [shards(): lax.all_to_all(cross, ('x', 'z'), split_axis=0, concat_axis=0, tiled=True)]
  transfers between devices with their start and end apart: 15 -> 21, of which waited for: 9 -> 14; matrix products, arithmetic and copies ran while one was open for 0% -> 0% of each run, Pallas kernels for 2% -> 2%
where the time goes in v5:
time: 164 us
  waiting for transfers between devices  54.1 us (33%)
  starting transfers between devices  49 us (30%)
  blocking collectives  44.5 us (27%)
  Pallas kernels  15.4 us (9%)
    ppermute x2, waiting for transfers between devices, from_ahead(): return lax.ppermute(value, ('z', 'y'), pairs)  34.3 us
    all_to_all x2, blocking collectives, shards(): lax.all_to_all(message, ('x', 'z'), split_axis=0, concat_axis=0, tiled=True)  31.2 us
    ppermute x17, starting transfers between devices, shift(): lax.ppermute(value, axis, [(i, (i + by) % size) for i in range(size)])  27 us
    all_to_all x1, blocking collectives, shards(): lax.all_to_all(cross, ('x', 'z'), split_axis=0, concat_axis=0, tiled=True)  13.3 us
    all_to_all x1, starting transfers between devices, shards(): got = lax.all_to_all(send, TGT, split_axis=0, concat_axis=0, tiled=True)  13.1 us
    ppermute x17, waiting for transfers between devices, shift(): lax.ppermute(value, axis, [(i, (i + by) % size) for i in range(size)])  12.5 us
    pallas_call x10, Pallas kernels, call(): pl.pallas_call(body, out_shape=outs, in_specs=[SMEM] * scalars + [VMEM] *...  11.9 us
    all_to_all x1, starting transfers between devices, shards(): lax.all_to_all(cross, ('x', 'z'), split_axis=0, concat_axis=0, tiled=True)  5.31 us
  transfers between devices with their start and end apart: 21, of which 14 were waited for; matrix products, arithmetic and copies ran while one was open for 0% of the time, Pallas kernels for 2%

profile of v5, /device:TPU:1, one launch (start us, length us, event | category | flops | bytes accessed | tf_op | source)
XLA Modules:
  0.0 163.8 jit_solution(2923476063439798656)
XLA Ops:
  0.6 3.6 %shard_map.68 = bf16[64,64,256]{2,1,0:T(8,128)(2,1)} custom-call(bf16[64,7808]{1,0:T(8,128)(2,1)} %flux_ref.1, bf16[64,7808]{1,0:T(8,128)(2,1)} %ivar_ref.1, s32[1,64]{1,0:T(1,128)} %bitcast.10), custom_call_target="tpu_custom_call" | custom-call | flops 999424 | bytes 3997696 | tf_op jit(solution)/shard_map/pallas_call | solution.py:65
  4.2 13.1 %all-to-all-start = ((bf16[64,64,256]{2,1,0:T(8,128)(2,1)}), bf16[64,64,256]{2,1,0:T(8,128)(2,1)S(1)}, u32[]{:S(2)}, u32[]{:S(2)}) async-start(bf16[64,64,256]{2,1,0:T(8,128)(2,1)} %shard_map.68), calls=%async_computation | async-start | bytes 4194304 | tf_op jit(solution)/shard_map/all_to_all | solution.py:318
  21.7 1.6 %collective-permute-start.1 = (f32[24,128]{1,0:T(8,128)S(1)}, f32[24,128]{1,0:T(8,128)S(1)}, u32[]{:S(2)}, u32[]{:S(2)}) collective-permute-start(f32[24,128]{1,0:T(8,128)S(1)} %add.32), channel_id=1, source_target_pairs={{0,128},{64,192},{128,0},{192,64},{1,129},{65,193},{129,1},{193,65... | collective-permute-start | bytes 36872 | tf_op jit(solution)/shard_map/ppermute | solution.py:284
  24.5 1.6 %collective-permute-done.1 = f32[24,128]{1,0:T(8,128)S(1)} collective-permute-done((f32[24,128]{1,0:T(8,128)S(1)}, f32[24,128]{1,0:T(8,128)S(1)}, u32[]{:S(2)}, u32[]{:S(2)}) %collective-permute-start.1) | collective-permute-done | bytes 12320 | tf_op jit(solution)/shard_map/ppermute | solution.py:284
  26.8 2.9 %collective-permute-start.5 = (f32[24,128]{1,0:T(8,128)S(1)}, f32[24,128]{1,0:T(8,128)S(1)}, u32[]{:S(2)}, u32[]{:S(2)}) collective-permute-start(f32[24,128]{1,0:T(8,128)S(1)} %add_add_fusion.1), channel_id=1, source_target_pairs={{8,0},{25,1},{42,2},{59,3},{16,8},{33,9},{50,10},{3,11},{24,16},{4... | collective-permute-start | bytes 36872 | tf_op jit(solution)/shard_map/ppermute | solution.py:297
  29.7 34.3 %collective-permute-done.5 = f32[24,128]{1,0:T(8,128)S(1)} collective-permute-done((f32[24,128]{1,0:T(8,128)S(1)}, f32[24,128]{1,0:T(8,128)S(1)}, u32[]{:S(2)}, u32[]{:S(2)}) %collective-permute-start.5) | collective-permute-done | bytes 12320 | tf_op jit(solution)/shard_map/ppermute | solution.py:297
  64.0 4.5 %all-to-all-done = bf16[64,64,256]{2,1,0:T(8,128)(2,1)S(1)} async-done(((bf16[64,64,256]{2,1,0:T(8,128)(2,1)}), bf16[64,64,256]{2,1,0:T(8,128)(2,1)S(1)}, u32[]{:S(2)}, u32[]{:S(2)}) %all-to-all-start) | async-done | bytes 2097184 | tf_op jit(solution)/shard_map/all_to_all | solution.py:318
  68.6 2.7 %shard_map.70 = (bf16[512,256]{1,0:T(8,128)(2,1)S(1)}, bf16[64,4096]{1,0:T(8,128)(2,1)S(1)}, f32[8,4096]{1,0:T(8,128)S(1)}) custom-call(s32[1]{0:T(128)} %bitcast.1.core_ref, bf16[4096,256]{1,0:T(8,128)(2,1)S(1)} %bitcast.5), custom_call_target="tpu_custom_call" | custom-call | flops 2147483648 | tf_op jit(solution)/shard_map/pallas_call | solution.py:28
  71.7 2.3 %shard_map.71.keep_ref = bf16[512,256]{1,0:T(8,128)(2,1)S(1)} custom-call(s32[1]{0:T(128)} %bitcast.1.core_ref, bf16[4096,256]{1,0:T(8,128)(2,1)S(1)} %bitcast.6, bf16[64,4096]{1,0:T(8,128)(2,1)S(1)} %get-tuple-element.24.low_ref, f32[8,4096]{1,0:T(8,128)S(1)} %get-tuple-element.25.high_ref), custom_call_target="tpu_custom_call" | custom-call | flops 2147483648 | tf_op jit(solution)/shard_map/pallas_call | solution.py:28
  75.1 5.3 %all-to-all-start.1 = ((f32[32,16,128]{2,1,0:T(8,128)}), f32[32,16,128]{2,1,0:T(8,128)S(1)}, u32[]{:S(2)}, u32[]{:S(2)}) async-start(f32[32,16,128]{2,1,0:T(8,128)} %shard_map.72), calls=%async_computation.1 | async-start | bytes 524288 | tf_op jit(solution)/shard_map/all_to_all | solution.py:342
  80.4 2.0 %collective-permute-start.9 = (f32[24,128]{1,0:T(8,128)S(1)}, f32[24,128]{1,0:T(8,128)S(1)}, u32[]{:S(2)}, u32[]{:S(2)}) collective-permute-start(f32[24,128]{1,0:T(8,128)S(1)} %add.36), channel_id=1, source_target_pairs={{0,1},{1,2},{2,3},{3,0},{4,5},{5,6},{6,7},{7,4},{8,9},{9,10},{10,1... | collective-permute-start | bytes 36872 | tf_op jit(solution)/shard_map/ppermute | solution.py:284
  83.5 1.9 %collective-permute-start.8 = (f32[24,128]{1,0:T(8,128)S(1)}, f32[24,128]{1,0:T(8,128)S(1)}, u32[]{:S(2)}, u32[]{:S(2)}) collective-permute-start(f32[24,128]{1,0:T(8,128)S(1)} %add.36), channel_id=1, source_target_pairs={{0,2},{1,3},{2,0},{3,1},{4,6},{5,7},{6,4},{7,5},{8,10},{9,11},{10,... | collective-permute-start | bytes 36872 | tf_op jit(solution)/shard_map/ppermute | solution.py:284
  85.5 2.4 %collective-permute-done.8 = f32[24,128]{1,0:T(8,128)S(1)} collective-permute-done((f32[24,128]{1,0:T(8,128)S(1)}, f32[24,128]{1,0:T(8,128)S(1)}, u32[]{:S(2)}, u32[]{:S(2)}) %collective-permute-start.8) | collective-permute-done | bytes 12320 | tf_op jit(solution)/shard_map/ppermute | solution.py:284
  87.9 2.8 %all-to-all-done.1.refs_0_ = f32[32,16,128]{2,1,0:T(8,128)S(1)} async-done(((f32[32,16,128]{2,1,0:T(8,128)}), f32[32,16,128]{2,1,0:T(8,128)S(1)}, u32[]{:S(2)}, u32[]{:S(2)}) %all-to-all-start.1) | async-done | bytes 262176 | tf_op jit(solution)/shard_map/all_to_all | solution.py:342
  91.7 15.4 %all_to_all.25 = bf16[32,16,128]{2,1,0:T(8,128)(2,1)S(1)} all-to-all(bf16[32,16,128]{2,1,0:T(8,128)(2,1)S(1)} %get-tuple-element.30), channel_id=1, replica_groups=mesh['x'=4,'z'=8,'c'=2,'y'=4] {'x','z'}, dimensions={0} | all-to-all | bytes 262144 | tf_op jit(solution)/shard_map/all_to_all | solution.py:348
  107.5 3.3 %collective-permute-start.11 = (f32[152,128]{1,0:T(8,128)S(1)}, f32[152,128]{1,0:T(8,128)S(1)}, u32[]{:S(2)}, u32[]{:S(2)}) collective-permute-start(f32[152,128]{1,0:T(8,128)S(1)} %get-tuple-element.32), channel_id=1, source_target_pairs={{0,4},{4,0},{1,5},{5,1},{2,6},{6,2},{3,7},{7,3},{8,12},{12,8},{9,1... | collective-permute-start | bytes 233480 | tf_op jit(solution)/shard_map/ppermute | solution.py:284
  112.7 2.1 %collective-permute-start.13 = (f32[152,128]{1,0:T(8,128)S(1)}, f32[152,128]{1,0:T(8,128)S(1)}, u32[]{:S(2)}, u32[]{:S(2)}) collective-permute-start(f32[152,128]{1,0:T(8,128)S(1)} %add.40.a_ref), channel_id=1, source_target_pairs={{0,2},{1,3},{2,0},{3,1},{4,6},{5,7},{6,4},{7,5},{8,10},{9,11},{10,... | collective-permute-start | bytes 233480 | tf_op jit(solution)/shard_map/ppermute | solution.py:284
  114.7 1.6 collective-permute-start.14
  116.6 1.9 %collective-permute-done.13.c_ref = f32[152,128]{1,0:T(8,128)S(1)} collective-permute-done((f32[152,128]{1,0:T(8,128)S(1)}, f32[152,128]{1,0:T(8,128)S(1)}, u32[]{:S(2)}, u32[]{:S(2)}) %collective-permute-start.13) | collective-permute-done | bytes 77856 | tf_op jit(solution)/shard_map/ppermute | solution.py:284
  120.6 13.3 %all_to_all.26.refs_0_ = bf16[32,40,128]{2,1,0:T(8,128)(2,1)S(1)} all-to-all(bf16[32,40,128]{2,1,0:T(8,128)(2,1)S(1)} %get-tuple-element.33), channel_id=1, replica_groups=mesh['x'=4,'z'=8,'c'=2,'y'=4] {'x','z'}, dimensions={0} | all-to-all | bytes 655360 | tf_op jit(solution)/shard_map/all_to_all | solution.py:342
  134.8 15.8 %all_to_all.27 = bf16[32,16,128]{2,1,0:T(8,128)(2,1)S(1)} all-to-all(bf16[32,16,128]{2,1,0:T(8,128)(2,1)S(1)} %get-tuple-element.35), channel_id=1, replica_groups=mesh['x'=4,'z'=8,'c'=2,'y'=4] {'x','z'}, dimensions={0} | all-to-all | bytes 262144 | tf_op jit(solution)/shard_map/all_to_all | solution.py:348
  151.0 3.7 %collective-permute-start.15 = (f32[88,128]{1,0:T(8,128)S(1)}, f32[88,128]{1,0:T(8,128)S(1)}, u32[]{:S(2)}, u32[]{:S(2)}) collective-permute-start(f32[88,128]{1,0:T(8,128)S(1)} %get-tuple-element.37), channel_id=1, source_target_pairs={{0,4},{4,0},{1,5},{5,1},{2,6},{6,2},{3,7},{7,3},{8,12},{12,8},{9,1... | collective-permute-start | bytes 135176 | tf_op jit(solution)/shard_map/ppermute | solution.py:284
  156.5 2.7 %collective-permute-start.17 = (f32[88,128]{1,0:T(8,128)S(1)}, f32[88,128]{1,0:T(8,128)S(1)}, u32[]{:S(2)}, u32[]{:S(2)}) collective-permute-start(f32[88,128]{1,0:T(8,128)S(1)} %add.41.a_ref), channel_id=1, source_target_pairs={{0,2},{1,3},{2,0},{3,1},{4,6},{5,7},{6,4},{7,5},{8,10},{9,11},{10,... | collective-permute-start | bytes 135176 | tf_op jit(solution)/shard_map/ppermute | solution.py:284
  159.7 1.6 collective-permute-done.17.c_ref
  (43 shorter events, 20.5 us)
Async XLA Ops:
  4.2 13.1 %copy-start.1 = (f32[64,122]{1,0:T(8,128)S(1)}, f32[64,122]{1,0:T(8,128)}, u32[]{:S(2)}) copy-start(f32[64,122]{1,0:T(8,128)} %param.9) | copy-start | bytes 93700
  4.2 64.4 %all-to-all-start = ((bf16[64,64,256]{2,1,0:T(8,128)(2,1)}), bf16[64,64,256]{2,1,0:T(8,128)(2,1)S(1)}, u32[]{:S(2)}, u32[]{:S(2)}) async-start(bf16[64,64,256]{2,1,0:T(8,128)(2,1)} %shard_map.68), calls=%async_computation | async-start | bytes 4194304 | tf_op jit(solution)/shard_map/all_to_all | solution.py:318
  17.6 1.3 collective-permute-start
  18.9 5.5 %collective-permute-start.2 = (f32[24,128]{1,0:T(8,128)S(1)}, f32[24,128]{1,0:T(8,128)S(1)}, u32[]{:S(2)}, u32[]{:S(2)}) collective-permute-start(f32[24,128]{1,0:T(8,128)S(1)} %add.32), channel_id=1, source_target_pairs={{0,64},{64,128},{128,192},{192,0},{1,65},{65,129},{129,193},{193,1... | collective-permute-start | bytes 36872 | tf_op jit(solution)/shard_map/ppermute | solution.py:284
  20.2 4.3 %collective-permute-start.3 = (f32[24,128]{1,0:T(8,128)S(1)}, f32[24,128]{1,0:T(8,128)S(1)}, u32[]{:S(2)}, u32[]{:S(2)}) collective-permute-start(f32[24,128]{1,0:T(8,128)S(1)} %add.32), channel_id=1, source_target_pairs={{0,192},{64,0},{128,64},{192,128},{1,193},{65,1},{129,65},{193,129... | collective-permute-start | bytes 36872 | tf_op jit(solution)/shard_map/ppermute | solution.py:284
  21.7 4.5 %collective-permute-start.1 = (f32[24,128]{1,0:T(8,128)S(1)}, f32[24,128]{1,0:T(8,128)S(1)}, u32[]{:S(2)}, u32[]{:S(2)}) collective-permute-start(f32[24,128]{1,0:T(8,128)S(1)} %add.32), channel_id=1, source_target_pairs={{0,128},{64,192},{128,0},{192,64},{1,129},{65,193},{129,1},{193,65... | collective-permute-start | bytes 36872 | tf_op jit(solution)/shard_map/ppermute | solution.py:284
  23.3 40.7 %collective-permute-start.6 = (f32[64,128]{1,0:T(8,128)S(1)}, f32[64,128]{1,0:T(8,128)S(1)}, u32[]{:S(2)}, u32[]{:S(2)}) collective-permute-start(f32[64,128]{1,0:T(8,128)S(1)} %pad.4.templ_ref.own_ref), channel_id=1, source_target_pairs={{0,4},{4,0},{1,5},{5,1},{2,6},{6,2},{3,7},{7,3},{8,12},{12,8},{9,1... | collective-permute-start | bytes 98312 | tf_op jit(solution)/shard_map/ppermute | solution.py:284
  26.2 3.6 %collective-permute-start.4 = (f32[24,128]{1,0:T(8,128)S(1)}, f32[24,128]{1,0:T(8,128)S(1)}, u32[]{:S(2)}, u32[]{:S(2)}) collective-permute-start(f32[24,128]{1,0:T(8,128)S(1)} %add_add_fusion.1), channel_id=1, source_target_pairs={{0,0},{17,1},{34,2},{51,3},{8,8},{25,9},{42,10},{59,11},{16,16},{3... | collective-permute-start | bytes 36872 | tf_op jit(solution)/shard_map/ppermute | solution.py:297
  26.8 37.2 %collective-permute-start.5 = (f32[24,128]{1,0:T(8,128)S(1)}, f32[24,128]{1,0:T(8,128)S(1)}, u32[]{:S(2)}, u32[]{:S(2)}) collective-permute-start(f32[24,128]{1,0:T(8,128)S(1)} %add_add_fusion.1), channel_id=1, source_target_pairs={{8,0},{25,1},{42,2},{59,3},{16,8},{33,9},{50,10},{3,11},{24,16},{4... | collective-permute-start | bytes 36872 | tf_op jit(solution)/shard_map/ppermute | solution.py:297
  71.2 2.8 %collective-permute-start.7 = (bf16[512,256]{1,0:T(8,128)(2,1)S(1)}, bf16[512,256]{1,0:T(8,128)(2,1)S(1)}, u32[]{:S(2)}, u32[]{:S(2)}) collective-permute-start(bf16[512,256]{1,0:T(8,128)(2,1)S(1)} %get-tuple-element.26), channel_id=1, source_target_pairs={{0,4},{4,0},{1,5},{5,1},{2,6},{6,2},{3,7},{7,3},{8,12},{12,8},{9,1... | collective-permute-start | bytes 786440 | tf_op jit(solution)/shard_map/ppermute | solution.py:284
  71.7 19.0 %copy-start = (f32[32,64]{1,0:T(8,128)S(1)}, f32[32,64]{1,0:T(8,128)}, u32[]{:S(2)}) copy-start(f32[32,64]{1,0:T(8,128)} %refs_2_.1) | copy-start | bytes 24580
  75.1 15.6 %all-to-all-start.1 = ((f32[32,16,128]{2,1,0:T(8,128)}), f32[32,16,128]{2,1,0:T(8,128)S(1)}, u32[]{:S(2)}, u32[]{:S(2)}) async-start(f32[32,16,128]{2,1,0:T(8,128)} %shard_map.72), calls=%async_computation.1 | async-start | bytes 524288 | tf_op jit(solution)/shard_map/all_to_all | solution.py:342
  80.4 5.1 %collective-permute-start.9 = (f32[24,128]{1,0:T(8,128)S(1)}, f32[24,128]{1,0:T(8,128)S(1)}, u32[]{:S(2)}, u32[]{:S(2)}) collective-permute-start(f32[24,128]{1,0:T(8,128)S(1)} %add.36), channel_id=1, source_target_pairs={{0,1},{1,2},{2,3},{3,0},{4,5},{5,6},{6,7},{7,4},{8,9},{9,10},{10,1... | collective-permute-start | bytes 36872 | tf_op jit(solution)/shard_map/ppermute | solution.py:284
  82.4 3.1 %collective-permute-start.10 = (f32[24,128]{1,0:T(8,128)S(1)}, f32[24,128]{1,0:T(8,128)S(1)}, u32[]{:S(2)}, u32[]{:S(2)}) collective-permute-start(f32[24,128]{1,0:T(8,128)S(1)} %add.36), channel_id=1, source_target_pairs={{0,3},{1,0},{2,1},{3,2},{4,7},{5,4},{6,5},{7,6},{8,11},{9,8},{10,9... | collective-permute-start | bytes 36872 | tf_op jit(solution)/shard_map/ppermute | solution.py:284
  83.5 4.3 %collective-permute-start.8 = (f32[24,128]{1,0:T(8,128)S(1)}, f32[24,128]{1,0:T(8,128)S(1)}, u32[]{:S(2)}, u32[]{:S(2)}) collective-permute-start(f32[24,128]{1,0:T(8,128)S(1)} %add.36), channel_id=1, source_target_pairs={{0,2},{1,3},{2,0},{3,1},{4,6},{5,7},{6,4},{7,5},{8,10},{9,11},{10,... | collective-permute-start | bytes 36872 | tf_op jit(solution)/shard_map/ppermute | solution.py:284
  107.5 4.2 %collective-permute-start.11 = (f32[152,128]{1,0:T(8,128)S(1)}, f32[152,128]{1,0:T(8,128)S(1)}, u32[]{:S(2)}, u32[]{:S(2)}) collective-permute-start(f32[152,128]{1,0:T(8,128)S(1)} %get-tuple-element.32), channel_id=1, source_target_pairs={{0,4},{4,0},{1,5},{5,1},{2,6},{6,2},{3,7},{7,3},{8,12},{12,8},{9,1... | collective-permute-start | bytes 233480 | tf_op jit(solution)/shard_map/ppermute | solution.py:284
  111.8 4.9 %collective-permute-start.12 = (f32[152,128]{1,0:T(8,128)S(1)}, f32[152,128]{1,0:T(8,128)S(1)}, u32[]{:S(2)}, u32[]{:S(2)}) collective-permute-start(f32[152,128]{1,0:T(8,128)S(1)} %add.40.a_ref), channel_id=1, source_target_pairs={{0,1},{1,2},{2,3},{3,0},{4,5},{5,6},{6,7},{7,4},{8,9},{9,10},{10,1... | collective-permute-start | bytes 233480 | tf_op jit(solution)/shard_map/ppermute | solution.py:284
  112.7 5.9 %collective-permute-start.13 = (f32[152,128]{1,0:T(8,128)S(1)}, f32[152,128]{1,0:T(8,128)S(1)}, u32[]{:S(2)}, u32[]{:S(2)}) collective-permute-start(f32[152,128]{1,0:T(8,128)S(1)} %add.40.a_ref), channel_id=1, source_target_pairs={{0,2},{1,3},{2,0},{3,1},{4,6},{5,7},{6,4},{7,5},{8,10},{9,11},{10,... | collective-permute-start | bytes 233480 | tf_op jit(solution)/shard_map/ppermute | solution.py:284
  114.7 4.4 %collective-permute-start.14 = (f32[152,128]{1,0:T(8,128)S(1)}, f32[152,128]{1,0:T(8,128)S(1)}, u32[]{:S(2)}, u32[]{:S(2)}) collective-permute-start(f32[152,128]{1,0:T(8,128)S(1)} %add.40.a_ref), channel_id=1, source_target_pairs={{0,3},{1,0},{2,1},{3,2},{4,7},{5,4},{6,5},{7,6},{8,11},{9,8},{10,9... | collective-permute-start | bytes 233480 | tf_op jit(solution)/shard_map/ppermute | solution.py:284
  151.0 4.5 %collective-permute-start.15 = (f32[88,128]{1,0:T(8,128)S(1)}, f32[88,128]{1,0:T(8,128)S(1)}, u32[]{:S(2)}, u32[]{:S(2)}) collective-permute-start(f32[88,128]{1,0:T(8,128)S(1)} %get-tuple-element.37), channel_id=1, source_target_pairs={{0,4},{4,0},{1,5},{5,1},{2,6},{6,2},{3,7},{7,3},{8,12},{12,8},{9,1... | collective-permute-start | bytes 135176 | tf_op jit(solution)/shard_map/ppermute | solution.py:284
  155.6 4.1 %collective-permute-start.16 = (f32[88,128]{1,0:T(8,128)S(1)}, f32[88,128]{1,0:T(8,128)S(1)}, u32[]{:S(2)}, u32[]{:S(2)}) collective-permute-start(f32[88,128]{1,0:T(8,128)S(1)} %add.41.a_ref), channel_id=1, source_target_pairs={{0,1},{1,2},{2,3},{3,0},{4,5},{5,6},{6,7},{7,4},{8,9},{9,10},{10,1... | collective-permute-start | bytes 135176 | tf_op jit(solution)/shard_map/ppermute | solution.py:284
  156.5 4.8 %collective-permute-start.17 = (f32[88,128]{1,0:T(8,128)S(1)}, f32[88,128]{1,0:T(8,128)S(1)}, u32[]{:S(2)}, u32[]{:S(2)}) collective-permute-start(f32[88,128]{1,0:T(8,128)S(1)} %add.41.a_ref), channel_id=1, source_target_pairs={{0,2},{1,3},{2,0},{3,1},{4,6},{5,7},{6,4},{7,5},{8,10},{9,11},{10,... | collective-permute-start | bytes 135176 | tf_op jit(solution)/shard_map/ppermute | solution.py:284
  159.2 3.2 %collective-permute-start.18 = (f32[88,128]{1,0:T(8,128)S(1)}, f32[88,128]{1,0:T(8,128)S(1)}, u32[]{:S(2)}, u32[]{:S(2)}) collective-permute-start(f32[88,128]{1,0:T(8,128)S(1)} %add.41.a_ref), channel_id=1, source_target_pairs={{0,3},{1,0},{2,1},{3,2},{4,7},{5,4},{6,5},{7,6},{8,11},{9,8},{10,9... | collective-permute-start | bytes 135176 | tf_op jit(solution)/shard_map/ppermute | solution.py:284

commit v6 on v5

--- a/solution.py
+++ b/solution.py
@@ -48,7 +48,8 @@
     target = jnp.where(here, jnp.broadcast_to(target_ref[...], (rows, ROWS)), 0)
     target = jnp.broadcast_to(jnp.sum(target, axis=1, keepdims=True), (rows, LANES))
     peer, local = target // 128, target % 32
-    index = (local // 16) * 1024 + (peer % 2) * 512 + (peer // 2) * 16 + local % 16
+    chip = peer // 2 % NZ * NX + peer // 16
+    index = (local // 16) * 1024 + (peer % 2) * 512 + chip * 16 + local % 16
     lane = lax.broadcasted_iota(jnp.int32, (rows, LANES), 1)
     extra = jnp.where(lane == 0, index // 64, jnp.where(lane == 1, index % 64, 0))
     extra = extra.astype(F32).astype(BF)
@@ -339,13 +340,13 @@
     state = start_w
     for sweep in range(SWEEPS):
         first = sweep == 0
-        cross = lax.all_to_all(cross, ("x", "z"), split_axis=0, concat_axis=0, tiled=True)
+        cross = lax.all_to_all(cross, ("z", "x"), split_axis=0, concat_axis=0, tiled=True)
         state, message = call(
             lambda *refs, first=first: activation_body(first, *refs),
             (sds(RANK, LANES), sds(32, 16, LANES, dtype=BF)),
             (cross, gram, state) if first else (cross, state),
         )
-        activ = lax.all_to_all(message, ("x", "z"), split_axis=0, concat_axis=0, tiled=True)
+        activ = lax.all_to_all(message, ("z", "x"), split_axis=0, concat_axis=0, tiled=True)
         activ = activ.reshape(512, LANES)
         size = 152 if first else 88
         part, away = call(

time: 164 us -> 164 us (level)
  waiting for transfers between devices: 54.1 us -> 55.8 us
    all_to_all x1, waiting for transfers between devices: 2.79 us -> 4.46 us  [shards(): lax.all_to_all(cross, ('z', 'x'), split_axis=0, concat_axis=0, tiled=True)]
where the time goes in v6:
time: 164 us
  waiting for transfers between devices  55.8 us (34%)
  starting transfers between devices  48.8 us (30%)
  blocking collectives  43 us (26%)
  Pallas kernels  15.4 us (9%)
    ppermute x2, waiting for transfers between devices, from_ahead(): return lax.ppermute(value, ('z', 'y'), pairs)  34.3 us
    all_to_all x2, blocking collectives, shards(): lax.all_to_all(message, ('z', 'x'), split_axis=0, concat_axis=0, tiled=True)  28.1 us
    ppermute x17, starting transfers between devices, shift(): lax.ppermute(value, axis, [(i, (i + by) % size) for i in range(size)])  26.8 us
    all_to_all x1, blocking collectives, shards(): lax.all_to_all(cross, ('z', 'x'), split_axis=0, concat_axis=0, tiled=True)  14.8 us
    all_to_all x1, starting transfers between devices, shards(): got = lax.all_to_all(send, TGT, split_axis=0, concat_axis=0, tiled=True)  13.1 us
    ppermute x17, waiting for transfers between devices, shift(): lax.ppermute(value, axis, [(i, (i + by) % size) for i in range(size)])  12.5 us
    pallas_call x10, Pallas kernels, call(): pl.pallas_call(body, out_shape=outs, in_specs=[SMEM] * scalars + [VMEM] *...  11.9 us
    all_to_all x1, starting transfers between devices, shards(): lax.all_to_all(cross, ('z', 'x'), split_axis=0, concat_axis=0, tiled=True)  5.31 us
  transfers between devices with their start and end apart: 21, of which 14 were waited for; matrix products, arithmetic and copies ran while one was open for 0% of the time, Pallas kernels for 2%

profile of v6, /device:TPU:1, one launch (start us, length us, event | category | flops | bytes accessed | tf_op | source)
XLA Modules:
  0.0 163.9 jit_solution(1673268443320712825)
XLA Ops:
  0.6 3.6 %shard_map.68 = bf16[64,64,256]{2,1,0:T(8,128)(2,1)} custom-call(bf16[64,7808]{1,0:T(8,128)(2,1)} %flux_ref.1, bf16[64,7808]{1,0:T(8,128)(2,1)} %ivar_ref.1, s32[1,64]{1,0:T(1,128)} %bitcast.10), custom_call_target="tpu_custom_call" | custom-call | flops 999424 | bytes 3997696 | tf_op jit(solution)/shard_map/pallas_call | solution.py:66
  4.2 13.1 %all-to-all-start = ((bf16[64,64,256]{2,1,0:T(8,128)(2,1)}), bf16[64,64,256]{2,1,0:T(8,128)(2,1)S(1)}, u32[]{:S(2)}, u32[]{:S(2)}) async-start(bf16[64,64,256]{2,1,0:T(8,128)(2,1)} %shard_map.68), calls=%async_computation | async-start | bytes 4194304 | tf_op jit(solution)/shard_map/all_to_all | solution.py:319
  21.7 1.6 %collective-permute-start.1 = (f32[24,128]{1,0:T(8,128)S(1)}, f32[24,128]{1,0:T(8,128)S(1)}, u32[]{:S(2)}, u32[]{:S(2)}) collective-permute-start(f32[24,128]{1,0:T(8,128)S(1)} %add.32), channel_id=1, source_target_pairs={{0,128},{64,192},{128,0},{192,64},{1,129},{65,193},{129,1},{193,65... | collective-permute-start | bytes 36872 | tf_op jit(solution)/shard_map/ppermute | solution.py:285
  24.5 1.6 %collective-permute-done.1 = f32[24,128]{1,0:T(8,128)S(1)} collective-permute-done((f32[24,128]{1,0:T(8,128)S(1)}, f32[24,128]{1,0:T(8,128)S(1)}, u32[]{:S(2)}, u32[]{:S(2)}) %collective-permute-start.1) | collective-permute-done | bytes 12320 | tf_op jit(solution)/shard_map/ppermute | solution.py:285
  26.8 2.9 %collective-permute-start.5 = (f32[24,128]{1,0:T(8,128)S(1)}, f32[24,128]{1,0:T(8,128)S(1)}, u32[]{:S(2)}, u32[]{:S(2)}) collective-permute-start(f32[24,128]{1,0:T(8,128)S(1)} %add_add_fusion.1), channel_id=1, source_target_pairs={{8,0},{25,1},{42,2},{59,3},{16,8},{33,9},{50,10},{3,11},{24,16},{4... | collective-permute-start | bytes 36872 | tf_op jit(solution)/shard_map/ppermute | solution.py:298
  29.8 34.3 %collective-permute-done.5 = f32[24,128]{1,0:T(8,128)S(1)} collective-permute-done((f32[24,128]{1,0:T(8,128)S(1)}, f32[24,128]{1,0:T(8,128)S(1)}, u32[]{:S(2)}, u32[]{:S(2)}) %collective-permute-start.5) | collective-permute-done | bytes 12320 | tf_op jit(solution)/shard_map/ppermute | solution.py:298
  64.1 4.5 %all-to-all-done = bf16[64,64,256]{2,1,0:T(8,128)(2,1)S(1)} async-done(((bf16[64,64,256]{2,1,0:T(8,128)(2,1)}), bf16[64,64,256]{2,1,0:T(8,128)(2,1)S(1)}, u32[]{:S(2)}, u32[]{:S(2)}) %all-to-all-start) | async-done | bytes 2097184 | tf_op jit(solution)/shard_map/all_to_all | solution.py:319
  68.6 2.6 %shard_map.70 = (bf16[512,256]{1,0:T(8,128)(2,1)S(1)}, bf16[64,4096]{1,0:T(8,128)(2,1)S(1)}, f32[8,4096]{1,0:T(8,128)S(1)}) custom-call(s32[1]{0:T(128)} %bitcast.1.core_ref, bf16[4096,256]{1,0:T(8,128)(2,1)S(1)} %bitcast.5), custom_call_target="tpu_custom_call" | custom-call | flops 2147483648 | tf_op jit(solution)/shard_map/pallas_call | solution.py:28
  71.7 2.3 %shard_map.71.keep_ref = bf16[512,256]{1,0:T(8,128)(2,1)S(1)} custom-call(s32[1]{0:T(128)} %bitcast.1.core_ref, bf16[4096,256]{1,0:T(8,128)(2,1)S(1)} %bitcast.6, bf16[64,4096]{1,0:T(8,128)(2,1)S(1)} %get-tuple-element.24.low_ref, f32[8,4096]{1,0:T(8,128)S(1)} %get-tuple-element.25.high_ref), custom_call_target="tpu_custom_call" | custom-call | flops 2147483648 | tf_op jit(solution)/shard_map/pallas_call | solution.py:28
  75.1 5.3 %all-to-all-start.1 = ((f32[32,16,128]{2,1,0:T(8,128)}), f32[32,16,128]{2,1,0:T(8,128)S(1)}, u32[]{:S(2)}, u32[]{:S(2)}) async-start(f32[32,16,128]{2,1,0:T(8,128)} %shard_map.72), calls=%async_computation.1 | async-start | bytes 524288 | tf_op jit(solution)/shard_map/all_to_all | solution.py:343
  80.4 2.0 %collective-permute-start.9 = (f32[24,128]{1,0:T(8,128)S(1)}, f32[24,128]{1,0:T(8,128)S(1)}, u32[]{:S(2)}, u32[]{:S(2)}) collective-permute-start(f32[24,128]{1,0:T(8,128)S(1)} %add.36), channel_id=1, source_target_pairs={{0,1},{1,2},{2,3},{3,0},{4,5},{5,6},{6,7},{7,4},{8,9},{9,10},{10,1... | collective-permute-start | bytes 36872 | tf_op jit(solution)/shard_map/ppermute | solution.py:285
  83.6 1.9 %collective-permute-start.8 = (f32[24,128]{1,0:T(8,128)S(1)}, f32[24,128]{1,0:T(8,128)S(1)}, u32[]{:S(2)}, u32[]{:S(2)}) collective-permute-start(f32[24,128]{1,0:T(8,128)S(1)} %add.36), channel_id=1, source_target_pairs={{0,2},{1,3},{2,0},{3,1},{4,6},{5,7},{6,4},{7,5},{8,10},{9,11},{10,... | collective-permute-start | bytes 36872 | tf_op jit(solution)/shard_map/ppermute | solution.py:285
  85.5 2.4 %collective-permute-done.8 = f32[24,128]{1,0:T(8,128)S(1)} collective-permute-done((f32[24,128]{1,0:T(8,128)S(1)}, f32[24,128]{1,0:T(8,128)S(1)}, u32[]{:S(2)}, u32[]{:S(2)}) %collective-permute-start.8) | collective-permute-done | bytes 12320 | tf_op jit(solution)/shard_map/ppermute | solution.py:285
  87.9 4.5 %all-to-all-done.1.refs_0_ = f32[32,16,128]{2,1,0:T(8,128)S(1)} async-done(((f32[32,16,128]{2,1,0:T(8,128)}), f32[32,16,128]{2,1,0:T(8,128)S(1)}, u32[]{:S(2)}, u32[]{:S(2)}) %all-to-all-start.1) | async-done | bytes 262176 | tf_op jit(solution)/shard_map/all_to_all | solution.py:343
  93.3 13.6 %all_to_all.25 = bf16[32,16,128]{2,1,0:T(8,128)(2,1)S(1)} all-to-all(bf16[32,16,128]{2,1,0:T(8,128)(2,1)S(1)} %get-tuple-element.30), channel_id=1, replica_groups=mesh['x'=4,'z'=8,'c'=2,'y'=4] {'z','x'}, dimensions={0} | all-to-all | bytes 262144 | tf_op jit(solution)/shard_map/all_to_all | solution.py:349
  107.4 3.6 %collective-permute-start.11 = (f32[152,128]{1,0:T(8,128)S(1)}, f32[152,128]{1,0:T(8,128)S(1)}, u32[]{:S(2)}, u32[]{:S(2)}) collective-permute-start(f32[152,128]{1,0:T(8,128)S(1)} %get-tuple-element.32), channel_id=1, source_target_pairs={{0,4},{4,0},{1,5},{5,1},{2,6},{6,2},{3,7},{7,3},{8,12},{12,8},{9,1... | collective-permute-start | bytes 233480 | tf_op jit(solution)/shard_map/ppermute | solution.py:285
  112.9 2.1 %collective-permute-start.13 = (f32[152,128]{1,0:T(8,128)S(1)}, f32[152,128]{1,0:T(8,128)S(1)}, u32[]{:S(2)}, u32[]{:S(2)}) collective-permute-start(f32[152,128]{1,0:T(8,128)S(1)} %add.40.a_ref), channel_id=1, source_target_pairs={{0,2},{1,3},{2,0},{3,1},{4,6},{5,7},{6,4},{7,5},{8,10},{9,11},{10,... | collective-permute-start | bytes 233480 | tf_op jit(solution)/shard_map/ppermute | solution.py:285
  114.9 1.6 collective-permute-start.14
  116.8 1.9 %collective-permute-done.13.c_ref = f32[152,128]{1,0:T(8,128)S(1)} collective-permute-done((f32[152,128]{1,0:T(8,128)S(1)}, f32[152,128]{1,0:T(8,128)S(1)}, u32[]{:S(2)}, u32[]{:S(2)}) %collective-permute-start.13) | collective-permute-done | bytes 77856 | tf_op jit(solution)/shard_map/ppermute | solution.py:285
  120.8 14.8 %all_to_all.26.refs_0_ = bf16[32,40,128]{2,1,0:T(8,128)(2,1)S(1)} all-to-all(bf16[32,40,128]{2,1,0:T(8,128)(2,1)S(1)} %get-tuple-element.33), channel_id=1, replica_groups=mesh['x'=4,'z'=8,'c'=2,'y'=4] {'z','x'}, dimensions={0} | all-to-all | bytes 655360 | tf_op jit(solution)/shard_map/all_to_all | solution.py:343
  136.5 14.5 %all_to_all.27 = bf16[32,16,128]{2,1,0:T(8,128)(2,1)S(1)} all-to-all(bf16[32,16,128]{2,1,0:T(8,128)(2,1)S(1)} %get-tuple-element.35), channel_id=1, replica_groups=mesh['x'=4,'z'=8,'c'=2,'y'=4] {'z','x'}, dimensions={0} | all-to-all | bytes 262144 | tf_op jit(solution)/shard_map/all_to_all | solution.py:349
  151.5 3.2 %collective-permute-start.15 = (f32[88,128]{1,0:T(8,128)S(1)}, f32[88,128]{1,0:T(8,128)S(1)}, u32[]{:S(2)}, u32[]{:S(2)}) collective-permute-start(f32[88,128]{1,0:T(8,128)S(1)} %get-tuple-element.37), channel_id=1, source_target_pairs={{0,4},{4,0},{1,5},{5,1},{2,6},{6,2},{3,7},{7,3},{8,12},{12,8},{9,1... | collective-permute-start | bytes 135176 | tf_op jit(solution)/shard_map/ppermute | solution.py:285
  156.6 2.7 %collective-permute-start.17 = (f32[88,128]{1,0:T(8,128)S(1)}, f32[88,128]{1,0:T(8,128)S(1)}, u32[]{:S(2)}, u32[]{:S(2)}) collective-permute-start(f32[88,128]{1,0:T(8,128)S(1)} %add.41.a_ref), channel_id=1, source_target_pairs={{0,2},{1,3},{2,0},{3,1},{4,6},{5,7},{6,4},{7,5},{8,10},{9,11},{10,... | collective-permute-start | bytes 135176 | tf_op jit(solution)/shard_map/ppermute | solution.py:285
  159.7 1.7 %collective-permute-done.17.c_ref = f32[88,128]{1,0:T(8,128)S(1)} collective-permute-done((f32[88,128]{1,0:T(8,128)S(1)}, f32[88,128]{1,0:T(8,128)S(1)}, u32[]{:S(2)}, u32[]{:S(2)}) %collective-permute-start.17) | collective-permute-done | bytes 45088 | tf_op jit(solution)/shard_map/ppermute | solution.py:285
  (43 shorter events, 20.6 us)
Async XLA Ops:
  4.2 13.1 %copy-start.1 = (f32[64,122]{1,0:T(8,128)S(1)}, f32[64,122]{1,0:T(8,128)}, u32[]{:S(2)}) copy-start(f32[64,122]{1,0:T(8,128)} %param.9) | copy-start | bytes 93700
  4.2 64.4 %all-to-all-start = ((bf16[64,64,256]{2,1,0:T(8,128)(2,1)}), bf16[64,64,256]{2,1,0:T(8,128)(2,1)S(1)}, u32[]{:S(2)}, u32[]{:S(2)}) async-start(bf16[64,64,256]{2,1,0:T(8,128)(2,1)} %shard_map.68), calls=%async_computation | async-start | bytes 4194304 | tf_op jit(solution)/shard_map/all_to_all | solution.py:319
  17.6 1.3 collective-permute-start
  19.0 5.5 %collective-permute-start.2 = (f32[24,128]{1,0:T(8,128)S(1)}, f32[24,128]{1,0:T(8,128)S(1)}, u32[]{:S(2)}, u32[]{:S(2)}) collective-permute-start(f32[24,128]{1,0:T(8,128)S(1)} %add.32), channel_id=1, source_target_pairs={{0,64},{64,128},{128,192},{192,0},{1,65},{65,129},{129,193},{193,1... | collective-permute-start | bytes 36872 | tf_op jit(solution)/shard_map/ppermute | solution.py:285
  20.3 4.3 %collective-permute-start.3 = (f32[24,128]{1,0:T(8,128)S(1)}, f32[24,128]{1,0:T(8,128)S(1)}, u32[]{:S(2)}, u32[]{:S(2)}) collective-permute-start(f32[24,128]{1,0:T(8,128)S(1)} %add.32), channel_id=1, source_target_pairs={{0,192},{64,0},{128,64},{192,128},{1,193},{65,1},{129,65},{193,129... | collective-permute-start | bytes 36872 | tf_op jit(solution)/shard_map/ppermute | solution.py:285
  21.7 4.5 %collective-permute-start.1 = (f32[24,128]{1,0:T(8,128)S(1)}, f32[24,128]{1,0:T(8,128)S(1)}, u32[]{:S(2)}, u32[]{:S(2)}) collective-permute-start(f32[24,128]{1,0:T(8,128)S(1)} %add.32), channel_id=1, source_target_pairs={{0,128},{64,192},{128,0},{192,64},{1,129},{65,193},{129,1},{193,65... | collective-permute-start | bytes 36872 | tf_op jit(solution)/shard_map/ppermute | solution.py:285
  23.3 40.7 %collective-permute-start.6 = (f32[64,128]{1,0:T(8,128)S(1)}, f32[64,128]{1,0:T(8,128)S(1)}, u32[]{:S(2)}, u32[]{:S(2)}) collective-permute-start(f32[64,128]{1,0:T(8,128)S(1)} %pad.4.templ_ref.own_ref), channel_id=1, source_target_pairs={{0,4},{4,0},{1,5},{5,1},{2,6},{6,2},{3,7},{7,3},{8,12},{12,8},{9,1... | collective-permute-start | bytes 98312 | tf_op jit(solution)/shard_map/ppermute | solution.py:285
  26.2 3.6 %collective-permute-start.4 = (f32[24,128]{1,0:T(8,128)S(1)}, f32[24,128]{1,0:T(8,128)S(1)}, u32[]{:S(2)}, u32[]{:S(2)}) collective-permute-start(f32[24,128]{1,0:T(8,128)S(1)} %add_add_fusion.1), channel_id=1, source_target_pairs={{0,0},{17,1},{34,2},{51,3},{8,8},{25,9},{42,10},{59,11},{16,16},{3... | collective-permute-start | bytes 36872 | tf_op jit(solution)/shard_map/ppermute | solution.py:298
  26.8 37.2 %collective-permute-start.5 = (f32[24,128]{1,0:T(8,128)S(1)}, f32[24,128]{1,0:T(8,128)S(1)}, u32[]{:S(2)}, u32[]{:S(2)}) collective-permute-start(f32[24,128]{1,0:T(8,128)S(1)} %add_add_fusion.1), channel_id=1, source_target_pairs={{8,0},{25,1},{42,2},{59,3},{16,8},{33,9},{50,10},{3,11},{24,16},{4... | collective-permute-start | bytes 36872 | tf_op jit(solution)/shard_map/ppermute | solution.py:298
  71.2 2.8 %collective-permute-start.7 = (bf16[512,256]{1,0:T(8,128)(2,1)S(1)}, bf16[512,256]{1,0:T(8,128)(2,1)S(1)}, u32[]{:S(2)}, u32[]{:S(2)}) collective-permute-start(bf16[512,256]{1,0:T(8,128)(2,1)S(1)} %get-tuple-element.26), channel_id=1, source_target_pairs={{0,4},{4,0},{1,5},{5,1},{2,6},{6,2},{3,7},{7,3},{8,12},{12,8},{9,1... | collective-permute-start | bytes 786440 | tf_op jit(solution)/shard_map/ppermute | solution.py:285
  71.7 20.7 %copy-start = (f32[32,64]{1,0:T(8,128)S(1)}, f32[32,64]{1,0:T(8,128)}, u32[]{:S(2)}) copy-start(f32[32,64]{1,0:T(8,128)} %refs_2_.1) | copy-start | bytes 24580
  75.1 17.3 %all-to-all-start.1 = ((f32[32,16,128]{2,1,0:T(8,128)}), f32[32,16,128]{2,1,0:T(8,128)S(1)}, u32[]{:S(2)}, u32[]{:S(2)}) async-start(f32[32,16,128]{2,1,0:T(8,128)} %shard_map.72), calls=%async_computation.1 | async-start | bytes 524288 | tf_op jit(solution)/shard_map/all_to_all | solution.py:343
  80.4 5.1 %collective-permute-start.9 = (f32[24,128]{1,0:T(8,128)S(1)}, f32[24,128]{1,0:T(8,128)S(1)}, u32[]{:S(2)}, u32[]{:S(2)}) collective-permute-start(f32[24,128]{1,0:T(8,128)S(1)} %add.36), channel_id=1, source_target_pairs={{0,1},{1,2},{2,3},{3,0},{4,5},{5,6},{6,7},{7,4},{8,9},{9,10},{10,1... | collective-permute-start | bytes 36872 | tf_op jit(solution)/shard_map/ppermute | solution.py:285
  82.4 3.1 %collective-permute-start.10 = (f32[24,128]{1,0:T(8,128)S(1)}, f32[24,128]{1,0:T(8,128)S(1)}, u32[]{:S(2)}, u32[]{:S(2)}) collective-permute-start(f32[24,128]{1,0:T(8,128)S(1)} %add.36), channel_id=1, source_target_pairs={{0,3},{1,0},{2,1},{3,2},{4,7},{5,4},{6,5},{7,6},{8,11},{9,8},{10,9... | collective-permute-start | bytes 36872 | tf_op jit(solution)/shard_map/ppermute | solution.py:285
  83.6 4.3 %collective-permute-start.8 = (f32[24,128]{1,0:T(8,128)S(1)}, f32[24,128]{1,0:T(8,128)S(1)}, u32[]{:S(2)}, u32[]{:S(2)}) collective-permute-start(f32[24,128]{1,0:T(8,128)S(1)} %add.36), channel_id=1, source_target_pairs={{0,2},{1,3},{2,0},{3,1},{4,6},{5,7},{6,4},{7,5},{8,10},{9,11},{10,... | collective-permute-start | bytes 36872 | tf_op jit(solution)/shard_map/ppermute | solution.py:285
  107.4 4.5 %collective-permute-start.11 = (f32[152,128]{1,0:T(8,128)S(1)}, f32[152,128]{1,0:T(8,128)S(1)}, u32[]{:S(2)}, u32[]{:S(2)}) collective-permute-start(f32[152,128]{1,0:T(8,128)S(1)} %get-tuple-element.32), channel_id=1, source_target_pairs={{0,4},{4,0},{1,5},{5,1},{2,6},{6,2},{3,7},{7,3},{8,12},{12,8},{9,1... | collective-permute-start | bytes 233480 | tf_op jit(solution)/shard_map/ppermute | solution.py:285
  111.9 4.9 %collective-permute-start.12 = (f32[152,128]{1,0:T(8,128)S(1)}, f32[152,128]{1,0:T(8,128)S(1)}, u32[]{:S(2)}, u32[]{:S(2)}) collective-permute-start(f32[152,128]{1,0:T(8,128)S(1)} %add.40.a_ref), channel_id=1, source_target_pairs={{0,1},{1,2},{2,3},{3,0},{4,5},{5,6},{6,7},{7,4},{8,9},{9,10},{10,1... | collective-permute-start | bytes 233480 | tf_op jit(solution)/shard_map/ppermute | solution.py:285
  112.9 5.9 %collective-permute-start.13 = (f32[152,128]{1,0:T(8,128)S(1)}, f32[152,128]{1,0:T(8,128)S(1)}, u32[]{:S(2)}, u32[]{:S(2)}) collective-permute-start(f32[152,128]{1,0:T(8,128)S(1)} %add.40.a_ref), channel_id=1, source_target_pairs={{0,2},{1,3},{2,0},{3,1},{4,6},{5,7},{6,4},{7,5},{8,10},{9,11},{10,... | collective-permute-start | bytes 233480 | tf_op jit(solution)/shard_map/ppermute | solution.py:285
  114.9 4.4 %collective-permute-start.14 = (f32[152,128]{1,0:T(8,128)S(1)}, f32[152,128]{1,0:T(8,128)S(1)}, u32[]{:S(2)}, u32[]{:S(2)}) collective-permute-start(f32[152,128]{1,0:T(8,128)S(1)} %add.40.a_ref), channel_id=1, source_target_pairs={{0,3},{1,0},{2,1},{3,2},{4,7},{5,4},{6,5},{7,6},{8,11},{9,8},{10,9... | collective-permute-start | bytes 233480 | tf_op jit(solution)/shard_map/ppermute | solution.py:285
  151.5 4.0 %collective-permute-start.15 = (f32[88,128]{1,0:T(8,128)S(1)}, f32[88,128]{1,0:T(8,128)S(1)}, u32[]{:S(2)}, u32[]{:S(2)}) collective-permute-start(f32[88,128]{1,0:T(8,128)S(1)} %get-tuple-element.37), channel_id=1, source_target_pairs={{0,4},{4,0},{1,5},{5,1},{2,6},{6,2},{3,7},{7,3},{8,12},{12,8},{9,1... | collective-permute-start | bytes 135176 | tf_op jit(solution)/shard_map/ppermute | solution.py:285
  155.5 4.1 %collective-permute-start.16 = (f32[88,128]{1,0:T(8,128)S(1)}, f32[88,128]{1,0:T(8,128)S(1)}, u32[]{:S(2)}, u32[]{:S(2)}) collective-permute-start(f32[88,128]{1,0:T(8,128)S(1)} %add.41.a_ref), channel_id=1, source_target_pairs={{0,1},{1,2},{2,3},{3,0},{4,5},{5,6},{6,7},{7,4},{8,9},{9,10},{10,1... | collective-permute-start | bytes 135176 | tf_op jit(solution)/shard_map/ppermute | solution.py:285
  156.6 4.7 %collective-permute-start.17 = (f32[88,128]{1,0:T(8,128)S(1)}, f32[88,128]{1,0:T(8,128)S(1)}, u32[]{:S(2)}, u32[]{:S(2)}) collective-permute-start(f32[88,128]{1,0:T(8,128)S(1)} %add.41.a_ref), channel_id=1, source_target_pairs={{0,2},{1,3},{2,0},{3,1},{4,6},{5,7},{6,4},{7,5},{8,10},{9,11},{10,... | collective-permute-start | bytes 135176 | tf_op jit(solution)/shard_map/ppermute | solution.py:285
  159.3 3.2 %collective-permute-start.18 = (f32[88,128]{1,0:T(8,128)S(1)}, f32[88,128]{1,0:T(8,128)S(1)}, u32[]{:S(2)}, u32[]{:S(2)}) collective-permute-start(f32[88,128]{1,0:T(8,128)S(1)} %add.41.a_ref), channel_id=1, source_target_pairs={{0,3},{1,0},{2,1},{3,2},{4,7},{5,4},{6,5},{7,6},{8,11},{9,8},{10,9... | collective-permute-start | bytes 135176 | tf_op jit(solution)/shard_map/ppermute | solution.py:285

commit v7 on v5

--- a/solution.py
+++ b/solution.py
@@ -292,14 +292,14 @@
 
 def from_ahead(value, by):
     pairs = [
-        ((z + 2 * y + by) % NZ * NY + y, z * NY + y) for z in range(NZ) for y in range(NY)
+        ((z + 4 * c + by) % NZ * NC + c, z * NC + c) for z in range(NZ) for c in range(NC)
     ]
-    return lax.ppermute(value, ("z", "y"), pairs)
+    return lax.ppermute(value, ("z", "c"), pairs)
 
 
 def near(part):
     part = ring_sum(part + shift(part, "c", NC, 1), "x", NX, 1)
-    return from_ahead(part, 0) + from_ahead(part, 1)
+    return sum(from_ahead(part, by) for by in range(4))
 
 
 def first_message_body(own_ref, other_ref, keep_ref, came_ref, out_ref):
@@ -319,6 +319,7 @@
     gram = near(call(first_gram_body, sds(24, LANES), (templates,)))
     other = shift(templates, "c", NC, 1)
     got, gram, other = lax.optimization_barrier((got, gram, other))
+    gram = gram + shift(gram, "c", NC, 1)
     rows = got.reshape(N_TGT * ROWS, 2 * LANES)
     half = sds(512, 2 * LANES, dtype=BF)
     cost = 2 * 1024 * N_TGT * ROWS * 2 * LANES
@@ -335,7 +336,6 @@
         first_message_body, sds(32, 16, LANES), (templates, other, keep, came)
     )
     cross, gram = lax.optimization_barrier((cross, gram))
-    gram = ring_sum(gram, "y", NY, 1)
     state = start_w
     for sweep in range(SWEEPS):
         first = sweep == 0

time: 164 us -> 163 us (level)
  blocking collectives: 44.5 us -> 59.5 us
  waiting for transfers between devices: 54.1 us -> 42.7 us
  starting transfers between devices: 49 us -> 44.3 us
    all_to_all x1 -> x2, blocking collectives: 13.3 us -> 28.2 us  [shards(): lax.all_to_all(cross, ('x', 'z'), split_axis=0, concat_axis=0, tiled=True)]
    ppermute x2 -> x4, starting transfers between devices: 3.58 us -> 10.7 us  [from_ahead(): return lax.ppermute(value, ('z', 'c'), pairs)]
    ppermute x17 -> x15, starting transfers between devices: 27 us -> 20.6 us  [shift(): lax.ppermute(value, axis, [(i, (i + by) % size) for i in range(size)])]
    all_to_all x1 -> x0, starting transfers between devices: 5.31 us -> none  [shards(): lax.all_to_all(cross, ('x', 'z'), split_axis=0, concat_axis=0, tiled=True)]
    all_to_all x1, waiting for transfers between devices: 4.53 us -> 0.01 us  [shards(): got = lax.all_to_all(send, TGT, split_axis=0, concat_axis=0, tiled=True)]
    all_to_all x1 -> x0, waiting for transfers between devices: 2.79 us -> none  [shards(): lax.all_to_all(cross, ('x', 'z'), split_axis=0, concat_axis=0, tiled=True)]
    ppermute x17 -> x15, waiting for transfers between devices: 12.5 us -> 10.3 us  [shift(): lax.ppermute(value, axis, [(i, (i + by) % size) for i in range(size)])]
    ppermute x2 -> x4, waiting for transfers between devices: 34.3 us -> 32.5 us  [from_ahead(): return lax.ppermute(value, ('z', 'c'), pairs)]
  transfers between devices with their start and end apart: 21 -> 20, of which waited for: 14 -> 13; matrix products, arithmetic and copies ran while one was open for 0% -> 0% of each run, Pallas kernels for 2% -> 2%
where the time goes in v7:
time: 163 us; the launch traced here: 162 us
  blocking collectives  59.5 us (37%)
  starting transfers between devices  44.3 us (27%)
  waiting for transfers between devices  42.7 us (26%)
  Pallas kernels  14.7 us (9%)
    ppermute x4, waiting for transfers between devices, from_ahead(): return lax.ppermute(value, ('z', 'c'), pairs)  32.5 us
    all_to_all x2, blocking collectives, shards(): lax.all_to_all(message, ('x', 'z'), split_axis=0, concat_axis=0, tiled=True)  31.3 us
    all_to_all x2, blocking collectives, shards(): lax.all_to_all(cross, ('x', 'z'), split_axis=0, concat_axis=0, tiled=True)  28.2 us
    ppermute x15, starting transfers between devices, shift(): lax.ppermute(value, axis, [(i, (i + by) % size) for i in range(size)])  20.6 us
    all_to_all x1, starting transfers between devices, shards(): got = lax.all_to_all(send, TGT, split_axis=0, concat_axis=0, tiled=True)  13.1 us
    pallas_call x10, Pallas kernels, call(): pl.pallas_call(body, out_shape=outs, in_specs=[SMEM] * scalars + [VMEM] *...  11.2 us
    ppermute x4, starting transfers between devices, from_ahead(): return lax.ppermute(value, ('z', 'c'), pairs)  10.7 us
    ppermute x15, waiting for transfers between devices, shift(): lax.ppermute(value, axis, [(i, (i + by) % size) for i in range(size)])  10.3 us
  transfers between devices with their start and end apart: 20, of which 13 were waited for; matrix products, arithmetic and copies ran while one was open for 0% of the time, Pallas kernels for 2%

profile of v7, /device:TPU:1, one launch (start us, length us, event | category | flops | bytes accessed | tf_op | source)
XLA Modules:
  0.0 162.1 jit_solution(6799834327653221737)
XLA Ops:
  0.6 3.6 %shard_map.68 = bf16[64,64,256]{2,1,0:T(8,128)(2,1)} custom-call(bf16[64,7808]{1,0:T(8,128)(2,1)} %flux_ref.1, bf16[64,7808]{1,0:T(8,128)(2,1)} %ivar_ref.1, s32[1,64]{1,0:T(1,128)} %bitcast.10), custom_call_target="tpu_custom_call" | custom-call | flops 999424 | bytes 3997696 | tf_op jit(solution)/shard_map/pallas_call | solution.py:65
  4.2 13.1 %all-to-all-start = ((bf16[64,64,256]{2,1,0:T(8,128)(2,1)}), bf16[64,64,256]{2,1,0:T(8,128)(2,1)S(1)}, u32[]{:S(2)}, u32[]{:S(2)}) async-start(bf16[64,64,256]{2,1,0:T(8,128)(2,1)} %shard_map.68), calls=%async_computation | async-start | bytes 4194304 | tf_op jit(solution)/shard_map/all_to_all | solution.py:318
  20.2 1.4 collective-permute-start.3
  21.7 1.6 %collective-permute-start.1 = (f32[24,128]{1,0:T(8,128)S(1)}, f32[24,128]{1,0:T(8,128)S(1)}, u32[]{:S(2)}, u32[]{:S(2)}) collective-permute-start(f32[24,128]{1,0:T(8,128)S(1)} %add.32), channel_id=1, source_target_pairs={{0,128},{64,192},{128,0},{192,64},{1,129},{65,193},{129,1},{193,65... | collective-permute-start | bytes 36872 | tf_op jit(solution)/shard_map/ppermute | solution.py:284
  23.7 2.4 %collective-permute-done.1 = f32[24,128]{1,0:T(8,128)S(1)} collective-permute-done((f32[24,128]{1,0:T(8,128)S(1)}, f32[24,128]{1,0:T(8,128)S(1)}, u32[]{:S(2)}, u32[]{:S(2)}) %collective-permute-start.1) | collective-permute-done | bytes 12320 | tf_op jit(solution)/shard_map/ppermute | solution.py:284
  26.2 2.0 %collective-permute-start.7 = (f32[24,128]{1,0:T(8,128)S(1)}, f32[24,128]{1,0:T(8,128)S(1)}, u32[]{:S(2)}, u32[]{:S(2)}) collective-permute-start(f32[24,128]{1,0:T(8,128)S(1)} %add_add_fusion.1), channel_id=1, source_target_pairs={{24,0},{60,4},{32,8},{4,12},{40,16},{12,20},{48,24},{20,28},{56,32... | collective-permute-start | bytes 36872 | tf_op jit(solution)/shard_map/ppermute | solution.py:297
  28.2 1.5 collective-permute-start.6
  29.7 4.5 %collective-permute-start.4 = (f32[24,128]{1,0:T(8,128)S(1)}, f32[24,128]{1,0:T(8,128)S(1)}, u32[]{:S(2)}, u32[]{:S(2)}) collective-permute-start(f32[24,128]{1,0:T(8,128)S(1)} %add_add_fusion.1), channel_id=1, source_target_pairs={{0,0},{36,4},{8,8},{44,12},{16,16},{52,20},{24,24},{60,28},{32,32}... | collective-permute-start | bytes 36872 | tf_op jit(solution)/shard_map/ppermute | solution.py:297
  34.2 2.6 %collective-permute-start.5 = (f32[24,128]{1,0:T(8,128)S(1)}, f32[24,128]{1,0:T(8,128)S(1)}, u32[]{:S(2)}, u32[]{:S(2)}) collective-permute-start(f32[24,128]{1,0:T(8,128)S(1)} %add_add_fusion.1), channel_id=1, source_target_pairs={{8,0},{44,4},{16,8},{52,12},{24,16},{60,20},{32,24},{4,28},{40,32}... | collective-permute-start | bytes 36872 | tf_op jit(solution)/shard_map/ppermute | solution.py:297
  36.8 26.6 %collective-permute-done.7 = f32[24,128]{1,0:T(8,128)S(1)} collective-permute-done((f32[24,128]{1,0:T(8,128)S(1)}, f32[24,128]{1,0:T(8,128)S(1)}, u32[]{:S(2)}, u32[]{:S(2)}) %collective-permute-start.7) | collective-permute-done | bytes 12320 | tf_op jit(solution)/shard_map/ppermute | solution.py:297
  63.4 3.1 %collective-permute-done.6 = f32[24,128]{1,0:T(8,128)S(1)} collective-permute-done((f32[24,128]{1,0:T(8,128)S(1)}, f32[24,128]{1,0:T(8,128)S(1)}, u32[]{:S(2)}, u32[]{:S(2)}) %collective-permute-start.6) | collective-permute-done | bytes 12320 | tf_op jit(solution)/shard_map/ppermute | solution.py:297
  66.5 2.8 %collective-permute-done.4 = f32[24,128]{1,0:T(8,128)S(1)} collective-permute-done((f32[24,128]{1,0:T(8,128)S(1)}, f32[24,128]{1,0:T(8,128)S(1)}, u32[]{:S(2)}, u32[]{:S(2)}) %collective-permute-start.4) | collective-permute-done | bytes 12320 | tf_op jit(solution)/shard_map/ppermute | solution.py:297
  69.3 2.7 %shard_map.70 = (bf16[512,256]{1,0:T(8,128)(2,1)S(1)}, bf16[64,4096]{1,0:T(8,128)(2,1)S(1)}, f32[8,4096]{1,0:T(8,128)S(1)}) custom-call(s32[1]{0:T(128)} %bitcast.1.core_ref, bf16[4096,256]{1,0:T(8,128)(2,1)S(1)} %bitcast.5), custom_call_target="tpu_custom_call" | custom-call | flops 2147483648 | tf_op jit(solution)/shard_map/pallas_call | solution.py:28
  72.6 2.3 %shard_map.71.keep_ref = bf16[512,256]{1,0:T(8,128)(2,1)S(1)} custom-call(s32[1]{0:T(128)} %bitcast.1.core_ref, bf16[4096,256]{1,0:T(8,128)(2,1)S(1)} %bitcast.6, bf16[64,4096]{1,0:T(8,128)(2,1)S(1)} %get-tuple-element.24.low_ref, f32[8,4096]{1,0:T(8,128)S(1)} %get-tuple-element.25.high_ref), custom_call_target="tpu_custom_call" | custom-call | flops 2147483648 | tf_op jit(solution)/shard_map/pallas_call | solution.py:28
  75.2 15.0 %all_to_all.25.refs_0_ = f32[32,16,128]{2,1,0:T(8,128)S(1)} all-to-all(f32[32,16,128]{2,1,0:T(8,128)S(1)} %shard_map.72), channel_id=1, replica_groups=mesh['x'=4,'z'=8,'c'=2,'y'=4] {'x','z'}, dimensions={0} | all-to-all | bytes 524288 | tf_op jit(solution)/shard_map/all_to_all | solution.py:342
  91.2 15.5 %all_to_all.26 = bf16[32,16,128]{2,1,0:T(8,128)(2,1)S(1)} all-to-all(bf16[32,16,128]{2,1,0:T(8,128)(2,1)S(1)} %get-tuple-element.30), channel_id=1, replica_groups=mesh['x'=4,'z'=8,'c'=2,'y'=4] {'x','z'}, dimensions={0} | all-to-all | bytes 262144 | tf_op jit(solution)/shard_map/all_to_all | solution.py:348
  107.1 2.4 %collective-permute-start.11 = (f32[152,128]{1,0:T(8,128)S(1)}, f32[152,128]{1,0:T(8,128)S(1)}, u32[]{:S(2)}, u32[]{:S(2)}) collective-permute-start(f32[152,128]{1,0:T(8,128)S(1)} %get-tuple-element.32), channel_id=1, source_target_pairs={{0,4},{4,0},{1,5},{5,1},{2,6},{6,2},{3,7},{7,3},{8,12},{12,8},{9,1... | collective-permute-start | bytes 233480 | tf_op jit(solution)/shard_map/ppermute | solution.py:284
  111.8 2.6 %collective-permute-start.13 = (f32[152,128]{1,0:T(8,128)S(1)}, f32[152,128]{1,0:T(8,128)S(1)}, u32[]{:S(2)}, u32[]{:S(2)}) collective-permute-start(f32[152,128]{1,0:T(8,128)S(1)} %add.40.a_ref), channel_id=1, source_target_pairs={{0,2},{1,3},{2,0},{3,1},{4,6},{5,7},{6,4},{7,5},{8,10},{9,11},{10,... | collective-permute-start | bytes 233480 | tf_op jit(solution)/shard_map/ppermute | solution.py:284
  115.5 2.7 %collective-permute-done.13.c_ref = f32[152,128]{1,0:T(8,128)S(1)} collective-permute-done((f32[152,128]{1,0:T(8,128)S(1)}, f32[152,128]{1,0:T(8,128)S(1)}, u32[]{:S(2)}, u32[]{:S(2)}) %collective-permute-start.13) | collective-permute-done | bytes 77856 | tf_op jit(solution)/shard_map/ppermute | solution.py:284
  118.2 1.5 shard_map.75
  119.7 13.2 %all_to_all.27.refs_0_ = bf16[32,40,128]{2,1,0:T(8,128)(2,1)S(1)} all-to-all(bf16[32,40,128]{2,1,0:T(8,128)(2,1)S(1)} %get-tuple-element.33), channel_id=1, replica_groups=mesh['x'=4,'z'=8,'c'=2,'y'=4] {'x','z'}, dimensions={0} | all-to-all | bytes 655360 | tf_op jit(solution)/shard_map/all_to_all | solution.py:342
  133.8 15.8 %all_to_all.28 = bf16[32,16,128]{2,1,0:T(8,128)(2,1)S(1)} all-to-all(bf16[32,16,128]{2,1,0:T(8,128)(2,1)S(1)} %get-tuple-element.35), channel_id=1, replica_groups=mesh['x'=4,'z'=8,'c'=2,'y'=4] {'x','z'}, dimensions={0} | all-to-all | bytes 262144 | tf_op jit(solution)/shard_map/all_to_all | solution.py:348
  150.1 3.7 %collective-permute-start.15 = (f32[88,128]{1,0:T(8,128)S(1)}, f32[88,128]{1,0:T(8,128)S(1)}, u32[]{:S(2)}, u32[]{:S(2)}) collective-permute-start(f32[88,128]{1,0:T(8,128)S(1)} %get-tuple-element.37), channel_id=1, source_target_pairs={{0,4},{4,0},{1,5},{5,1},{2,6},{6,2},{3,7},{7,3},{8,12},{12,8},{9,1... | collective-permute-start | bytes 135176 | tf_op jit(solution)/shard_map/ppermute | solution.py:284
  154.7 2.8 %collective-permute-start.17 = (f32[88,128]{1,0:T(8,128)S(1)}, f32[88,128]{1,0:T(8,128)S(1)}, u32[]{:S(2)}, u32[]{:S(2)}) collective-permute-start(f32[88,128]{1,0:T(8,128)S(1)} %add.41.a_ref), channel_id=1, source_target_pairs={{0,2},{1,3},{2,0},{3,1},{4,6},{5,7},{6,4},{7,5},{8,10},{9,11},{10,... | collective-permute-start | bytes 135176 | tf_op jit(solution)/shard_map/ppermute | solution.py:284
  (42 shorter events, 15.9 us)
Async XLA Ops:
  4.2 13.1 %copy-start.1 = (f32[64,122]{1,0:T(8,128)S(1)}, f32[64,122]{1,0:T(8,128)}, u32[]{:S(2)}) copy-start(f32[64,122]{1,0:T(8,128)} %param.9) | copy-start | bytes 93700
  4.2 65.1 %all-to-all-start = ((bf16[64,64,256]{2,1,0:T(8,128)(2,1)}), bf16[64,64,256]{2,1,0:T(8,128)(2,1)S(1)}, u32[]{:S(2)}, u32[]{:S(2)}) async-start(bf16[64,64,256]{2,1,0:T(8,128)(2,1)} %shard_map.68), calls=%async_computation | async-start | bytes 4194304 | tf_op jit(solution)/shard_map/all_to_all | solution.py:318
  17.6 1.3 collective-permute-start
  18.9 4.5 %collective-permute-start.2 = (f32[24,128]{1,0:T(8,128)S(1)}, f32[24,128]{1,0:T(8,128)S(1)}, u32[]{:S(2)}, u32[]{:S(2)}) collective-permute-start(f32[24,128]{1,0:T(8,128)S(1)} %add.32), channel_id=1, source_target_pairs={{0,64},{64,128},{128,192},{192,0},{1,65},{65,129},{129,193},{193,1... | collective-permute-start | bytes 36872 | tf_op jit(solution)/shard_map/ppermute | solution.py:284
  20.2 3.5 %collective-permute-start.3 = (f32[24,128]{1,0:T(8,128)S(1)}, f32[24,128]{1,0:T(8,128)S(1)}, u32[]{:S(2)}, u32[]{:S(2)}) collective-permute-start(f32[24,128]{1,0:T(8,128)S(1)} %add.32), channel_id=1, source_target_pairs={{0,192},{64,0},{128,64},{192,128},{1,193},{65,1},{129,65},{193,129... | collective-permute-start | bytes 36872 | tf_op jit(solution)/shard_map/ppermute | solution.py:284
  21.7 4.5 %collective-permute-start.1 = (f32[24,128]{1,0:T(8,128)S(1)}, f32[24,128]{1,0:T(8,128)S(1)}, u32[]{:S(2)}, u32[]{:S(2)}) collective-permute-start(f32[24,128]{1,0:T(8,128)S(1)} %add.32), channel_id=1, source_target_pairs={{0,128},{64,192},{128,0},{192,64},{1,129},{65,193},{129,1},{193,65... | collective-permute-start | bytes 36872 | tf_op jit(solution)/shard_map/ppermute | solution.py:284
  26.2 37.3 %collective-permute-start.7 = (f32[24,128]{1,0:T(8,128)S(1)}, f32[24,128]{1,0:T(8,128)S(1)}, u32[]{:S(2)}, u32[]{:S(2)}) collective-permute-start(f32[24,128]{1,0:T(8,128)S(1)} %add_add_fusion.1), channel_id=1, source_target_pairs={{24,0},{60,4},{32,8},{4,12},{40,16},{12,20},{48,24},{20,28},{56,32... | collective-permute-start | bytes 36872 | tf_op jit(solution)/shard_map/ppermute | solution.py:297
  28.2 38.4 %collective-permute-start.6 = (f32[24,128]{1,0:T(8,128)S(1)}, f32[24,128]{1,0:T(8,128)S(1)}, u32[]{:S(2)}, u32[]{:S(2)}) collective-permute-start(f32[24,128]{1,0:T(8,128)S(1)} %add_add_fusion.1), channel_id=1, source_target_pairs={{16,0},{52,4},{24,8},{60,12},{32,16},{4,20},{40,24},{12,28},{48,32... | collective-permute-start | bytes 36872 | tf_op jit(solution)/shard_map/ppermute | solution.py:297
  29.7 39.6 %collective-permute-start.4 = (f32[24,128]{1,0:T(8,128)S(1)}, f32[24,128]{1,0:T(8,128)S(1)}, u32[]{:S(2)}, u32[]{:S(2)}) collective-permute-start(f32[24,128]{1,0:T(8,128)S(1)} %add_add_fusion.1), channel_id=1, source_target_pairs={{0,0},{36,4},{8,8},{44,12},{16,16},{52,20},{24,24},{60,28},{32,32}... | collective-permute-start | bytes 36872 | tf_op jit(solution)/shard_map/ppermute | solution.py:297
  34.2 35.1 %collective-permute-start.5 = (f32[24,128]{1,0:T(8,128)S(1)}, f32[24,128]{1,0:T(8,128)S(1)}, u32[]{:S(2)}, u32[]{:S(2)}) collective-permute-start(f32[24,128]{1,0:T(8,128)S(1)} %add_add_fusion.1), channel_id=1, source_target_pairs={{8,0},{44,4},{16,8},{52,12},{24,16},{60,20},{32,24},{4,28},{40,32}... | collective-permute-start | bytes 36872 | tf_op jit(solution)/shard_map/ppermute | solution.py:297
  36.8 32.5 %collective-permute-start.8 = (f32[64,128]{1,0:T(8,128)S(1)}, f32[64,128]{1,0:T(8,128)S(1)}, u32[]{:S(2)}, u32[]{:S(2)}) collective-permute-start(f32[64,128]{1,0:T(8,128)S(1)} %pad.4.templ_ref.own_ref), channel_id=1, source_target_pairs={{0,4},{4,0},{1,5},{5,1},{2,6},{6,2},{3,7},{7,3},{8,12},{12,8},{9,1... | collective-permute-start | bytes 98312 | tf_op jit(solution)/shard_map/ppermute | solution.py:284
  72.0 3.0 %collective-permute-start.9 = (bf16[512,256]{1,0:T(8,128)(2,1)S(1)}, bf16[512,256]{1,0:T(8,128)(2,1)S(1)}, u32[]{:S(2)}, u32[]{:S(2)}) collective-permute-start(bf16[512,256]{1,0:T(8,128)(2,1)S(1)} %get-tuple-element.26), channel_id=1, source_target_pairs={{0,4},{4,0},{1,5},{5,1},{2,6},{6,2},{3,7},{7,3},{8,12},{12,8},{9,1... | collective-permute-start | bytes 786440 | tf_op jit(solution)/shard_map/ppermute | solution.py:284
  72.1 2.8 %collective-permute-start.10 = (f32[24,128]{1,0:T(8,128)S(1)}, f32[24,128]{1,0:T(8,128)S(1)}, u32[]{:S(2)}, u32[]{:S(2)}) collective-permute-start(f32[24,128]{1,0:T(8,128)S(1)} %add_add_fusion), channel_id=1, source_target_pairs={{0,4},{4,0},{1,5},{5,1},{2,6},{6,2},{3,7},{7,3},{8,12},{12,8},{9,1... | collective-permute-start | bytes 36872 | tf_op jit(solution)/shard_map/ppermute | solution.py:284
  72.6 17.6 %copy-start = (f32[32,64]{1,0:T(8,128)S(1)}, f32[32,64]{1,0:T(8,128)}, u32[]{:S(2)}) copy-start(f32[32,64]{1,0:T(8,128)} %refs_2_.1) | copy-start | bytes 24580
  107.1 3.3 %collective-permute-start.11 = (f32[152,128]{1,0:T(8,128)S(1)}, f32[152,128]{1,0:T(8,128)S(1)}, u32[]{:S(2)}, u32[]{:S(2)}) collective-permute-start(f32[152,128]{1,0:T(8,128)S(1)} %get-tuple-element.32), channel_id=1, source_target_pairs={{0,4},{4,0},{1,5},{5,1},{2,6},{6,2},{3,7},{7,3},{8,12},{12,8},{9,1... | collective-permute-start | bytes 233480 | tf_op jit(solution)/shard_map/ppermute | solution.py:284
  110.4 5.1 %collective-permute-start.12 = (f32[152,128]{1,0:T(8,128)S(1)}, f32[152,128]{1,0:T(8,128)S(1)}, u32[]{:S(2)}, u32[]{:S(2)}) collective-permute-start(f32[152,128]{1,0:T(8,128)S(1)} %add.40.a_ref), channel_id=1, source_target_pairs={{0,1},{1,2},{2,3},{3,0},{4,5},{5,6},{6,7},{7,4},{8,9},{9,10},{10,1... | collective-permute-start | bytes 233480 | tf_op jit(solution)/shard_map/ppermute | solution.py:284
  111.8 6.4 %collective-permute-start.13 = (f32[152,128]{1,0:T(8,128)S(1)}, f32[152,128]{1,0:T(8,128)S(1)}, u32[]{:S(2)}, u32[]{:S(2)}) collective-permute-start(f32[152,128]{1,0:T(8,128)S(1)} %add.40.a_ref), channel_id=1, source_target_pairs={{0,2},{1,3},{2,0},{3,1},{4,6},{5,7},{6,4},{7,5},{8,10},{9,11},{10,... | collective-permute-start | bytes 233480 | tf_op jit(solution)/shard_map/ppermute | solution.py:284
  114.4 3.8 %collective-permute-start.14 = (f32[152,128]{1,0:T(8,128)S(1)}, f32[152,128]{1,0:T(8,128)S(1)}, u32[]{:S(2)}, u32[]{:S(2)}) collective-permute-start(f32[152,128]{1,0:T(8,128)S(1)} %add.40.a_ref), channel_id=1, source_target_pairs={{0,3},{1,0},{2,1},{3,2},{4,7},{5,4},{6,5},{7,6},{8,11},{9,8},{10,9... | collective-permute-start | bytes 233480 | tf_op jit(solution)/shard_map/ppermute | solution.py:284
  150.1 4.6 %collective-permute-start.15 = (f32[88,128]{1,0:T(8,128)S(1)}, f32[88,128]{1,0:T(8,128)S(1)}, u32[]{:S(2)}, u32[]{:S(2)}) collective-permute-start(f32[88,128]{1,0:T(8,128)S(1)} %get-tuple-element.37), channel_id=1, source_target_pairs={{0,4},{4,0},{1,5},{5,1},{2,6},{6,2},{3,7},{7,3},{8,12},{12,8},{9,1... | collective-permute-start | bytes 135176 | tf_op jit(solution)/shard_map/ppermute | solution.py:284
  154.7 4.1 %collective-permute-start.16 = (f32[88,128]{1,0:T(8,128)S(1)}, f32[88,128]{1,0:T(8,128)S(1)}, u32[]{:S(2)}, u32[]{:S(2)}) collective-permute-start(f32[88,128]{1,0:T(8,128)S(1)} %add.41.a_ref), channel_id=1, source_target_pairs={{0,1},{1,2},{2,3},{3,0},{4,5},{5,6},{6,7},{7,4},{8,9},{9,10},{10,1... | collective-permute-start | bytes 135176 | tf_op jit(solution)/shard_map/ppermute | solution.py:284
  154.7 4.8 %collective-permute-start.17 = (f32[88,128]{1,0:T(8,128)S(1)}, f32[88,128]{1,0:T(8,128)S(1)}, u32[]{:S(2)}, u32[]{:S(2)}) collective-permute-start(f32[88,128]{1,0:T(8,128)S(1)} %add.41.a_ref), channel_id=1, source_target_pairs={{0,2},{1,3},{2,0},{3,1},{4,6},{5,7},{6,4},{7,5},{8,10},{9,11},{10,... | collective-permute-start | bytes 135176 | tf_op jit(solution)/shard_map/ppermute | solution.py:284
  157.5 3.3 %collective-permute-start.18 = (f32[88,128]{1,0:T(8,128)S(1)}, f32[88,128]{1,0:T(8,128)S(1)}, u32[]{:S(2)}, u32[]{:S(2)}) collective-permute-start(f32[88,128]{1,0:T(8,128)S(1)} %add.41.a_ref), channel_id=1, source_target_pairs={{0,3},{1,0},{2,1},{3,2},{4,7},{5,4},{6,5},{7,6},{8,11},{9,8},{10,9... | collective-permute-start | bytes 135176 | tf_op jit(solution)/shard_map/ppermute | solution.py:284

commit v8 on v7

--- a/solution.py
+++ b/solution.py
@@ -222,30 +222,47 @@
     out_ref[...] = jnp.broadcast_to(both[0:16, :].astype(BF)[None], out_ref.shape)
 
 
+def plain_gram(packed):
+    return jnp.concatenate(
+        [packed[:, 0:RANK], pltpu.roll(packed, RANK, 1)[:, 0:RANK]], axis=0
+    )
+
+
+def project(activ, spectra):
+    proj = lax.dot_general(activ, spectra, TN, preferred_element_type=F32)
+    return proj[0:64, 0:LANES] + proj[64:128, LANES:]
+
+
+def activ_gram(activ):
+    gram = lax.dot_general(activ, activ, TN, preferred_element_type=F32)
+    gram = gram[0:64, 0:64] + pltpu.roll(gram[64:128, :], 64, 1)[:, 0:64]
+    return spread(gram[0:32, :], 0) + spread(gram[32:64, :], 64)
+
+
 def project_body(activ_ref, keep_ref, came_ref, own_ref, send_ref):
     activ = activ_ref[...]
-    gram = lax.dot_general(activ, activ, TN, preferred_element_type=F32)
-    gram = pack_gram(gram[0:64, 0:64] + pltpu.roll(gram[64:128, :], 64, 1)[:, 0:64])
-    blocks = []
-    for ref in (keep_ref, came_ref):
-        proj = lax.dot_general(activ, ref[...], TN, preferred_element_type=F32)
-        blocks.append(proj[0:64, 0:LANES] + proj[64:128, LANES:])
-    own_ref[0:24, :] = gram
-    own_ref[24:88, :] = blocks[0]
-    send_ref[0:24, :] = gram
-    send_ref[24:88, :] = blocks[1]
-    if own_ref.shape[0] > 88:
-        own_ref[88:152, :] = blocks[1]
-        send_ref[24:88, :] = blocks[1]
-        send_ref[88:152, :] = blocks[0]
+    gram = activ_gram(activ)
+    own, other = project(activ, keep_ref[...]), project(activ, came_ref[...])
+    own_ref[0:32, :] = gram
+    own_ref[32:96, :] = own
+    own_ref[96:160, :] = other
+    send_ref[0:32, :] = gram
+    send_ref[32:96, :] = other
+    send_ref[96:160, :] = own
+
+
+def last_project_body(activ_ref, other_ref, keep_ref, away_ref, out_ref):
+    activ, other = activ_ref[...], other_ref[...]
+    out_ref[0:32, :] = activ_gram(activ) + activ_gram(other)
+    out_ref[32:96, :] = project(activ, keep_ref[...]) + project(other, away_ref[...])
 
 
 def new_templates(part_refs, templ):
     one, two, three, four = (ref[...] for ref in part_refs)
     total = (one + three) + (two + four)
-    gram, proj = unpack_gram(total[0:24, :]), total[24:88, :]
-    if total.shape[0] > 88:
-        proj = jnp.concatenate([proj, total[88:152, :]], axis=1)
+    gram, proj = plain_gram(total[0:32, :]), total[32:96, :]
+    if total.shape[0] > 96:
+        proj = jnp.concatenate([proj, total[96:160, :]], axis=1)
     return descend(templ, proj - exact(gram, templ), gram)
 
 
@@ -347,11 +364,16 @@
         )
         activ = lax.all_to_all(message, ("x", "z"), split_axis=0, concat_axis=0, tiled=True)
         activ = activ.reshape(512, LANES)
-        size = 152 if first else 88
-        part, away = call(
-            project_body, (sds(size, LANES), sds(size, LANES)), (activ, keep, came)
-        )
-        part = part + shift(away, "c", NC, 1)
+        if first:
+            both = (sds(160, LANES), sds(160, LANES))
+            part, sent = call(project_body, both, (activ, keep, came))
+            part = part + shift(sent, "c", NC, 1)
+        else:
+            part = call(
+                last_project_body,
+                sds(96, LANES),
+                (activ, shift(activ, "c", NC, 1), keep, away),
+            )
         parts = (part, *(shift(part, "y", NY, by) for by in (1, 2, 3)))
         if first:
             templates, cross = call(

time: 163 us -> 163 us (level)
  no operation moved by 1% of the time
where the time goes in v8:
time: 163 us; the launch traced here: 162 us
  blocking collectives  59.5 us (37%)
  starting transfers between devices  44.3 us (27%)
  waiting for transfers between devices  43 us (26%)
  Pallas kernels  14.4 us (9%)
    ppermute x4, waiting for transfers between devices, from_ahead(): return lax.ppermute(value, ('z', 'c'), pairs)  32.5 us
    all_to_all x2, blocking collectives, shards(): lax.all_to_all(message, ('x', 'z'), split_axis=0, concat_axis=0, tiled=True)  31.3 us
    all_to_all x2, blocking collectives, shards(): lax.all_to_all(cross, ('x', 'z'), split_axis=0, concat_axis=0, tiled=True)  28.2 us
    ppermute x15, starting transfers between devices, shift(): lax.ppermute(value, axis, [(i, (i + by) % size) for i in range(size)])  20.6 us
    all_to_all x1, starting transfers between devices, shards(): got = lax.all_to_all(send, TGT, split_axis=0, concat_axis=0, tiled=True)  13.1 us
    pallas_call x10, Pallas kernels, call(): pl.pallas_call(body, out_shape=outs, in_specs=[SMEM] * scalars + [VMEM] *...  10.8 us
    ppermute x4, starting transfers between devices, from_ahead(): return lax.ppermute(value, ('z', 'c'), pairs)  10.7 us
    ppermute x15, waiting for transfers between devices, shift(): lax.ppermute(value, axis, [(i, (i + by) % size) for i in range(size)])  10.5 us
  transfers between devices with their start and end apart: 20, of which 13 were waited for; matrix products, arithmetic and copies ran while one was open for 0% of the time, Pallas kernels for 2%

profile of v8, /device:TPU:1, one launch (start us, length us, event | category | flops | bytes accessed | tf_op | source)
XLA Modules:
  0.0 162.1 jit_solution(10108080573688194001)
XLA Ops:
  0.6 3.6 %shard_map.68 = bf16[64,64,256]{2,1,0:T(8,128)(2,1)} custom-call(bf16[64,7808]{1,0:T(8,128)(2,1)} %flux_ref.1, bf16[64,7808]{1,0:T(8,128)(2,1)} %ivar_ref.1, s32[1,64]{1,0:T(1,128)} %bitcast.11), custom_call_target="tpu_custom_call" | custom-call | flops 999424 | bytes 3997696 | tf_op jit(solution)/shard_map/pallas_call | solution.py:65
  4.2 13.1 %all-to-all-start = ((bf16[64,64,256]{2,1,0:T(8,128)(2,1)}), bf16[64,64,256]{2,1,0:T(8,128)(2,1)S(1)}, u32[]{:S(2)}, u32[]{:S(2)}) async-start(bf16[64,64,256]{2,1,0:T(8,128)(2,1)} %shard_map.68), calls=%async_computation | async-start | bytes 4194304 | tf_op jit(solution)/shard_map/all_to_all | solution.py:335
  20.2 1.4 collective-permute-start.3
  21.7 1.6 %collective-permute-start.1 = (f32[24,128]{1,0:T(8,128)S(1)}, f32[24,128]{1,0:T(8,128)S(1)}, u32[]{:S(2)}, u32[]{:S(2)}) collective-permute-start(f32[24,128]{1,0:T(8,128)S(1)} %add.29), channel_id=1, source_target_pairs={{0,128},{64,192},{128,0},{192,64},{1,129},{65,193},{129,1},{193,65... | collective-permute-start | bytes 36872 | tf_op jit(solution)/shard_map/ppermute | solution.py:301
  23.7 2.4 %collective-permute-done.1 = f32[24,128]{1,0:T(8,128)S(1)} collective-permute-done((f32[24,128]{1,0:T(8,128)S(1)}, f32[24,128]{1,0:T(8,128)S(1)}, u32[]{:S(2)}, u32[]{:S(2)}) %collective-permute-start.1) | collective-permute-done | bytes 12320 | tf_op jit(solution)/shard_map/ppermute | solution.py:301
  26.2 2.0 %collective-permute-start.7 = (f32[24,128]{1,0:T(8,128)S(1)}, f32[24,128]{1,0:T(8,128)S(1)}, u32[]{:S(2)}, u32[]{:S(2)}) collective-permute-start(f32[24,128]{1,0:T(8,128)S(1)} %add_add_fusion.1), channel_id=1, source_target_pairs={{24,0},{60,4},{32,8},{4,12},{40,16},{12,20},{48,24},{20,28},{56,32... | collective-permute-start | bytes 36872 | tf_op jit(solution)/shard_map/ppermute | solution.py:314
  28.2 1.5 collective-permute-start.6
  29.7 4.5 %collective-permute-start.4 = (f32[24,128]{1,0:T(8,128)S(1)}, f32[24,128]{1,0:T(8,128)S(1)}, u32[]{:S(2)}, u32[]{:S(2)}) collective-permute-start(f32[24,128]{1,0:T(8,128)S(1)} %add_add_fusion.1), channel_id=1, source_target_pairs={{0,0},{36,4},{8,8},{44,12},{16,16},{52,20},{24,24},{60,28},{32,32}... | collective-permute-start | bytes 36872 | tf_op jit(solution)/shard_map/ppermute | solution.py:314
  34.2 2.6 %collective-permute-start.5 = (f32[24,128]{1,0:T(8,128)S(1)}, f32[24,128]{1,0:T(8,128)S(1)}, u32[]{:S(2)}, u32[]{:S(2)}) collective-permute-start(f32[24,128]{1,0:T(8,128)S(1)} %add_add_fusion.1), channel_id=1, source_target_pairs={{8,0},{44,4},{16,8},{52,12},{24,16},{60,20},{32,24},{4,28},{40,32}... | collective-permute-start | bytes 36872 | tf_op jit(solution)/shard_map/ppermute | solution.py:314
  36.8 26.6 %collective-permute-done.7 = f32[24,128]{1,0:T(8,128)S(1)} collective-permute-done((f32[24,128]{1,0:T(8,128)S(1)}, f32[24,128]{1,0:T(8,128)S(1)}, u32[]{:S(2)}, u32[]{:S(2)}) %collective-permute-start.7) | collective-permute-done | bytes 12320 | tf_op jit(solution)/shard_map/ppermute | solution.py:314
  63.4 3.1 %collective-permute-done.6 = f32[24,128]{1,0:T(8,128)S(1)} collective-permute-done((f32[24,128]{1,0:T(8,128)S(1)}, f32[24,128]{1,0:T(8,128)S(1)}, u32[]{:S(2)}, u32[]{:S(2)}) %collective-permute-start.6) | collective-permute-done | bytes 12320 | tf_op jit(solution)/shard_map/ppermute | solution.py:314
  66.5 2.8 %collective-permute-done.4 = f32[24,128]{1,0:T(8,128)S(1)} collective-permute-done((f32[24,128]{1,0:T(8,128)S(1)}, f32[24,128]{1,0:T(8,128)S(1)}, u32[]{:S(2)}, u32[]{:S(2)}) %collective-permute-start.4) | collective-permute-done | bytes 12320 | tf_op jit(solution)/shard_map/ppermute | solution.py:314
  69.3 2.7 %shard_map.70 = (bf16[512,256]{1,0:T(8,128)(2,1)S(1)}, bf16[64,4096]{1,0:T(8,128)(2,1)S(1)}, f32[8,4096]{1,0:T(8,128)S(1)}) custom-call(s32[1]{0:T(128)} %bitcast.1.core_ref, bf16[4096,256]{1,0:T(8,128)(2,1)S(1)} %bitcast.5), custom_call_target="tpu_custom_call" | custom-call | flops 2147483648 | tf_op jit(solution)/shard_map/pallas_call | solution.py:28
  72.6 2.3 %shard_map.71.keep_ref = bf16[512,256]{1,0:T(8,128)(2,1)S(1)} custom-call(s32[1]{0:T(128)} %bitcast.1.core_ref, bf16[4096,256]{1,0:T(8,128)(2,1)S(1)} %bitcast.6, bf16[64,4096]{1,0:T(8,128)(2,1)S(1)} %get-tuple-element.22.low_ref, f32[8,4096]{1,0:T(8,128)S(1)} %get-tuple-element.23.high_ref), custom_call_target="tpu_custom_call" | custom-call | flops 2147483648 | tf_op jit(solution)/shard_map/pallas_call | solution.py:28
  75.2 15.0 %all_to_all.25.refs_0_ = f32[32,16,128]{2,1,0:T(8,128)S(1)} all-to-all(f32[32,16,128]{2,1,0:T(8,128)S(1)} %shard_map.72), channel_id=1, replica_groups=mesh['x'=4,'z'=8,'c'=2,'y'=4] {'x','z'}, dimensions={0} | all-to-all | bytes 524288 | tf_op jit(solution)/shard_map/all_to_all | solution.py:359
  91.2 15.5 %all_to_all.26 = bf16[32,16,128]{2,1,0:T(8,128)(2,1)S(1)} all-to-all(bf16[32,16,128]{2,1,0:T(8,128)(2,1)S(1)} %get-tuple-element.28), channel_id=1, replica_groups=mesh['x'=4,'z'=8,'c'=2,'y'=4] {'x','z'}, dimensions={0} | all-to-all | bytes 262144 | tf_op jit(solution)/shard_map/all_to_all | solution.py:365
  107.0 2.4 %collective-permute-start.11 = (f32[160,128]{1,0:T(8,128)S(1)}, f32[160,128]{1,0:T(8,128)S(1)}, u32[]{:S(2)}, u32[]{:S(2)}) collective-permute-start(f32[160,128]{1,0:T(8,128)S(1)} %get-tuple-element.30), channel_id=1, source_target_pairs={{0,4},{4,0},{1,5},{5,1},{2,6},{6,2},{3,7},{7,3},{8,12},{12,8},{9,1... | collective-permute-start | bytes 245768 | tf_op jit(solution)/shard_map/ppermute | solution.py:301
  110.4 1.4 collective-permute-start.12
  111.7 2.6 %collective-permute-start.13 = (f32[160,128]{1,0:T(8,128)S(1)}, f32[160,128]{1,0:T(8,128)S(1)}, u32[]{:S(2)}, u32[]{:S(2)}) collective-permute-start(f32[160,128]{1,0:T(8,128)S(1)} %add.37.a_ref), channel_id=1, source_target_pairs={{0,2},{1,3},{2,0},{3,1},{4,6},{5,7},{6,4},{7,5},{8,10},{9,11},{10,... | collective-permute-start | bytes 245768 | tf_op jit(solution)/shard_map/ppermute | solution.py:301
  115.5 2.9 %collective-permute-done.13.c_ref = f32[160,128]{1,0:T(8,128)S(1)} collective-permute-done((f32[160,128]{1,0:T(8,128)S(1)}, f32[160,128]{1,0:T(8,128)S(1)}, u32[]{:S(2)}, u32[]{:S(2)}) %collective-permute-start.13) | collective-permute-done | bytes 81952 | tf_op jit(solution)/shard_map/ppermute | solution.py:301
  119.7 13.2 %all_to_all.27.refs_0_ = bf16[32,40,128]{2,1,0:T(8,128)(2,1)S(1)} all-to-all(bf16[32,40,128]{2,1,0:T(8,128)(2,1)S(1)} %get-tuple-element.31), channel_id=1, replica_groups=mesh['x'=4,'z'=8,'c'=2,'y'=4] {'x','z'}, dimensions={0} | all-to-all | bytes 655360 | tf_op jit(solution)/shard_map/all_to_all | solution.py:359
  133.8 15.8 %all_to_all.28 = bf16[32,16,128]{2,1,0:T(8,128)(2,1)S(1)} all-to-all(bf16[32,16,128]{2,1,0:T(8,128)(2,1)S(1)} %get-tuple-element.33), channel_id=1, replica_groups=mesh['x'=4,'z'=8,'c'=2,'y'=4] {'x','z'}, dimensions={0} | all-to-all | bytes 262144 | tf_op jit(solution)/shard_map/all_to_all | solution.py:365
  149.7 3.6 %collective-permute-start.15 = (bf16[512,128]{1,0:T(8,128)(2,1)S(1)}, bf16[512,128]{1,0:T(8,128)(2,1)S(1)}, u32[]{:S(2)}, u32[]{:S(2)}) collective-permute-start(bf16[512,128]{1,0:T(8,128)(2,1)S(1)} %bitcast.9), channel_id=1, source_target_pairs={{0,4},{4,0},{1,5},{5,1},{2,6},{6,2},{3,7},{7,3},{8,12},{12,8},{9,1... | collective-permute-start | bytes 393224 | tf_op jit(solution)/shard_map/ppermute | solution.py:301
  154.8 2.7 %collective-permute-start.17 = (f32[96,128]{1,0:T(8,128)S(1)}, f32[96,128]{1,0:T(8,128)S(1)}, u32[]{:S(2)}, u32[]{:S(2)}) collective-permute-start(f32[96,128]{1,0:T(8,128)S(1)} %shard_map.77.a_ref), channel_id=1, source_target_pairs={{0,2},{1,3},{2,0},{3,1},{4,6},{5,7},{6,4},{7,5},{8,10},{9,11},{10,... | collective-permute-start | bytes 147464 | tf_op jit(solution)/shard_map/ppermute | solution.py:301
  (41 shorter events, 15.9 us)
Async XLA Ops:
  4.2 13.1 %copy-start.1 = (f32[64,122]{1,0:T(8,128)S(1)}, f32[64,122]{1,0:T(8,128)}, u32[]{:S(2)}) copy-start(f32[64,122]{1,0:T(8,128)} %param.9) | copy-start | bytes 93700
  4.2 65.1 %all-to-all-start = ((bf16[64,64,256]{2,1,0:T(8,128)(2,1)}), bf16[64,64,256]{2,1,0:T(8,128)(2,1)S(1)}, u32[]{:S(2)}, u32[]{:S(2)}) async-start(bf16[64,64,256]{2,1,0:T(8,128)(2,1)} %shard_map.68), calls=%async_computation | async-start | bytes 4194304 | tf_op jit(solution)/shard_map/all_to_all | solution.py:335
  17.6 1.3 collective-permute-start
  18.9 4.5 %collective-permute-start.2 = (f32[24,128]{1,0:T(8,128)S(1)}, f32[24,128]{1,0:T(8,128)S(1)}, u32[]{:S(2)}, u32[]{:S(2)}) collective-permute-start(f32[24,128]{1,0:T(8,128)S(1)} %add.29), channel_id=1, source_target_pairs={{0,64},{64,128},{128,192},{192,0},{1,65},{65,129},{129,193},{193,1... | collective-permute-start | bytes 36872 | tf_op jit(solution)/shard_map/ppermute | solution.py:301
  20.2 3.5 %collective-permute-start.3 = (f32[24,128]{1,0:T(8,128)S(1)}, f32[24,128]{1,0:T(8,128)S(1)}, u32[]{:S(2)}, u32[]{:S(2)}) collective-permute-start(f32[24,128]{1,0:T(8,128)S(1)} %add.29), channel_id=1, source_target_pairs={{0,192},{64,0},{128,64},{192,128},{1,193},{65,1},{129,65},{193,129... | collective-permute-start | bytes 36872 | tf_op jit(solution)/shard_map/ppermute | solution.py:301
  21.7 4.5 %collective-permute-start.1 = (f32[24,128]{1,0:T(8,128)S(1)}, f32[24,128]{1,0:T(8,128)S(1)}, u32[]{:S(2)}, u32[]{:S(2)}) collective-permute-start(f32[24,128]{1,0:T(8,128)S(1)} %add.29), channel_id=1, source_target_pairs={{0,128},{64,192},{128,0},{192,64},{1,129},{65,193},{129,1},{193,65... | collective-permute-start | bytes 36872 | tf_op jit(solution)/shard_map/ppermute | solution.py:301
  26.2 37.3 %collective-permute-start.7 = (f32[24,128]{1,0:T(8,128)S(1)}, f32[24,128]{1,0:T(8,128)S(1)}, u32[]{:S(2)}, u32[]{:S(2)}) collective-permute-start(f32[24,128]{1,0:T(8,128)S(1)} %add_add_fusion.1), channel_id=1, source_target_pairs={{24,0},{60,4},{32,8},{4,12},{40,16},{12,20},{48,24},{20,28},{56,32... | collective-permute-start | bytes 36872 | tf_op jit(solution)/shard_map/ppermute | solution.py:314
  28.2 38.4 %collective-permute-start.6 = (f32[24,128]{1,0:T(8,128)S(1)}, f32[24,128]{1,0:T(8,128)S(1)}, u32[]{:S(2)}, u32[]{:S(2)}) collective-permute-start(f32[24,128]{1,0:T(8,128)S(1)} %add_add_fusion.1), channel_id=1, source_target_pairs={{16,0},{52,4},{24,8},{60,12},{32,16},{4,20},{40,24},{12,28},{48,32... | collective-permute-start | bytes 36872 | tf_op jit(solution)/shard_map/ppermute | solution.py:314
  29.7 39.6 %collective-permute-start.4 = (f32[24,128]{1,0:T(8,128)S(1)}, f32[24,128]{1,0:T(8,128)S(1)}, u32[]{:S(2)}, u32[]{:S(2)}) collective-permute-start(f32[24,128]{1,0:T(8,128)S(1)} %add_add_fusion.1), channel_id=1, source_target_pairs={{0,0},{36,4},{8,8},{44,12},{16,16},{52,20},{24,24},{60,28},{32,32}... | collective-permute-start | bytes 36872 | tf_op jit(solution)/shard_map/ppermute | solution.py:314
  34.2 35.1 %collective-permute-start.5 = (f32[24,128]{1,0:T(8,128)S(1)}, f32[24,128]{1,0:T(8,128)S(1)}, u32[]{:S(2)}, u32[]{:S(2)}) collective-permute-start(f32[24,128]{1,0:T(8,128)S(1)} %add_add_fusion.1), channel_id=1, source_target_pairs={{8,0},{44,4},{16,8},{52,12},{24,16},{60,20},{32,24},{4,28},{40,32}... | collective-permute-start | bytes 36872 | tf_op jit(solution)/shard_map/ppermute | solution.py:314
  36.8 32.5 %collective-permute-start.8 = (f32[64,128]{1,0:T(8,128)S(1)}, f32[64,128]{1,0:T(8,128)S(1)}, u32[]{:S(2)}, u32[]{:S(2)}) collective-permute-start(f32[64,128]{1,0:T(8,128)S(1)} %pad.4.templ_ref.own_ref), channel_id=1, source_target_pairs={{0,4},{4,0},{1,5},{5,1},{2,6},{6,2},{3,7},{7,3},{8,12},{12,8},{9,1... | collective-permute-start | bytes 98312 | tf_op jit(solution)/shard_map/ppermute | solution.py:301
  72.0 3.0 %collective-permute-start.9 = (bf16[512,256]{1,0:T(8,128)(2,1)S(1)}, bf16[512,256]{1,0:T(8,128)(2,1)S(1)}, u32[]{:S(2)}, u32[]{:S(2)}) collective-permute-start(bf16[512,256]{1,0:T(8,128)(2,1)S(1)} %get-tuple-element.24.away_ref), channel_id=1, source_target_pairs={{0,4},{4,0},{1,5},{5,1},{2,6},{6,2},{3,7},{7,3},{8,12},{12,8},{9,1... | collective-permute-start | bytes 786440 | tf_op jit(solution)/shard_map/ppermute | solution.py:301
  72.1 2.8 %collective-permute-start.10 = (f32[24,128]{1,0:T(8,128)S(1)}, f32[24,128]{1,0:T(8,128)S(1)}, u32[]{:S(2)}, u32[]{:S(2)}) collective-permute-start(f32[24,128]{1,0:T(8,128)S(1)} %add_add_fusion), channel_id=1, source_target_pairs={{0,4},{4,0},{1,5},{5,1},{2,6},{6,2},{3,7},{7,3},{8,12},{12,8},{9,1... | collective-permute-start | bytes 36872 | tf_op jit(solution)/shard_map/ppermute | solution.py:301
  72.6 17.6 %copy-start = (f32[32,64]{1,0:T(8,128)S(1)}, f32[32,64]{1,0:T(8,128)}, u32[]{:S(2)}) copy-start(f32[32,64]{1,0:T(8,128)} %refs_2_.1) | copy-start | bytes 24580
  107.0 3.3 %collective-permute-start.11 = (f32[160,128]{1,0:T(8,128)S(1)}, f32[160,128]{1,0:T(8,128)S(1)}, u32[]{:S(2)}, u32[]{:S(2)}) collective-permute-start(f32[160,128]{1,0:T(8,128)S(1)} %get-tuple-element.30), channel_id=1, source_target_pairs={{0,4},{4,0},{1,5},{5,1},{2,6},{6,2},{3,7},{7,3},{8,12},{12,8},{9,1... | collective-permute-start | bytes 245768 | tf_op jit(solution)/shard_map/ppermute | solution.py:301
  110.4 5.1 %collective-permute-start.12 = (f32[160,128]{1,0:T(8,128)S(1)}, f32[160,128]{1,0:T(8,128)S(1)}, u32[]{:S(2)}, u32[]{:S(2)}) collective-permute-start(f32[160,128]{1,0:T(8,128)S(1)} %add.37.a_ref), channel_id=1, source_target_pairs={{0,1},{1,2},{2,3},{3,0},{4,5},{5,6},{6,7},{7,4},{8,9},{9,10},{10,1... | collective-permute-start | bytes 245768 | tf_op jit(solution)/shard_map/ppermute | solution.py:301
  111.7 6.6 %collective-permute-start.13 = (f32[160,128]{1,0:T(8,128)S(1)}, f32[160,128]{1,0:T(8,128)S(1)}, u32[]{:S(2)}, u32[]{:S(2)}) collective-permute-start(f32[160,128]{1,0:T(8,128)S(1)} %add.37.a_ref), channel_id=1, source_target_pairs={{0,2},{1,3},{2,0},{3,1},{4,6},{5,7},{6,4},{7,5},{8,10},{9,11},{10,... | collective-permute-start | bytes 245768 | tf_op jit(solution)/shard_map/ppermute | solution.py:301
  114.3 4.0 %collective-permute-start.14 = (f32[160,128]{1,0:T(8,128)S(1)}, f32[160,128]{1,0:T(8,128)S(1)}, u32[]{:S(2)}, u32[]{:S(2)}) collective-permute-start(f32[160,128]{1,0:T(8,128)S(1)} %add.37.a_ref), channel_id=1, source_target_pairs={{0,3},{1,0},{2,1},{3,2},{4,7},{5,4},{6,5},{7,6},{8,11},{9,8},{10,9... | collective-permute-start | bytes 245768 | tf_op jit(solution)/shard_map/ppermute | solution.py:301
  149.7 4.6 %collective-permute-start.15 = (bf16[512,128]{1,0:T(8,128)(2,1)S(1)}, bf16[512,128]{1,0:T(8,128)(2,1)S(1)}, u32[]{:S(2)}, u32[]{:S(2)}) collective-permute-start(bf16[512,128]{1,0:T(8,128)(2,1)S(1)} %bitcast.9), channel_id=1, source_target_pairs={{0,4},{4,0},{1,5},{5,1},{2,6},{6,2},{3,7},{7,3},{8,12},{12,8},{9,1... | collective-permute-start | bytes 393224 | tf_op jit(solution)/shard_map/ppermute | solution.py:301
  154.7 4.2 %collective-permute-start.16 = (f32[96,128]{1,0:T(8,128)S(1)}, f32[96,128]{1,0:T(8,128)S(1)}, u32[]{:S(2)}, u32[]{:S(2)}) collective-permute-start(f32[96,128]{1,0:T(8,128)S(1)} %shard_map.77.a_ref), channel_id=1, source_target_pairs={{0,1},{1,2},{2,3},{3,0},{4,5},{5,6},{6,7},{7,4},{8,9},{9,10},{10,1... | collective-permute-start | bytes 147464 | tf_op jit(solution)/shard_map/ppermute | solution.py:301
  154.8 4.9 %collective-permute-start.17 = (f32[96,128]{1,0:T(8,128)S(1)}, f32[96,128]{1,0:T(8,128)S(1)}, u32[]{:S(2)}, u32[]{:S(2)}) collective-permute-start(f32[96,128]{1,0:T(8,128)S(1)} %shard_map.77.a_ref), channel_id=1, source_target_pairs={{0,2},{1,3},{2,0},{3,1},{4,6},{5,7},{6,4},{7,5},{8,10},{9,11},{10,... | collective-permute-start | bytes 147464 | tf_op jit(solution)/shard_map/ppermute | solution.py:301
  157.5 3.3 %collective-permute-start.18 = (f32[96,128]{1,0:T(8,128)S(1)}, f32[96,128]{1,0:T(8,128)S(1)}, u32[]{:S(2)}, u32[]{:S(2)}) collective-permute-start(f32[96,128]{1,0:T(8,128)S(1)} %shard_map.77.a_ref), channel_id=1, source_target_pairs={{0,3},{1,0},{2,1},{3,2},{4,7},{5,4},{6,5},{7,6},{8,11},{9,8},{10,9... | collective-permute-start | bytes 147464 | tf_op jit(solution)/shard_map/ppermute | solution.py:301

commit v9 on v8

--- a/solution.py
+++ b/solution.py
@@ -251,10 +251,16 @@
     send_ref[96:160, :] = own
 
 
-def last_project_body(activ_ref, other_ref, keep_ref, away_ref, out_ref):
-    activ, other = activ_ref[...], other_ref[...]
-    out_ref[0:32, :] = activ_gram(activ) + activ_gram(other)
-    out_ref[32:96, :] = project(activ, keep_ref[...]) + project(other, away_ref[...])
+def own_project_body(activ_ref, keep_ref, out_ref):
+    activ = activ_ref[...]
+    out_ref[0:32, :] = activ_gram(activ)
+    out_ref[32:96, :] = project(activ, keep_ref[...])
+
+
+def add_project_body(activ_ref, away_ref, part_ref, out_ref):
+    activ = activ_ref[...]
+    out_ref[0:32, :] = part_ref[0:32, :] + activ_gram(activ)
+    out_ref[32:96, :] = part_ref[32:96, :] + project(activ, away_ref[...])
 
 
 def new_templates(part_refs, templ):
@@ -369,11 +375,11 @@
             part, sent = call(project_body, both, (activ, keep, came))
             part = part + shift(sent, "c", NC, 1)
         else:
+            came_activ = shift(activ, "c", NC, 1)
             part = call(
-                last_project_body,
-                sds(96, LANES),
-                (activ, shift(activ, "c", NC, 1), keep, away),
+                own_project_body, sds(96, LANES), (activ, keep), flops=2 * 128 * 512 * 384
             )
+            part = call(add_project_body, sds(96, LANES), (came_activ, away, part))
         parts = (part, *(shift(part, "y", NY, by) for by in (1, 2, 3)))
         if first:
             templates, cross = call(

time: 163 us -> 162 us (level)
    pallas_call x10 -> x11, Pallas kernels: 10.8 us -> 11.2 us  [call(): pl.pallas_call(body, out_shape=outs, in_specs=[SMEM] * scalars + [VMEM] *...]
where the time goes in v9:
time: 162 us
  blocking collectives  59.5 us (37%)
  starting transfers between devices  44.3 us (27%)
  waiting for transfers between devices  42.6 us (26%)
  Pallas kernels  14.7 us (9%)
    ppermute x4, waiting for transfers between devices, from_ahead(): return lax.ppermute(value, ('z', 'c'), pairs)  32.5 us
    all_to_all x2, blocking collectives, shards(): lax.all_to_all(message, ('x', 'z'), split_axis=0, concat_axis=0, tiled=True)  31.3 us
    all_to_all x2, blocking collectives, shards(): lax.all_to_all(cross, ('x', 'z'), split_axis=0, concat_axis=0, tiled=True)  28.2 us
    ppermute x15, starting transfers between devices, shift(): lax.ppermute(value, axis, [(i, (i + by) % size) for i in range(size)])  20.6 us
    all_to_all x1, starting transfers between devices, shards(): got = lax.all_to_all(send, TGT, split_axis=0, concat_axis=0, tiled=True)  13.1 us
    pallas_call x11, Pallas kernels, call(): pl.pallas_call(body, out_shape=outs, in_specs=[SMEM] * scalars + [VMEM] *...  11.2 us
    ppermute x4, starting transfers between devices, from_ahead(): return lax.ppermute(value, ('z', 'c'), pairs)  10.7 us
    ppermute x15, waiting for transfers between devices, shift(): lax.ppermute(value, axis, [(i, (i + by) % size) for i in range(size)])  10.2 us
  transfers between devices with their start and end apart: 20, of which 13 were waited for; matrix products, arithmetic and copies ran while one was open for 0% of the time, Pallas kernels for 2%

profile of v9, /device:TPU:1, one launch (start us, length us, event | category | flops | bytes accessed | tf_op | source)
XLA Modules:
  0.0 162.0 jit_solution(4427585638596522397)
XLA Ops:
  0.6 3.6 %shard_map.68 = bf16[64,64,256]{2,1,0:T(8,128)(2,1)} custom-call(bf16[64,7808]{1,0:T(8,128)(2,1)} %flux_ref.1, bf16[64,7808]{1,0:T(8,128)(2,1)} %ivar_ref.1, s32[1,64]{1,0:T(1,128)} %bitcast.11), custom_call_target="tpu_custom_call" | custom-call | flops 999424 | bytes 3997696 | tf_op jit(solution)/shard_map/pallas_call | solution.py:65
  4.2 13.1 %all-to-all-start = ((bf16[64,64,256]{2,1,0:T(8,128)(2,1)}), bf16[64,64,256]{2,1,0:T(8,128)(2,1)S(1)}, u32[]{:S(2)}, u32[]{:S(2)}) async-start(bf16[64,64,256]{2,1,0:T(8,128)(2,1)} %shard_map.68), calls=%async_computation | async-start | bytes 4194304 | tf_op jit(solution)/shard_map/all_to_all | solution.py:341
  20.2 1.4 collective-permute-start.3
  21.7 1.6 %collective-permute-start.1 = (f32[24,128]{1,0:T(8,128)S(1)}, f32[24,128]{1,0:T(8,128)S(1)}, u32[]{:S(2)}, u32[]{:S(2)}) collective-permute-start(f32[24,128]{1,0:T(8,128)S(1)} %add.29), channel_id=1, source_target_pairs={{0,128},{64,192},{128,0},{192,64},{1,129},{65,193},{129,1},{193,65... | collective-permute-start | bytes 36872 | tf_op jit(solution)/shard_map/ppermute | solution.py:307
  23.7 2.4 %collective-permute-done.1 = f32[24,128]{1,0:T(8,128)S(1)} collective-permute-done((f32[24,128]{1,0:T(8,128)S(1)}, f32[24,128]{1,0:T(8,128)S(1)}, u32[]{:S(2)}, u32[]{:S(2)}) %collective-permute-start.1) | collective-permute-done | bytes 12320 | tf_op jit(solution)/shard_map/ppermute | solution.py:307
  26.2 2.0 %collective-permute-start.7 = (f32[24,128]{1,0:T(8,128)S(1)}, f32[24,128]{1,0:T(8,128)S(1)}, u32[]{:S(2)}, u32[]{:S(2)}) collective-permute-start(f32[24,128]{1,0:T(8,128)S(1)} %add_add_fusion.1), channel_id=1, source_target_pairs={{24,0},{60,4},{32,8},{4,12},{40,16},{12,20},{48,24},{20,28},{56,32... | collective-permute-start | bytes 36872 | tf_op jit(solution)/shard_map/ppermute | solution.py:320
  28.2 1.5 collective-permute-start.6
  29.7 4.5 %collective-permute-start.4 = (f32[24,128]{1,0:T(8,128)S(1)}, f32[24,128]{1,0:T(8,128)S(1)}, u32[]{:S(2)}, u32[]{:S(2)}) collective-permute-start(f32[24,128]{1,0:T(8,128)S(1)} %add_add_fusion.1), channel_id=1, source_target_pairs={{0,0},{36,4},{8,8},{44,12},{16,16},{52,20},{24,24},{60,28},{32,32}... | collective-permute-start | bytes 36872 | tf_op jit(solution)/shard_map/ppermute | solution.py:320
  34.2 2.6 %collective-permute-start.5 = (f32[24,128]{1,0:T(8,128)S(1)}, f32[24,128]{1,0:T(8,128)S(1)}, u32[]{:S(2)}, u32[]{:S(2)}) collective-permute-start(f32[24,128]{1,0:T(8,128)S(1)} %add_add_fusion.1), channel_id=1, source_target_pairs={{8,0},{44,4},{16,8},{52,12},{24,16},{60,20},{32,24},{4,28},{40,32}... | collective-permute-start | bytes 36872 | tf_op jit(solution)/shard_map/ppermute | solution.py:320
  36.8 26.6 %collective-permute-done.7 = f32[24,128]{1,0:T(8,128)S(1)} collective-permute-done((f32[24,128]{1,0:T(8,128)S(1)}, f32[24,128]{1,0:T(8,128)S(1)}, u32[]{:S(2)}, u32[]{:S(2)}) %collective-permute-start.7) | collective-permute-done | bytes 12320 | tf_op jit(solution)/shard_map/ppermute | solution.py:320
  63.4 3.1 %collective-permute-done.6 = f32[24,128]{1,0:T(8,128)S(1)} collective-permute-done((f32[24,128]{1,0:T(8,128)S(1)}, f32[24,128]{1,0:T(8,128)S(1)}, u32[]{:S(2)}, u32[]{:S(2)}) %collective-permute-start.6) | collective-permute-done | bytes 12320 | tf_op jit(solution)/shard_map/ppermute | solution.py:320
  66.5 2.8 %collective-permute-done.4 = f32[24,128]{1,0:T(8,128)S(1)} collective-permute-done((f32[24,128]{1,0:T(8,128)S(1)}, f32[24,128]{1,0:T(8,128)S(1)}, u32[]{:S(2)}, u32[]{:S(2)}) %collective-permute-start.4) | collective-permute-done | bytes 12320 | tf_op jit(solution)/shard_map/ppermute | solution.py:320
  69.3 2.7 %shard_map.70 = (bf16[512,256]{1,0:T(8,128)(2,1)S(1)}, bf16[64,4096]{1,0:T(8,128)(2,1)S(1)}, f32[8,4096]{1,0:T(8,128)S(1)}) custom-call(s32[1]{0:T(128)} %bitcast.1.core_ref, bf16[4096,256]{1,0:T(8,128)(2,1)S(1)} %bitcast.5), custom_call_target="tpu_custom_call" | custom-call | flops 2147483648 | tf_op jit(solution)/shard_map/pallas_call | solution.py:28
  72.6 2.3 %shard_map.71.keep_ref = bf16[512,256]{1,0:T(8,128)(2,1)S(1)} custom-call(s32[1]{0:T(128)} %bitcast.1.core_ref, bf16[4096,256]{1,0:T(8,128)(2,1)S(1)} %bitcast.6, bf16[64,4096]{1,0:T(8,128)(2,1)S(1)} %get-tuple-element.22.low_ref, f32[8,4096]{1,0:T(8,128)S(1)} %get-tuple-element.23.high_ref), custom_call_target="tpu_custom_call" | custom-call | flops 2147483648 | tf_op jit(solution)/shard_map/pallas_call | solution.py:28
  75.2 15.0 %all_to_all.25.refs_0_ = f32[32,16,128]{2,1,0:T(8,128)S(1)} all-to-all(f32[32,16,128]{2,1,0:T(8,128)S(1)} %shard_map.72), channel_id=1, replica_groups=mesh['x'=4,'z'=8,'c'=2,'y'=4] {'x','z'}, dimensions={0} | all-to-all | bytes 524288 | tf_op jit(solution)/shard_map/all_to_all | solution.py:365
  91.2 15.5 %all_to_all.26 = bf16[32,16,128]{2,1,0:T(8,128)(2,1)S(1)} all-to-all(bf16[32,16,128]{2,1,0:T(8,128)(2,1)S(1)} %get-tuple-element.28), channel_id=1, replica_groups=mesh['x'=4,'z'=8,'c'=2,'y'=4] {'x','z'}, dimensions={0} | all-to-all | bytes 262144 | tf_op jit(solution)/shard_map/all_to_all | solution.py:371
  107.0 2.4 %collective-permute-start.11 = (f32[160,128]{1,0:T(8,128)S(1)}, f32[160,128]{1,0:T(8,128)S(1)}, u32[]{:S(2)}, u32[]{:S(2)}) collective-permute-start(f32[160,128]{1,0:T(8,128)S(1)} %get-tuple-element.30), channel_id=1, source_target_pairs={{0,4},{4,0},{1,5},{5,1},{2,6},{6,2},{3,7},{7,3},{8,12},{12,8},{9,1... | collective-permute-start | bytes 245768 | tf_op jit(solution)/shard_map/ppermute | solution.py:307
  110.4 1.4 collective-permute-start.12
  111.7 2.6 %collective-permute-start.13 = (f32[160,128]{1,0:T(8,128)S(1)}, f32[160,128]{1,0:T(8,128)S(1)}, u32[]{:S(2)}, u32[]{:S(2)}) collective-permute-start(f32[160,128]{1,0:T(8,128)S(1)} %add.37.a_ref), channel_id=1, source_target_pairs={{0,2},{1,3},{2,0},{3,1},{4,6},{5,7},{6,4},{7,5},{8,10},{9,11},{10,... | collective-permute-start | bytes 245768 | tf_op jit(solution)/shard_map/ppermute | solution.py:307
  115.5 2.9 %collective-permute-done.13.c_ref = f32[160,128]{1,0:T(8,128)S(1)} collective-permute-done((f32[160,128]{1,0:T(8,128)S(1)}, f32[160,128]{1,0:T(8,128)S(1)}, u32[]{:S(2)}, u32[]{:S(2)}) %collective-permute-start.13) | collective-permute-done | bytes 81952 | tf_op jit(solution)/shard_map/ppermute | solution.py:307
  119.7 13.2 %all_to_all.27.refs_0_ = bf16[32,40,128]{2,1,0:T(8,128)(2,1)S(1)} all-to-all(bf16[32,40,128]{2,1,0:T(8,128)(2,1)S(1)} %get-tuple-element.31), channel_id=1, replica_groups=mesh['x'=4,'z'=8,'c'=2,'y'=4] {'x','z'}, dimensions={0} | all-to-all | bytes 655360 | tf_op jit(solution)/shard_map/all_to_all | solution.py:365
  133.8 15.8 %all_to_all.28 = bf16[32,16,128]{2,1,0:T(8,128)(2,1)S(1)} all-to-all(bf16[32,16,128]{2,1,0:T(8,128)(2,1)S(1)} %get-tuple-element.33), channel_id=1, replica_groups=mesh['x'=4,'z'=8,'c'=2,'y'=4] {'x','z'}, dimensions={0} | all-to-all | bytes 262144 | tf_op jit(solution)/shard_map/all_to_all | solution.py:371
  149.7 3.6 %collective-permute-start.15 = (bf16[512,128]{1,0:T(8,128)(2,1)S(1)}, bf16[512,128]{1,0:T(8,128)(2,1)S(1)}, u32[]{:S(2)}, u32[]{:S(2)}) collective-permute-start(bf16[512,128]{1,0:T(8,128)(2,1)S(1)} %bitcast.9), channel_id=1, source_target_pairs={{0,4},{4,0},{1,5},{5,1},{2,6},{6,2},{3,7},{7,3},{8,12},{12,8},{9,1... | collective-permute-start | bytes 393224 | tf_op jit(solution)/shard_map/ppermute | solution.py:307
  154.7 2.7 %collective-permute-start.17 = (f32[96,128]{1,0:T(8,128)S(1)}, f32[96,128]{1,0:T(8,128)S(1)}, u32[]{:S(2)}, u32[]{:S(2)}) collective-permute-start(f32[96,128]{1,0:T(8,128)S(1)} %shard_map.78.a_ref), channel_id=1, source_target_pairs={{0,2},{1,3},{2,0},{3,1},{4,6},{5,7},{6,4},{7,5},{8,10},{9,11},{10,... | collective-permute-start | bytes 147464 | tf_op jit(solution)/shard_map/ppermute | solution.py:307
  (42 shorter events, 15.9 us)
Async XLA Ops:
  4.2 13.1 %copy-start.1 = (f32[64,122]{1,0:T(8,128)S(1)}, f32[64,122]{1,0:T(8,128)}, u32[]{:S(2)}) copy-start(f32[64,122]{1,0:T(8,128)} %param.9) | copy-start | bytes 93700
  4.2 65.1 %all-to-all-start = ((bf16[64,64,256]{2,1,0:T(8,128)(2,1)}), bf16[64,64,256]{2,1,0:T(8,128)(2,1)S(1)}, u32[]{:S(2)}, u32[]{:S(2)}) async-start(bf16[64,64,256]{2,1,0:T(8,128)(2,1)} %shard_map.68), calls=%async_computation | async-start | bytes 4194304 | tf_op jit(solution)/shard_map/all_to_all | solution.py:341
  17.6 1.3 collective-permute-start
  18.9 4.5 %collective-permute-start.2 = (f32[24,128]{1,0:T(8,128)S(1)}, f32[24,128]{1,0:T(8,128)S(1)}, u32[]{:S(2)}, u32[]{:S(2)}) collective-permute-start(f32[24,128]{1,0:T(8,128)S(1)} %add.29), channel_id=1, source_target_pairs={{0,64},{64,128},{128,192},{192,0},{1,65},{65,129},{129,193},{193,1... | collective-permute-start | bytes 36872 | tf_op jit(solution)/shard_map/ppermute | solution.py:307
  20.2 3.5 %collective-permute-start.3 = (f32[24,128]{1,0:T(8,128)S(1)}, f32[24,128]{1,0:T(8,128)S(1)}, u32[]{:S(2)}, u32[]{:S(2)}) collective-permute-start(f32[24,128]{1,0:T(8,128)S(1)} %add.29), channel_id=1, source_target_pairs={{0,192},{64,0},{128,64},{192,128},{1,193},{65,1},{129,65},{193,129... | collective-permute-start | bytes 36872 | tf_op jit(solution)/shard_map/ppermute | solution.py:307
  21.7 4.5 %collective-permute-start.1 = (f32[24,128]{1,0:T(8,128)S(1)}, f32[24,128]{1,0:T(8,128)S(1)}, u32[]{:S(2)}, u32[]{:S(2)}) collective-permute-start(f32[24,128]{1,0:T(8,128)S(1)} %add.29), channel_id=1, source_target_pairs={{0,128},{64,192},{128,0},{192,64},{1,129},{65,193},{129,1},{193,65... | collective-permute-start | bytes 36872 | tf_op jit(solution)/shard_map/ppermute | solution.py:307
  26.2 37.3 %collective-permute-start.7 = (f32[24,128]{1,0:T(8,128)S(1)}, f32[24,128]{1,0:T(8,128)S(1)}, u32[]{:S(2)}, u32[]{:S(2)}) collective-permute-start(f32[24,128]{1,0:T(8,128)S(1)} %add_add_fusion.1), channel_id=1, source_target_pairs={{24,0},{60,4},{32,8},{4,12},{40,16},{12,20},{48,24},{20,28},{56,32... | collective-permute-start | bytes 36872 | tf_op jit(solution)/shard_map/ppermute | solution.py:320
  28.2 38.4 %collective-permute-start.6 = (f32[24,128]{1,0:T(8,128)S(1)}, f32[24,128]{1,0:T(8,128)S(1)}, u32[]{:S(2)}, u32[]{:S(2)}) collective-permute-start(f32[24,128]{1,0:T(8,128)S(1)} %add_add_fusion.1), channel_id=1, source_target_pairs={{16,0},{52,4},{24,8},{60,12},{32,16},{4,20},{40,24},{12,28},{48,32... | collective-permute-start | bytes 36872 | tf_op jit(solution)/shard_map/ppermute | solution.py:320
  29.7 39.6 %collective-permute-start.4 = (f32[24,128]{1,0:T(8,128)S(1)}, f32[24,128]{1,0:T(8,128)S(1)}, u32[]{:S(2)}, u32[]{:S(2)}) collective-permute-start(f32[24,128]{1,0:T(8,128)S(1)} %add_add_fusion.1), channel_id=1, source_target_pairs={{0,0},{36,4},{8,8},{44,12},{16,16},{52,20},{24,24},{60,28},{32,32}... | collective-permute-start | bytes 36872 | tf_op jit(solution)/shard_map/ppermute | solution.py:320
  34.2 35.1 %collective-permute-start.5 = (f32[24,128]{1,0:T(8,128)S(1)}, f32[24,128]{1,0:T(8,128)S(1)}, u32[]{:S(2)}, u32[]{:S(2)}) collective-permute-start(f32[24,128]{1,0:T(8,128)S(1)} %add_add_fusion.1), channel_id=1, source_target_pairs={{8,0},{44,4},{16,8},{52,12},{24,16},{60,20},{32,24},{4,28},{40,32}... | collective-permute-start | bytes 36872 | tf_op jit(solution)/shard_map/ppermute | solution.py:320
  36.8 32.5 %collective-permute-start.8 = (f32[64,128]{1,0:T(8,128)S(1)}, f32[64,128]{1,0:T(8,128)S(1)}, u32[]{:S(2)}, u32[]{:S(2)}) collective-permute-start(f32[64,128]{1,0:T(8,128)S(1)} %pad.4.templ_ref.own_ref), channel_id=1, source_target_pairs={{0,4},{4,0},{1,5},{5,1},{2,6},{6,2},{3,7},{7,3},{8,12},{12,8},{9,1... | collective-permute-start | bytes 98312 | tf_op jit(solution)/shard_map/ppermute | solution.py:307
  72.0 3.0 %collective-permute-start.9 = (bf16[512,256]{1,0:T(8,128)(2,1)S(1)}, bf16[512,256]{1,0:T(8,128)(2,1)S(1)}, u32[]{:S(2)}, u32[]{:S(2)}) collective-permute-start(bf16[512,256]{1,0:T(8,128)(2,1)S(1)} %get-tuple-element.24.away_ref), channel_id=1, source_target_pairs={{0,4},{4,0},{1,5},{5,1},{2,6},{6,2},{3,7},{7,3},{8,12},{12,8},{9,1... | collective-permute-start | bytes 786440 | tf_op jit(solution)/shard_map/ppermute | solution.py:307
  72.1 2.8 %collective-permute-start.10 = (f32[24,128]{1,0:T(8,128)S(1)}, f32[24,128]{1,0:T(8,128)S(1)}, u32[]{:S(2)}, u32[]{:S(2)}) collective-permute-start(f32[24,128]{1,0:T(8,128)S(1)} %add_add_fusion), channel_id=1, source_target_pairs={{0,4},{4,0},{1,5},{5,1},{2,6},{6,2},{3,7},{7,3},{8,12},{12,8},{9,1... | collective-permute-start | bytes 36872 | tf_op jit(solution)/shard_map/ppermute | solution.py:307
  72.6 17.6 %copy-start = (f32[32,64]{1,0:T(8,128)S(1)}, f32[32,64]{1,0:T(8,128)}, u32[]{:S(2)}) copy-start(f32[32,64]{1,0:T(8,128)} %refs_2_.1) | copy-start | bytes 24580
  107.0 3.3 %collective-permute-start.11 = (f32[160,128]{1,0:T(8,128)S(1)}, f32[160,128]{1,0:T(8,128)S(1)}, u32[]{:S(2)}, u32[]{:S(2)}) collective-permute-start(f32[160,128]{1,0:T(8,128)S(1)} %get-tuple-element.30), channel_id=1, source_target_pairs={{0,4},{4,0},{1,5},{5,1},{2,6},{6,2},{3,7},{7,3},{8,12},{12,8},{9,1... | collective-permute-start | bytes 245768 | tf_op jit(solution)/shard_map/ppermute | solution.py:307
  110.4 5.1 %collective-permute-start.12 = (f32[160,128]{1,0:T(8,128)S(1)}, f32[160,128]{1,0:T(8,128)S(1)}, u32[]{:S(2)}, u32[]{:S(2)}) collective-permute-start(f32[160,128]{1,0:T(8,128)S(1)} %add.37.a_ref), channel_id=1, source_target_pairs={{0,1},{1,2},{2,3},{3,0},{4,5},{5,6},{6,7},{7,4},{8,9},{9,10},{10,1... | collective-permute-start | bytes 245768 | tf_op jit(solution)/shard_map/ppermute | solution.py:307
  111.7 6.6 %collective-permute-start.13 = (f32[160,128]{1,0:T(8,128)S(1)}, f32[160,128]{1,0:T(8,128)S(1)}, u32[]{:S(2)}, u32[]{:S(2)}) collective-permute-start(f32[160,128]{1,0:T(8,128)S(1)} %add.37.a_ref), channel_id=1, source_target_pairs={{0,2},{1,3},{2,0},{3,1},{4,6},{5,7},{6,4},{7,5},{8,10},{9,11},{10,... | collective-permute-start | bytes 245768 | tf_op jit(solution)/shard_map/ppermute | solution.py:307
  114.3 4.0 %collective-permute-start.14 = (f32[160,128]{1,0:T(8,128)S(1)}, f32[160,128]{1,0:T(8,128)S(1)}, u32[]{:S(2)}, u32[]{:S(2)}) collective-permute-start(f32[160,128]{1,0:T(8,128)S(1)} %add.37.a_ref), channel_id=1, source_target_pairs={{0,3},{1,0},{2,1},{3,2},{4,7},{5,4},{6,5},{7,6},{8,11},{9,8},{10,9... | collective-permute-start | bytes 245768 | tf_op jit(solution)/shard_map/ppermute | solution.py:307
  149.7 4.6 %collective-permute-start.15 = (bf16[512,128]{1,0:T(8,128)(2,1)S(1)}, bf16[512,128]{1,0:T(8,128)(2,1)S(1)}, u32[]{:S(2)}, u32[]{:S(2)}) collective-permute-start(bf16[512,128]{1,0:T(8,128)(2,1)S(1)} %bitcast.9), channel_id=1, source_target_pairs={{0,4},{4,0},{1,5},{5,1},{2,6},{6,2},{3,7},{7,3},{8,12},{12,8},{9,1... | collective-permute-start | bytes 393224 | tf_op jit(solution)/shard_map/ppermute | solution.py:307
  154.7 4.2 %collective-permute-start.16 = (f32[96,128]{1,0:T(8,128)S(1)}, f32[96,128]{1,0:T(8,128)S(1)}, u32[]{:S(2)}, u32[]{:S(2)}) collective-permute-start(f32[96,128]{1,0:T(8,128)S(1)} %shard_map.78.a_ref), channel_id=1, source_target_pairs={{0,1},{1,2},{2,3},{3,0},{4,5},{5,6},{6,7},{7,4},{8,9},{9,10},{10,1... | collective-permute-start | bytes 147464 | tf_op jit(solution)/shard_map/ppermute | solution.py:307
  154.7 4.9 %collective-permute-start.17 = (f32[96,128]{1,0:T(8,128)S(1)}, f32[96,128]{1,0:T(8,128)S(1)}, u32[]{:S(2)}, u32[]{:S(2)}) collective-permute-start(f32[96,128]{1,0:T(8,128)S(1)} %shard_map.78.a_ref), channel_id=1, source_target_pairs={{0,2},{1,3},{2,0},{3,1},{4,6},{5,7},{6,4},{7,5},{8,10},{9,11},{10,... | collective-permute-start | bytes 147464 | tf_op jit(solution)/shard_map/ppermute | solution.py:307
  157.4 3.3 %collective-permute-start.18 = (f32[96,128]{1,0:T(8,128)S(1)}, f32[96,128]{1,0:T(8,128)S(1)}, u32[]{:S(2)}, u32[]{:S(2)}) collective-permute-start(f32[96,128]{1,0:T(8,128)S(1)} %shard_map.78.a_ref), channel_id=1, source_target_pairs={{0,3},{1,0},{2,1},{3,2},{4,7},{5,4},{6,5},{7,6},{8,11},{9,8},{10,9... | collective-permute-start | bytes 147464 | tf_op jit(solution)/shard_map/ppermute | solution.py:307
